TPU v7x, 32 devices: a whole 2x2x4 slice. The times are simulated.
32 devices in a mesh: groups: 2 (over y), date: 4 (over x, core), col: 4 (over z).
Axes of the slice: x: 2, y: 2, z: 4, core: 2. Of those that a mesh axis runs over, the one named last changes fastest.
Arguments:
- scenes: bfloat16 [16, 2, 128, 1024], P('date', None, 'groups', 'col'), parts along dimension 2, may hold values from -6 to 6
- pair_dates: int32 [96, 2], P('date'), may hold values from 0 to 15, as said below
- pair_count: int32 [4], P('date'), may hold values from 12 to 24, as said below
- inverse: float32 [15, 96], replicated, may hold values from -0.625 to 0.625
Outputs:
- series: float32 [15, 2, 64, 128], P(None, None, ('groups', 'date'), 'col'), parts along dimension 2
There are 2 independent parts, one for each index of `groups`. A program takes and returns all parts, laid end to end along the dimension named above; an argument that names none is the same for every part. Nothing has to cross between parts.
Inputs may be any that keep to these rules, and one draw needn't show every extreme that they name: `pair_dates`: each row names a reference acquisition and a later secondary one. Slots i * 24 to (i + 1) * 24 - 1 belong to owner i (index i of date); every slot of owner i names acquisitions held by indices i - 2 to i + 2 of date (as far as these exist), and one live pair of every owner names the lowest and the highest acquisition of that range. `pair_count`: entry i is the number of live slots of owner i; they come first in its block and the other slots are ignored. Some owner has all its slots live.
All inputs are finite; a program needn't handle non-finite values.
Results may differ from a plain program's by a relative error of at most 0.0003.
Values may be sent and summed in bfloat16 or wider, within the bound.
No kernel may reach another device: no remote copies, remote signals or barrier semaphores. Data moves between devices by JAX's collectives and lax.ppermute only.
A program may use at most 64 MiB of HBM per device.

v0:
```python
import jax
import jax.numpy as jnp
from jax import lax
from jax.sharding import PartitionSpec as P


def padded(cells, sides, width):
    for axis, dim in sides:
        count = lax.axis_size(axis)
        ends = count - 1
        head = lax.slice_in_dim(cells, 0, width, axis=dim)
        tail = lax.slice_in_dim(cells, cells.shape[dim] - width, cells.shape[dim], axis=dim)
        cells = jnp.concatenate(
            [
                lax.ppermute(tail, axis, [(i, (i + 1) % count) for i in range(ends)]),
                cells,
                lax.ppermute(head, axis, [((i + 1) % count, i) for i in range(ends)]),
            ],
            axis=dim,
        )
    return cells


def look_matrix(padded_width, looks_here):
    column = jnp.arange(padded_width, dtype=jnp.int32)[:, None]
    target = jnp.arange(looks_here, dtype=jnp.int32)[None, :]
    offset = (column - 8 * target).astype(jnp.float32)
    inside = (offset >= 0.0) & (offset < 16.0)
    return jnp.where(inside, (8.0 - jnp.abs(offset - 7.5)) / 64.0, 0.0)


def per_device(scenes, pair_dates, pair_count, inverse):
    slot_count = pair_dates.shape[0]
    looks_here = scenes.shape[3] // 8
    base = lax.all_to_all(scenes, "date", split_axis=2, concat_axis=0, tiled=True)
    used_dates, used_counts = (
        lax.all_gather(pair_dates, "date", axis=0, tiled=True),
        lax.all_gather(pair_count, "date", axis=0, tiled=True),
    )
    slot_index = jnp.arange(used_dates.shape[0], dtype=jnp.int32)
    living = (slot_index % slot_count < jnp.take(used_counts, slot_index // slot_count)).astype(
        jnp.float32
    )
    primary = jnp.take(base, used_dates[:, 0], axis=0)
    secondary = jnp.take(base, used_dates[:, 1], axis=0)
    p_real = primary[:, 0].astype(jnp.float32)
    p_imag = primary[:, 1].astype(jnp.float32)
    s_real = secondary[:, 0].astype(jnp.float32)
    s_imag = secondary[:, 1].astype(jnp.float32)
    real_part = p_real * s_real + p_imag * s_imag
    imaginary = p_imag * s_real - p_real * s_imag
    products = jnp.stack([real_part, imaginary], axis=1) * living[:, None, None, None]
    products = padded(products, (("col", 3),), 4)
    pair_total = products.shape[0]
    padded_width = products.shape[3]
    half_rows = products.shape[2] // 2
    halved = products.reshape(pair_total, 2, half_rows, 2, padded_width).sum(axis=3) * 0.5
    looked = jnp.dot(
        halved.reshape(-1, padded_width),
        look_matrix(padded_width, looks_here),
        precision=lax.Precision.HIGHEST,
        preferred_element_type=jnp.float32,
    )
    looked = looked.reshape(pair_total, 2, half_rows, looks_here)
    return jnp.einsum("qk,kcrm->qcrm", inverse, looked, precision=lax.Precision.HIGHEST)


def solution(mesh):
    placed = (P("date", None, "groups", "col"), P("date", None), P("date"), P())
    return jax.shard_map(
        per_device,
        mesh=mesh,
        in_specs=placed,
        out_specs=P(None, None, ("groups", "date"), "col"),
        check_vma=False,
    )
```

profile of v0, /device:TPU:0, one launch (start us, length us, event | category | flops | bytes accessed | tf_op | source)
XLA Modules:
  0.0 63.4 jit_solution(10447233835666667164)
XLA Ops:
  0.0 0.0 copy-start
  0.0 1.9 %copy.27 = bf16[4,2,64,256]{3,0,1,2:T(4,128)(2,1)} copy(bf16[4,2,64,256]{3,2,1,0:T(8,128)(2,1)} %param.6) | data formatting | bytes 524288 | tf_op args[0]
  1.9 4.2 %all-to-all-start = ((bf16[4,2,64,256]{3,0,1,2:T(4,128)(2,1)}), bf16[4,2,64,256]{3,0,1,2:T(4,128)(2,1)S(1)}, u32[]{:S(2)}, u32[]{:S(2)}) async-start(bf16[4,2,64,256]{3,0,1,2:T(4,128)(2,1)} %copy.27), calls=%async_computation | async-start | bytes 524288 | tf_op jit(solution)/shard_map/all_to_all | solution.py:35
  6.1 6.9 %all-gather = s32[4,24,2]{1,2,0:T(2,128)S(1)} all-gather(s32[1,24,2]{1,2,0:T(2,128)} %bitcast.40), channel_id=1, replica_groups=mesh['groups'=2,'date'=4,'col'=4] {'date'}, dimensions={0}, use_global_device_ids=true | all-gather | bytes 960 | tf_op jit(solution)/shard_map/all_gather | solution.py:37
  13.0 0.1 reshape.140
  13.8 1.2 %dynamic-slice = u32[1]{0:T(128)} dynamic-slice(u32[32]{0:T(128)} %constant.69, u32[]{:T(128)S(6)} %add.68), dynamic_slice_sizes={1} | dynamic-slice | bytes 12
  15.0 0.8 %dynamic-update-slice = s32[4]{0:T(128)S(1)} dynamic-update-slice(s32[4]{0:T(128)S(1)} %broadcast.160, s32[1]{0:T(128)S(6)} %copy.39, u32[]{:T(128)} %bitcast.6) | dynamic-update-slice | bytes 12
  15.8 4.3 %all-reduce = s32[4]{0:T(128)S(1)} all-reduce(s32[4]{0:T(128)S(1)} %dynamic-update-slice), channel_id=1, replica_groups=mesh['groups'=2,'date'=4,'col'=4] {'date'}, use_global_device_ids=true, to_apply=%add | all-reduce | flops 4 | bytes 32
  20.0 0.6 fusion.29
  20.7 2.5 %compare_convert_fusion = f32[96]{0:T(128)S(1)} fusion(s32[]{:T(128)} %bitcast.7, s32[]{:T(128)} %bitcast.8, s32[]{:T(128)} %bitcast.10, s32[]{:T(128)} %bitcast.9), kind=kLoop, calls=%fused_computation.45 | loop fusion | flops 3648 | bytes 400 | tf_op jit(solution)/shard_map/convert_element_type | solution.py:41
  23.2 0.0 all-to-all-done
  23.3 0.7 %gather_fusion = bf16[96,2,16,256]{3,2,1,0:T(8,128)(2,1)S(1)} fusion(bf16[16,2,16,256]{3,2,1,0:T(8,128)(2,1)S(1)} %bitcast.36, s32[1024]{0:T(1024)S(1)} %pad_clamp_fusion.1), kind=kCustom, calls=%fused_computation.clone | custom fusion | bytes 3146112 | tf_op jit(solution)/shard_map/jit(_take)/gather | solution.py:44
  24.0 0.7 %gather_fusion.1 = bf16[96,2,16,256]{3,2,1,0:T(8,128)(2,1)S(1)} fusion(bf16[16,2,16,256]{3,2,1,0:T(8,128)(2,1)S(1)} %bitcast.37, s32[1024]{0:T(1024)S(1)} %pad_clamp_fusion), kind=kCustom, calls=%fused_computation.1.clone | custom fusion | bytes 3146112 | tf_op jit(solution)/shard_map/jit(_take)/gather | solution.py:45
  24.7 0.6 broadcast_select_fusion
  25.3 0.5 fusion.2
  25.8 0.3 maximum_multiply_fusion
  26.1 2.2 %fusion.28 = (f32[96,2,16,4]{3,2,1,0:T(8,128)}, f32[96,2,16,4]{3,2,1,0:T(8,128)}) fusion(f32[96,2,16,256]{3,2,1,0:T(8,128)S(1)} %maximum_multiply_fusion), kind=kLoop, calls=%fused_computation.63 | loop fusion | bytes 196608 | tf_op jit(solution)/shard_map/slice | solution.py:12
  28.3 2.2 %copy.30 = f32[96,2,16,4]{0,2,3,1:T(8,128)S(1)} copy(f32[96,2,16,4]{3,2,1,0:T(8,128)} %get-tuple-element.10) | data formatting | bytes 98304 | tf_op jit(solution)/shard_map/slice | solution.py:12
  30.6 4.1 %collective-permute-start = (f32[96,2,16,4]{0,2,3,1:T(8,128)S(1)}, f32[96,2,16,4]{0,2,3,1:T(8,128)S(1)}, u32[]{:S(2)}, u32[]{:S(2)}) collective-permute-start(f32[96,2,16,4]{0,2,3,1:T(8,128)S(1)} %copy.30), channel_id=1, source_target_pairs={{0,1},{1,2},{2,3},{4,5},{5,6},{6,7},{8,9},{9,10},{10,11},{12,13},{... | collective-permute-start | bytes 147464 | tf_op jit(solution)/shard_map/ppermute | solution.py:15
  34.7 2.2 %copy.31 = f32[96,2,16,4]{0,2,3,1:T(8,128)S(1)} copy(f32[96,2,16,4]{3,2,1,0:T(8,128)} %get-tuple-element.11) | data formatting | bytes 98304 | tf_op jit(solution)/shard_map/slice | solution.py:11
  36.9 1.3 %collective-permute-start.1 = (f32[96,2,16,4]{0,2,3,1:T(8,128)S(1)}, f32[96,2,16,4]{0,2,3,1:T(8,128)S(1)}, u32[]{:S(2)}, u32[]{:S(2)}) collective-permute-start(f32[96,2,16,4]{0,2,3,1:T(8,128)S(1)} %copy.31), channel_id=1, source_target_pairs={{1,0},{2,1},{3,2},{5,4},{6,5},{7,6},{9,8},{10,9},{11,10},{13,12},{... | collective-permute-start | bytes 147464 | tf_op jit(solution)/shard_map/ppermute | solution.py:17
  38.2 0.0 collective-permute-done
  38.2 2.3 %copy.32 = f32[96,2,16,4]{3,2,1,0:T(8,128)} copy(f32[96,2,16,4]{0,2,3,1:T(8,128)S(1)} %collective-permute-done) | data formatting | bytes 98304 | tf_op jit(solution)/shard_map/ppermute | solution.py:15
  40.5 2.5 %collective-permute-done.1 = f32[96,2,16,4]{0,2,3,1:T(8,128)S(1)} collective-permute-done((f32[96,2,16,4]{0,2,3,1:T(8,128)S(1)}, f32[96,2,16,4]{0,2,3,1:T(8,128)S(1)}, u32[]{:S(2)}, u32[]{:S(2)}) %collective-permute-start.1) | collective-permute-done | bytes 49184 | tf_op jit(solution)/shard_map/ppermute | solution.py:17
  43.0 2.4 %copy.33 = f32[96,2,16,4]{3,2,1,0:T(8,128)} copy(f32[96,2,16,4]{0,2,3,1:T(8,128)S(1)} %collective-permute-done.1) | data formatting | bytes 98304 | tf_op jit(solution)/shard_map/ppermute | solution.py:17
  45.4 5.8 %pad_maximum_fusion = f32[96,2,16,264]{3,2,1,0:T(8,128)} fusion(f32[96,2,16,4]{3,2,1,0:T(8,128)} %copy.33, f32[96,2,16,256]{3,2,1,0:T(8,128)S(1)} %maximum_multiply_fusion, f32[96,2,16,4]{3,2,1,0:T(8,128)} %copy.32), kind=kLoop, calls=%fused_computation.2 | loop fusion | flops 1622016 | bytes 6488064 | tf_op jit(solution)/shard_map/concatenate | solution.py:13
  51.2 5.7 %copy.34 = f32[96,2,16,264]{0,3,2,1:T(8,128)} copy(f32[96,2,16,264]{3,2,1,0:T(8,128)} %pad_maximum_fusion) | data formatting | bytes 6488064 | tf_op jit(solution)/shard_map/concatenate | solution.py:13
  57.0 2.8 %reduce_sum.9 = f32[96,2,8,264]{0,3,2,1:T(8,128)S(1)} reduce(f32[96,2,8,2,264]{0,4,3,2,1:T(8,128)} %bitcast.38, f32[]{:T(128)} %constant.55.clone.1), dimensions={3}, to_apply=%region_0.2 | reduce | flops 405504 | bytes 4866052 | tf_op jit(solution)/shard_map/reduce_sum | solution.py:57
  59.8 1.7 %fusion = f32[96,2,8,32]{0,3,2,1:T(8,128)S(1)} fusion(f32[96,2,8,264]{0,3,2,1:T(8,128)S(1)} %reduce_sum.9, s32[32]{0:T(128)S(1)} %iota_multiply_fusion), kind=kOutput, calls=%fused_computation.4 | convolution fusion | flops 156203520 | bytes 1818752 | tf_op jit(solution)/shard_map/dot_general | solution.py:58
  61.6 0.0 copy-done
  61.6 1.1 %convolution_bitcast_fusion = f32[15,2,8,32]{3,0,2,1:T(8,128)S(1)} fusion(f32[96,2,8,32]{0,3,2,1:T(8,128)S(1)} %fusion, f32[15,96]{1,0:T(8,128)S(1)} %copy-done), kind=kOutput, calls=%fused_computation.14 | convolution fusion | flops 8847360 | bytes 233088 | tf_op jit(solution)/shard_map/qk,kcrm->qcrm/dot_general | solution.py:65
  62.7 0.7 %copy.35 = f32[15,2,8,32]{3,2,1,0:T(8,128)} copy(f32[15,2,8,32]{3,0,2,1:T(8,128)S(1)} %convolution_bitcast_fusion) | data formatting | bytes 61440 | tf_op jit(solution)/shard_map/qk,kcrm->qcrm/dot_general | solution.py:65
  (8 shorter events, 0.1 us)
Async XLA Ops:
  0.0 61.6 %copy-start = (f32[15,96]{1,0:T(8,128)S(1)}, f32[15,96]{1,0:T(8,128)}, u32[]{:S(2)}) copy-start(f32[15,96]{1,0:T(8,128)} %param.9) | copy-start | bytes 17284
  1.9 21.3 %all-to-all-start = ((bf16[4,2,64,256]{3,0,1,2:T(4,128)(2,1)}), bf16[4,2,64,256]{3,0,1,2:T(4,128)(2,1)S(1)}, u32[]{:S(2)}, u32[]{:S(2)}) async-start(bf16[4,2,64,256]{3,0,1,2:T(4,128)(2,1)} %copy.27), calls=%async_computation | async-start | bytes 524288 | tf_op jit(solution)/shard_map/all_to_all | solution.py:35
  30.6 7.6 %collective-permute-start = (f32[96,2,16,4]{0,2,3,1:T(8,128)S(1)}, f32[96,2,16,4]{0,2,3,1:T(8,128)S(1)}, u32[]{:S(2)}, u32[]{:S(2)}) collective-permute-start(f32[96,2,16,4]{0,2,3,1:T(8,128)S(1)} %copy.30), channel_id=1, source_target_pairs={{0,1},{1,2},{2,3},{4,5},{5,6},{6,7},{8,9},{9,10},{10,11},{12,13},{... | collective-permute-start | bytes 147464 | tf_op jit(solution)/shard_map/ppermute | solution.py:15
  36.9 6.1 %collective-permute-start.1 = (f32[96,2,16,4]{0,2,3,1:T(8,128)S(1)}, f32[96,2,16,4]{0,2,3,1:T(8,128)S(1)}, u32[]{:S(2)}, u32[]{:S(2)}) collective-permute-start(f32[96,2,16,4]{0,2,3,1:T(8,128)S(1)} %copy.31), channel_id=1, source_target_pairs={{1,0},{2,1},{3,2},{5,4},{6,5},{7,6},{9,8},{10,9},{11,10},{13,12},{... | collective-permute-start | bytes 147464 | tf_op jit(solution)/shard_map/ppermute | solution.py:17
where the time goes:
time: 63.9 us; the launch traced here: 63.4 us
  local copies, waits for them, and re-layouts  23.9 us (37%)
  other arithmetic  12.6 us (20%)
  blocking collectives  11.2 us (18%)
  starting transfers between devices  9.58 us (15%)
  matrix products  2.86 us (4%)
  waiting for transfers between devices  2.51 us (4%)
  between operations  0.79 us (1%)
    all_gather x1, blocking collectives, per_device(): lax.all_gather(pair_dates, 'date', axis=0, tiled=True)  6.92 us
    concatenate x1, other arithmetic, padded(): jnp.concatenate([lax.ppermute(tail, axis, [(i, (i + 1) % count) for i in...  5.82 us
    concatenate x1, local copies, waits for them, and re-layouts, padded(): jnp.concatenate([lax.ppermute(tail, axis, [(i, (i + 1) % count) for i in...  5.75 us
    slice x2, local copies, waits for them, and re-layouts, padded(): lax.slice_in_dim(cells, cells.shape[dim] - width, cells.shape[dim], axis=...  4.45 us
    unnamed x1, blocking collectives  4.29 us
    all_to_all x1, starting transfers between devices, per_device(): lax.all_to_all(scenes, 'date', split_axis=2, concat_axis=0, tiled=True)  4.21 us
    ppermute x1, starting transfers between devices, padded(): lax.ppermute(tail, axis, [(i, (i + 1) % count) for i in range(ends)])  4.09 us
    unnamed x7, local copies, waits for them, and re-layouts  3.95 us
  transfers between devices with their start and end apart: 3, of which 1 were waited for; matrix products, arithmetic and copies ran while one was open for 15% of the time, Pallas kernels for 0%

commit v1 on v0

v1 whole, which is shorter than its diff:
```python
import functools

import jax
import jax.numpy as jnp
from jax import lax
from jax.experimental import pallas as pl
from jax.experimental.pallas import tpu as pltpu
from jax.sharding import PartitionSpec as P

F32, BF16 = jnp.float32, jnp.bfloat16
LANES = 128
NOTE_ROWS = 16
IN_VMEM = pl.BlockSpec(memory_space=pltpu.VMEM)
IN_SMEM = pl.BlockSpec(memory_space=pltpu.SMEM)


def round_up(value, step):
    return -(-value // step) * step


def held(array):
    return pltpu.with_memory_space_constraint(array, pltpu.VMEM)


def iota(shape, axis):
    return lax.broadcasted_iota(jnp.int32, shape, axis)


def halves(value):
    high = value.astype(BF16)
    return high, (value - high.astype(F32)).astype(BF16)


def note_of(pair_dates, count):
    slots = pair_dates.shape[0]
    here = iota((slots, LANES), 0) == iota((slots, LANES), 1)
    dates = pair_dates.astype(F32)
    row, lane = iota((NOTE_ROWS, LANES), 0), iota((NOTE_ROWS, LANES), 1)
    note = jnp.where((row == 2) & (lane < jnp.minimum(count, slots)), 1.0, 0.0)
    for side in range(2):
        along = jnp.sum(jnp.where(here, dates[:, side : side + 1], 0.0), axis=0, keepdims=True)
        note = jnp.where(row == side, along, note)
    return note.astype(BF16)


def cut_kernel(count_ref, scenes_ref, dates_ref, inverse_ref, *outs):
    *block_refs, wide_ref = outs
    owners = len(block_refs)
    me = lax.axis_index("date")
    rows = scenes_ref.shape[2] // owners
    note = note_of(dates_ref[...], count_ref[0])
    for step, block_ref in enumerate(block_refs):
        first = pl.multiple_of(lax.rem(me + owners - step, owners) * rows, rows)
        cells = scenes_ref[:, :, pl.ds(first, rows), :]
        height = block_ref.shape[0] - NOTE_ROWS
        block_ref[:height] = cells.reshape(height, block_ref.shape[1])
        block_ref[height:, :LANES] = note
    wide_ref[...] = jnp.zeros_like(wide_ref)
    wide_ref[: inverse_ref.shape[0], : inverse_ref.shape[1]] = inverse_ref[...]


def note_kernel(count_ref, dates_ref, inverse_ref, note_ref, wide_ref):
    note_ref[...] = jnp.zeros_like(note_ref)
    note_ref[:, :LANES] = note_of(dates_ref[...], count_ref[0])
    wide_ref[...] = jnp.zeros_like(wide_ref)
    wide_ref[: inverse_ref.shape[0], : inverse_ref.shape[1]] = inverse_ref[...]


def cut(scenes, pair_dates, pair_count, inverse, owners):
    dates_here, parts, all_rows, columns = scenes.shape
    rows = all_rows // owners
    height = dates_here * parts * rows
    wide = pltpu.VMEM(
        (round_up(inverse.shape[0], 16), round_up(inverse.shape[1], LANES)), F32
    )
    if rows % 16 == 0:
        *blocks, wide = pl.pallas_call(
            cut_kernel,
            out_shape=[pltpu.VMEM((height + NOTE_ROWS, columns), BF16)] * owners + [wide],
            in_specs=[IN_SMEM] + [IN_VMEM] * 3,
            out_specs=[IN_VMEM] * (owners + 1),
        )(pair_count, scenes, pair_dates, inverse)
        return blocks, wide
    note, wide = pl.pallas_call(
        note_kernel,
        out_shape=[pltpu.VMEM((NOTE_ROWS, columns), BF16), wide],
        in_specs=[IN_SMEM] + [IN_VMEM] * 2,
        out_specs=[IN_VMEM] * 2,
    )(pair_count, pair_dates, inverse)
    me = lax.axis_index("date")
    apart = scenes.reshape(dates_here * parts, owners, rows, columns)
    blocks = []
    for step in range(owners):
        cells = lax.dynamic_index_in_dim(apart, lax.rem(me + owners - step, owners), 1, False)
        blocks.append(jnp.concatenate([cells.reshape(height, columns), note], axis=0))
    return blocks, wide


def pair_weights(block_refs, wide, dates_here, slots):
    owners = len(block_refs)
    dates = owners * dates_here
    reach = dates // 2
    me = lax.axis_index("date")
    lanes = wide.shape[1]
    ring = jnp.zeros((8, lanes), F32)
    for step, block_ref in enumerate(block_refs):
        height = block_ref.shape[0]
        note = block_ref[height - NOTE_ROWS : height, :LANES].astype(F32)[:8]
        if lanes > LANES:
            note = jnp.concatenate([note, jnp.zeros((8, lanes - LANES), F32)], axis=1)
        ring = ring + pltpu.roll(note, lax.rem(me + step, owners) * slots, 1)
    start = jnp.full((1, lanes), me * dates_here, jnp.int32).astype(F32)

    def wrapped(value):
        return jnp.where(value < 0.0, value + dates, value)

    first, second = wrapped(ring[0:1] - start), wrapped(ring[1:2] - start)
    ahead = wrapped(second - first)
    onward = ahead <= reach
    place = jnp.where(onward, (ahead - 1.0) * dates + first, (dates - ahead - 1.0) * dates + second)
    place = jnp.where(ring[2:3] > 0.5, place, -1.0)
    pairs = reach * dates
    chosen = jnp.where(iota((pairs, lanes), 0).astype(F32) == place, 1.0, 0.0).astype(BF16)
    signed = jnp.where(onward, wide, -wide)
    stacked = jnp.concatenate([*halves(wide), *halves(signed)], axis=0)
    spread = lax.dot_general(
        stacked, chosen, (((1,), (1,)), ((), ())), preferred_element_type=F32
    )
    tall = wide.shape[0]
    weights = []
    for part in range(2):
        summed = spread[2 * part * tall : (2 * part + 1) * tall]
        summed = summed + spread[(2 * part + 1) * tall : (2 * part + 2) * tall]
        high, low = halves(summed)
        weights.append(
            jnp.concatenate(
                [jnp.concatenate([high, high], axis=1), jnp.concatenate([low, low], axis=1)], axis=0
            )
        )
    return weights


def look_weights(columns):
    looks = columns // 8
    column, look = iota((columns, LANES), 0), iota((columns, LANES), 1)
    target = jnp.where(look == looks + 1, -1, look)
    offset = (column - 8 * target + 4).astype(F32)
    inside = (offset >= 0.0) & (offset < 16.0) & (look < looks + 2)
    return jnp.where(inside, (8.0 - jnp.abs(offset - 7.5)) / 128.0, 0.0).astype(BF16)


def series_kernel(dates_here, slots, *refs):
    *block_refs, wide_ref, looked_ref, first_ref, second_ref, ring_ref, pair_ref = refs
    owners = len(block_refs)
    dates = owners * dates_here
    reach = dates // 2
    pairs = reach * dates
    columns = block_refs[0].shape[1]
    looks = columns // 8
    rows = (block_refs[0].shape[0] - NOTE_ROWS) // (2 * dates_here)
    extent = ring_ref.shape[2] // rows
    tall = wide_ref.shape[0]

    for step, block_ref in enumerate(block_refs):
        for own in range(dates_here):
            for part in range(2):
                at = (own * 2 + part) * rows
                cells = block_ref[at : at + rows].astype(F32)
                date = step * dates_here + own
                for place in range(date, extent, dates):
                    for side in range(columns // LANES):
                        ring_ref[part, side, pl.ds(place, rows, stride=extent), :] = cells[
                            :, side * LANES : (side + 1) * LANES
                        ]

    weights = pair_weights(block_refs, wide_ref[...], dates_here, slots)
    look = look_weights(columns)

    lane = iota((tall, LANES), 1)
    to_right = jnp.zeros((tall, LANES), F32)
    to_left = jnp.zeros((tall, LANES), F32)
    for half_row in range(rows // 2):
        for side in range(columns // LANES):

            def load(part, odd, shift):
                at = (2 * half_row + odd) * extent + shift
                return ring_ref[part, side, at : at + dates, :]

            real_0, real_1, imag_0, imag_1 = (load(c, o, 0) for c in range(2) for o in range(2))
            for shift in range(1, reach + 1):
                other_0, other_1 = load(0, 0, shift), load(0, 1, shift)
                turned_0, turned_1 = load(1, 0, shift), load(1, 1, shift)
                real = (real_0 * other_0 + imag_0 * turned_0) + (
                    real_1 * other_1 + imag_1 * turned_1
                )
                imaginary = (imag_0 * other_0 - real_0 * turned_0) + (
                    imag_1 * other_1 - real_1 * turned_1
                )
                at = (shift - 1) * dates
                for part, value in enumerate((real, imaginary)):
                    high, low = halves(value)
                    across = slice(
                        part * columns + side * LANES, part * columns + (side + 1) * LANES
                    )
                    pair_ref[half_row, at : at + dates, across] = high
                    pair_ref[half_row, pairs + at : pairs + at + dates, across] = low
        for part in range(2):
            summed = jnp.dot(
                weights[part],
                pair_ref[half_row, :, part * columns : (part + 1) * columns],
                preferred_element_type=F32,
            )
            summed = summed[:tall] + summed[tall:]
            looked = jnp.dot(
                jnp.concatenate(halves(summed), axis=0), look, preferred_element_type=F32
            )
            looked = looked[:tall] + looked[tall:]
            index = part * (rows // 2) + half_row
            looked_ref[index * tall : (index + 1) * tall, :] = looked
            to_right = jnp.where(
                lane == index, pltpu.roll(looked, (index - looks) % LANES, 1), to_right
            )
            to_left = jnp.where(
                lane == index, pltpu.roll(looked, (index - looks - 1) % LANES, 1), to_left
            )
    even = lax.rem(lax.axis_index("col"), 2) == 0
    first_ref[...] = jnp.where(even, to_right, to_left)
    second_ref[...] = jnp.where(even, to_left, to_right)


def finish_kernel(looked_ref, first_ref, second_ref, out_ref, sum_ref):
    times, parts, half_rows, looks = out_ref.shape
    tall = first_ref.shape[0]
    here, last = lax.axis_index("col"), lax.axis_size("col") - 1
    even = lax.rem(here, 2) == 0
    first, second = first_ref[...], second_ref[...]
    nothing = jnp.zeros_like(first)
    from_right = jnp.where(here == last, nothing, jnp.where(even, first, second))
    from_left = jnp.where(here == 0, nothing, jnp.where(even, second, first))
    lane = iota((tall, LANES), 1)
    for index in range(parts * half_rows):
        value = looked_ref[index * tall : (index + 1) * tall, :]
        value = value + jnp.where(
            lane == looks - 1, pltpu.roll(from_right, (looks - 1 - index) % LANES, 1), 0.0
        )
        value = value + jnp.where(lane == 0, pltpu.roll(from_left, -index % LANES, 1), 0.0)
        sum_ref[index * tall : (index + 1) * tall, :] = value
    for time in range(times):
        for part in range(parts):
            rows = sum_ref[pl.ds(part * half_rows * tall + time, half_rows, stride=tall), :]
            out_ref[time, part] = rows[:, :looks]


def column_swap(first, owners, count):
    moves = []
    for owner in range(owners):
        for column in range(count):
            partner = column + 1 if (column - first) % 2 == 0 else column - 1
            to = owner
            if not 0 <= partner < count:
                partner = column
                to = owner ^ 1 if owners % 2 == 0 else owner
            moves.append((owner * count + column, to * count + partner))
    return moves


def per_device(scenes, pair_dates, pair_count, inverse):
    owners, count = lax.axis_size("date"), lax.axis_size("col")
    dates_here, parts, all_rows, columns = scenes.shape
    half_rows = all_rows // owners // 2
    dates = owners * dates_here
    reach = dates // 2
    extent = round_up(dates + reach, 8)

    blocks, wide = cut(scenes, pair_dates, pair_count, inverse, owners)
    for step in range(1, owners):
        moves = [(owner, (owner - step) % owners) for owner in range(owners)]
        blocks[step] = lax.ppermute(blocks[step], "date", moves)

    tall = wide.shape[0]
    looked, first, second = pl.pallas_call(
        functools.partial(series_kernel, dates_here, pair_dates.shape[0]),
        out_shape=[
            pltpu.VMEM((parts * half_rows * tall, LANES), F32),
            pltpu.VMEM((tall, LANES), F32),
            pltpu.VMEM((tall, LANES), F32),
        ],
        in_specs=[IN_VMEM] * (owners + 1),
        out_specs=[IN_VMEM] * 3,
        scratch_shapes=[
            pltpu.VMEM((parts, columns // LANES, 2 * half_rows * extent, LANES), F32),
            pltpu.VMEM((half_rows, 2 * reach * dates, parts * columns), BF16),
        ],
        compiler_params=pltpu.CompilerParams(vmem_limit_bytes=40 << 20),
    )(*[held(block) for block in blocks], held(wide))

    first = lax.ppermute(first, ("date", "col"), column_swap(0, owners, count))
    second = lax.ppermute(second, ("date", "col"), column_swap(1, owners, count))
    return pl.pallas_call(
        finish_kernel,
        out_shape=jax.ShapeDtypeStruct(
            (inverse.shape[0], parts, half_rows, columns // 8), F32
        ),
        in_specs=[IN_VMEM] * 3,
        out_specs=IN_VMEM,
        scratch_shapes=[pltpu.VMEM((parts * half_rows * tall, LANES), F32)],
    )(held(looked), held(first), held(second))


def solution(mesh):
    placed = (P("date", None, "groups", "col"), P("date", None), P("date"), P())
    return jax.shard_map(
        per_device,
        mesh=mesh,
        in_specs=placed,
        out_specs=P(None, None, ("groups", "date"), "col"),
        check_vma=False,
    )
```

time: 63.9 us -> 17.8 us (0.28)
  the two profiles are of different devices: /device:TPU:0 before, /device:TPU:16 now
where the time goes in v1:
time: 17.8 us; the launch traced here: 17.6 us
  waiting for transfers between devices  8.1 us (46%)
  Pallas kernels  4.74 us (27%)
  starting transfers between devices  3.38 us (19%)
  local copies, waits for them, and re-layouts  0.7 us (4%)
  between operations  0.68 us (4%)
    ppermute x3, waiting for transfers between devices, per_device(): blocks[step] = lax.ppermute(blocks[step], 'date', moves)  4.46 us
    pallas_call x1, Pallas kernels, per_device(): pl.pallas_call(functools.partial(series_kernel, dates_here, pair_dates.sh...  2.88 us
    ppermute x1, waiting for transfers between devices, per_device(): first = lax.ppermute(first, ('date', 'col'), column_swap(0, owners, count))  2.07 us
    ppermute x3, starting transfers between devices, per_device(): blocks[step] = lax.ppermute(blocks[step], 'date', moves)  1.79 us
    ppermute x1, starting transfers between devices, per_device(): first = lax.ppermute(first, ('date', 'col'), column_swap(0, owners, count))  1.59 us
    ppermute x1, waiting for transfers between devices, per_device(): lax.ppermute(second, ('date', 'col'), column_swap(1, owners, count))  1.58 us
    pallas_call x1, Pallas kernels, cut(): pl.pallas_call(cut_kernel, out_shape=[pltpu.VMEM((height + NOTE_ROWS, col...  1.05 us
    pallas_call x1, Pallas kernels, per_device(): pl.pallas_call(finish_kernel, out_shape=jax.ShapeDtypeStruct((inverse.sha...  0.81 us
  transfers between devices with their start and end apart: 5, of which 5 were waited for; matrix products, arithmetic and copies ran while one was open for 0% of the time, Pallas kernels for 0%

profile of v1, /device:TPU:16, one launch (start us, length us, event | category | flops | bytes accessed | tf_op | source)
XLA Modules:
  0.0 17.6 jit_solution(10220939524588993448)
XLA Ops:
  0.0 0.0 copy-start
  0.7 0.0 copy-done
  0.7 0.7 %copy.5.dates_ref = s32[24,2]{1,0:T(8,128)} copy(s32[24,2]{0,1:T(2,128)S(1)} %copy-done) | data formatting | bytes 384 | tf_op args[1]
  1.4 1.0 %shard_map.46 = (bf16[144,256]{1,0:T(8,128)(2,1)S(1)}, bf16[144,256]{1,0:T(8,128)(2,1)S(1)}, bf16[144,256]{1,0:T(8,128)(2,1)S(1)}, bf16[144,256]{1,0:T(8,128)(2,1)S(1)}, f32[16,128]{1,0:T(8,128)S(1)}) custom-call(s32[1]{0:T(128)S(6)} %copy.6.count_ref, bf16[4,2,64,256]{3,2,1,0:T(8,128)(2,1)} %scenes_ref.1, s32[24,2]{1,0:T(8,128)} %copy.5.dates_ref, ...), custom_call_target="tpu_custom_call" | custom-call | tf_op jit(solution)/shard_map/pallas_call | solution.py:77
  2.4 1.0 %collective-permute-start = (bf16[144,256]{1,0:T(8,128)(2,1)S(1)}, bf16[144,256]{1,0:T(8,128)(2,1)S(1)}, u32[]{:S(2)}, u32[]{:S(2)}) collective-permute-start(bf16[144,256]{1,0:T(8,128)(2,1)S(1)} %get-tuple-element.14), channel_id=1, source_target_pairs={{0,12},{4,0},{8,4},{12,8},{1,13},{5,1},{9,5},{13,9},{2,14},{6,2},{... | collective-permute-start | bytes 221192 | tf_op jit(solution)/shard_map/ppermute | solution.py:278
  3.4 0.6 %collective-permute-start.1 = (bf16[144,256]{1,0:T(8,128)(2,1)S(1)}, bf16[144,256]{1,0:T(8,128)(2,1)S(1)}, u32[]{:S(2)}, u32[]{:S(2)}) collective-permute-start(bf16[144,256]{1,0:T(8,128)(2,1)S(1)} %get-tuple-element.15), channel_id=1, source_target_pairs={{0,8},{4,12},{8,0},{12,4},{1,9},{5,13},{9,1},{13,5},{2,10},{6,14},... | collective-permute-start | bytes 221192 | tf_op jit(solution)/shard_map/ppermute | solution.py:278
  4.0 0.2 collective-permute-start.2
  4.2 1.7 %collective-permute-done.refs_1_ = bf16[144,256]{1,0:T(8,128)(2,1)S(1)} collective-permute-done((bf16[144,256]{1,0:T(8,128)(2,1)S(1)}, bf16[144,256]{1,0:T(8,128)(2,1)S(1)}, u32[]{:S(2)}, u32[]{:S(2)}) %collective-permute-start) | collective-permute-done | bytes 73760 | tf_op jit(solution)/shard_map/ppermute | solution.py:278
  5.9 2.7 %collective-permute-done.1.refs_2_ = bf16[144,256]{1,0:T(8,128)(2,1)S(1)} collective-permute-done((bf16[144,256]{1,0:T(8,128)(2,1)S(1)}, bf16[144,256]{1,0:T(8,128)(2,1)S(1)}, u32[]{:S(2)}, u32[]{:S(2)}) %collective-permute-start.1) | collective-permute-done | bytes 73760 | tf_op jit(solution)/shard_map/ppermute | solution.py:278
  8.6 0.1 collective-permute-done.2.refs_3_
  8.7 2.9 %shard_map.47 = (f32[256,128]{1,0:T(8,128)S(1)}, f32[16,128]{1,0:T(8,128)S(1)}, f32[16,128]{1,0:T(8,128)S(1)}) custom-call(bf16[144,256]{1,0:T(8,128)(2,1)S(1)} %get-tuple-element.13.refs_0_, bf16[144,256]{1,0:T(8,128)(2,1)S(1)} %collective-permute-done.refs_1_, bf16[144,256]{1,0:T(8,128)(2,1)S(1)} %collective-permute-done.1.refs_2_, ...), custom_call_target="tpu_custom_call" | custom-call | tf_op jit(solution)/shard_map/pallas_call | solution.py:281
  11.5 1.6 %collective-permute-start.3 = (f32[16,128]{1,0:T(8,128)S(1)}, f32[16,128]{1,0:T(8,128)S(1)}, u32[]{:S(2)}, u32[]{:S(2)}) collective-permute-start(f32[16,128]{1,0:T(8,128)S(1)} %get-tuple-element.19), channel_id=1, source_target_pairs={{0,1},{1,0},{2,3},{3,2},{4,5},{5,4},{6,7},{7,6},{8,9},{9,8},{10,11... | collective-permute-start | bytes 24584 | tf_op jit(solution)/shard_map/ppermute | solution.py:297
  13.1 0.0 collective-permute-start.4
  13.1 2.1 %collective-permute-done.3.first_ref = f32[16,128]{1,0:T(8,128)S(1)} collective-permute-done((f32[16,128]{1,0:T(8,128)S(1)}, f32[16,128]{1,0:T(8,128)S(1)}, u32[]{:S(2)}, u32[]{:S(2)}) %collective-permute-start.3) | collective-permute-done | bytes 8224 | tf_op jit(solution)/shard_map/ppermute | solution.py:297
  15.2 1.6 %collective-permute-done.4.second_ref = f32[16,128]{1,0:T(8,128)S(1)} collective-permute-done((f32[16,128]{1,0:T(8,128)S(1)}, f32[16,128]{1,0:T(8,128)S(1)}, u32[]{:S(2)}, u32[]{:S(2)}) %collective-permute-start.4) | collective-permute-done | bytes 8224 | tf_op jit(solution)/shard_map/ppermute | solution.py:298
  16.8 0.8 %shard_map.48 = f32[15,2,8,32]{3,2,1,0:T(8,128)} custom-call(f32[256,128]{1,0:T(8,128)S(1)} %get-tuple-element.18.looked_ref, f32[16,128]{1,0:T(8,128)S(1)} %collective-permute-done.3.first_ref, f32[16,128]{1,0:T(8,128)S(1)} %collective-permute-done.4.second_ref), custom_call_target="tpu_custom_call" | custom-call | tf_op jit(solution)/shard_map/pallas_call | solution.py:299
Async XLA Ops:
  0.0 0.7 %copy-start = (s32[24,2]{0,1:T(2,128)S(1)}, s32[24,2]{0,1:T(2,128)}, u32[]{:S(2)}) copy-start(s32[24,2]{0,1:T(2,128)} %param.5) | copy-start | bytes 580
  2.4 3.5 %collective-permute-start = (bf16[144,256]{1,0:T(8,128)(2,1)S(1)}, bf16[144,256]{1,0:T(8,128)(2,1)S(1)}, u32[]{:S(2)}, u32[]{:S(2)}) collective-permute-start(bf16[144,256]{1,0:T(8,128)(2,1)S(1)} %get-tuple-element.14), channel_id=1, source_target_pairs={{0,12},{4,0},{8,4},{12,8},{1,13},{5,1},{9,5},{13,9},{2,14},{6,2},{... | collective-permute-start | bytes 221192 | tf_op jit(solution)/shard_map/ppermute | solution.py:278
  3.4 5.2 %collective-permute-start.1 = (bf16[144,256]{1,0:T(8,128)(2,1)S(1)}, bf16[144,256]{1,0:T(8,128)(2,1)S(1)}, u32[]{:S(2)}, u32[]{:S(2)}) collective-permute-start(bf16[144,256]{1,0:T(8,128)(2,1)S(1)} %get-tuple-element.15), channel_id=1, source_target_pairs={{0,8},{4,12},{8,0},{12,4},{1,9},{5,13},{9,1},{13,5},{2,10},{6,14},... | collective-permute-start | bytes 221192 | tf_op jit(solution)/shard_map/ppermute | solution.py:278
  4.0 4.6 %collective-permute-start.2 = (bf16[144,256]{1,0:T(8,128)(2,1)S(1)}, bf16[144,256]{1,0:T(8,128)(2,1)S(1)}, u32[]{:S(2)}, u32[]{:S(2)}) collective-permute-start(bf16[144,256]{1,0:T(8,128)(2,1)S(1)} %get-tuple-element.16), channel_id=1, source_target_pairs={{0,4},{4,8},{8,12},{12,0},{1,5},{5,9},{9,13},{13,1},{2,6},{6,10},{... | collective-permute-start | bytes 221192 | tf_op jit(solution)/shard_map/ppermute | solution.py:278
  11.5 3.7 %collective-permute-start.3 = (f32[16,128]{1,0:T(8,128)S(1)}, f32[16,128]{1,0:T(8,128)S(1)}, u32[]{:S(2)}, u32[]{:S(2)}) collective-permute-start(f32[16,128]{1,0:T(8,128)S(1)} %get-tuple-element.19), channel_id=1, source_target_pairs={{0,1},{1,0},{2,3},{3,2},{4,5},{5,4},{6,7},{7,6},{8,9},{9,8},{10,11... | collective-permute-start | bytes 24584 | tf_op jit(solution)/shard_map/ppermute | solution.py:297
  13.1 3.7 %collective-permute-start.4 = (f32[16,128]{1,0:T(8,128)S(1)}, f32[16,128]{1,0:T(8,128)S(1)}, u32[]{:S(2)}, u32[]{:S(2)}) collective-permute-start(f32[16,128]{1,0:T(8,128)S(1)} %get-tuple-element.20), channel_id=1, source_target_pairs={{0,4},{1,2},{2,1},{3,7},{4,0},{5,6},{6,5},{7,3},{8,12},{9,10},{10,... | collective-permute-start | bytes 24584 | tf_op jit(solution)/shard_map/ppermute | solution.py:298

commit v2 on v1

--- a/solution.py
+++ b/solution.py
@@ -32,14 +32,12 @@
 
 
 def note_of(pair_dates, count):
-    slots = pair_dates.shape[0]
-    here = iota((slots, LANES), 0) == iota((slots, LANES), 1)
-    dates = pair_dates.astype(F32)
+    slots = pair_dates.shape[1]
+    dates = jnp.concatenate([pair_dates.astype(F32), jnp.zeros((2, LANES - slots), F32)], axis=1)
     row, lane = iota((NOTE_ROWS, LANES), 0), iota((NOTE_ROWS, LANES), 1)
     note = jnp.where((row == 2) & (lane < jnp.minimum(count, slots)), 1.0, 0.0)
     for side in range(2):
-        along = jnp.sum(jnp.where(here, dates[:, side : side + 1], 0.0), axis=0, keepdims=True)
-        note = jnp.where(row == side, along, note)
+        note = jnp.where(row == side, dates[side : side + 1], note)
     return note.astype(BF16)
 
 
@@ -272,8 +270,8 @@
     reach = dates // 2
     extent = round_up(dates + reach, 8)
 
-    blocks, wide = cut(scenes, pair_dates, pair_count, inverse, owners)
-    for step in range(1, owners):
+    blocks, wide = cut(scenes, pair_dates.T, pair_count, inverse, owners)
+    for step in reversed(range(1, owners)):
         moves = [(owner, (owner - step) % owners) for owner in range(owners)]
         blocks[step] = lax.ppermute(blocks[step], "date", moves)
 

time: 17.8 us -> 17 us (0.955)
  local copies, waits for them, and re-layouts: 0.7 us -> 0 us
    unnamed x3 -> x0, local copies, waits for them, and re-layouts: 0.7 us -> none
where the time goes in v2:
time: 17 us; the launch traced here: 16.8 us
  waiting for transfers between devices  8.1 us (48%)
  Pallas kernels  4.68 us (28%)
  starting transfers between devices  3.38 us (20%)
  between operations  0.66 us (4%)
    ppermute x3, waiting for transfers between devices, per_device(): blocks[step] = lax.ppermute(blocks[step], 'date', moves)  4.46 us
    pallas_call x1, Pallas kernels, per_device(): pl.pallas_call(functools.partial(series_kernel, dates_here, pair_dates.sh...  2.88 us
    ppermute x1, waiting for transfers between devices, per_device(): first = lax.ppermute(first, ('date', 'col'), column_swap(0, owners, count))  2.07 us
    ppermute x3, starting transfers between devices, per_device(): blocks[step] = lax.ppermute(blocks[step], 'date', moves)  1.79 us
    ppermute x1, starting transfers between devices, per_device(): first = lax.ppermute(first, ('date', 'col'), column_swap(0, owners, count))  1.59 us
    ppermute x1, waiting for transfers between devices, per_device(): lax.ppermute(second, ('date', 'col'), column_swap(1, owners, count))  1.58 us
    pallas_call x1, Pallas kernels, cut(): pl.pallas_call(cut_kernel, out_shape=[pltpu.VMEM((height + NOTE_ROWS, col...  1 us
    pallas_call x1, Pallas kernels, per_device(): pl.pallas_call(finish_kernel, out_shape=jax.ShapeDtypeStruct((inverse.sha...  0.81 us
  transfers between devices with their start and end apart: 5, of which 5 were waited for; matrix products, arithmetic and copies ran while one was open for 0% of the time, Pallas kernels for 0%

profile of v2, /device:TPU:16, one launch (start us, length us, event | category | flops | bytes accessed | tf_op | source)
XLA Modules:
  0.0 16.8 jit_solution(12778885848206025430)
XLA Ops:
  0.7 1.0 %shard_map.46 = (bf16[144,256]{1,0:T(8,128)(2,1)S(1)}, bf16[144,256]{1,0:T(8,128)(2,1)S(1)}, bf16[144,256]{1,0:T(8,128)(2,1)S(1)}, bf16[144,256]{1,0:T(8,128)(2,1)S(1)}, f32[16,128]{1,0:T(8,128)S(1)}) custom-call(s32[1]{0:T(128)S(6)} %copy.5.count_ref, bf16[4,2,64,256]{3,2,1,0:T(8,128)(2,1)} %scenes_ref.1, s32[2,24]{1,0:T(2,128)} %bitcast.1, ...), custom_call_target="tpu_custom_call" | custom-call | tf_op jit(solution)/shard_map/pallas_call | solution.py:75
  1.7 1.0 %collective-permute-start = (bf16[144,256]{1,0:T(8,128)(2,1)S(1)}, bf16[144,256]{1,0:T(8,128)(2,1)S(1)}, u32[]{:S(2)}, u32[]{:S(2)}) collective-permute-start(bf16[144,256]{1,0:T(8,128)(2,1)S(1)} %get-tuple-element.14), channel_id=1, source_target_pairs={{0,12},{4,0},{8,4},{12,8},{1,13},{5,1},{9,5},{13,9},{2,14},{6,2},{... | collective-permute-start | bytes 221192 | tf_op jit(solution)/shard_map/ppermute | solution.py:276
  2.6 0.6 %collective-permute-start.1 = (bf16[144,256]{1,0:T(8,128)(2,1)S(1)}, bf16[144,256]{1,0:T(8,128)(2,1)S(1)}, u32[]{:S(2)}, u32[]{:S(2)}) collective-permute-start(bf16[144,256]{1,0:T(8,128)(2,1)S(1)} %get-tuple-element.15), channel_id=1, source_target_pairs={{0,8},{4,12},{8,0},{12,4},{1,9},{5,13},{9,1},{13,5},{2,10},{6,14},... | collective-permute-start | bytes 221192 | tf_op jit(solution)/shard_map/ppermute | solution.py:276
  3.3 0.2 collective-permute-start.2
  3.4 1.7 %collective-permute-done.refs_1_ = bf16[144,256]{1,0:T(8,128)(2,1)S(1)} collective-permute-done((bf16[144,256]{1,0:T(8,128)(2,1)S(1)}, bf16[144,256]{1,0:T(8,128)(2,1)S(1)}, u32[]{:S(2)}, u32[]{:S(2)}) %collective-permute-start) | collective-permute-done | bytes 73760 | tf_op jit(solution)/shard_map/ppermute | solution.py:276
  5.2 2.7 %collective-permute-done.1.refs_2_ = bf16[144,256]{1,0:T(8,128)(2,1)S(1)} collective-permute-done((bf16[144,256]{1,0:T(8,128)(2,1)S(1)}, bf16[144,256]{1,0:T(8,128)(2,1)S(1)}, u32[]{:S(2)}, u32[]{:S(2)}) %collective-permute-start.1) | collective-permute-done | bytes 73760 | tf_op jit(solution)/shard_map/ppermute | solution.py:276
  7.8 0.1 collective-permute-done.2.refs_3_
  7.9 2.9 %shard_map.47 = (f32[256,128]{1,0:T(8,128)S(1)}, f32[16,128]{1,0:T(8,128)S(1)}, f32[16,128]{1,0:T(8,128)S(1)}) custom-call(bf16[144,256]{1,0:T(8,128)(2,1)S(1)} %get-tuple-element.13.refs_0_, bf16[144,256]{1,0:T(8,128)(2,1)S(1)} %collective-permute-done.refs_1_, bf16[144,256]{1,0:T(8,128)(2,1)S(1)} %collective-permute-done.1.refs_2_, ...), custom_call_target="tpu_custom_call" | custom-call | tf_op jit(solution)/shard_map/pallas_call | solution.py:279
  10.8 1.6 %collective-permute-start.3 = (f32[16,128]{1,0:T(8,128)S(1)}, f32[16,128]{1,0:T(8,128)S(1)}, u32[]{:S(2)}, u32[]{:S(2)}) collective-permute-start(f32[16,128]{1,0:T(8,128)S(1)} %get-tuple-element.19), channel_id=1, source_target_pairs={{0,1},{1,0},{2,3},{3,2},{4,5},{5,4},{6,7},{7,6},{8,9},{9,8},{10,11... | collective-permute-start | bytes 24584 | tf_op jit(solution)/shard_map/ppermute | solution.py:295
  12.4 0.0 collective-permute-start.4
  12.4 2.1 %collective-permute-done.3.first_ref = f32[16,128]{1,0:T(8,128)S(1)} collective-permute-done((f32[16,128]{1,0:T(8,128)S(1)}, f32[16,128]{1,0:T(8,128)S(1)}, u32[]{:S(2)}, u32[]{:S(2)}) %collective-permute-start.3) | collective-permute-done | bytes 8224 | tf_op jit(solution)/shard_map/ppermute | solution.py:295
  14.4 1.6 %collective-permute-done.4.second_ref = f32[16,128]{1,0:T(8,128)S(1)} collective-permute-done((f32[16,128]{1,0:T(8,128)S(1)}, f32[16,128]{1,0:T(8,128)S(1)}, u32[]{:S(2)}, u32[]{:S(2)}) %collective-permute-start.4) | collective-permute-done | bytes 8224 | tf_op jit(solution)/shard_map/ppermute | solution.py:296
  16.0 0.8 %shard_map.48 = f32[15,2,8,32]{3,2,1,0:T(8,128)} custom-call(f32[256,128]{1,0:T(8,128)S(1)} %get-tuple-element.18.looked_ref, f32[16,128]{1,0:T(8,128)S(1)} %collective-permute-done.3.first_ref, f32[16,128]{1,0:T(8,128)S(1)} %collective-permute-done.4.second_ref), custom_call_target="tpu_custom_call" | custom-call | tf_op jit(solution)/shard_map/pallas_call | solution.py:297
Async XLA Ops:
  1.7 3.5 %collective-permute-start = (bf16[144,256]{1,0:T(8,128)(2,1)S(1)}, bf16[144,256]{1,0:T(8,128)(2,1)S(1)}, u32[]{:S(2)}, u32[]{:S(2)}) collective-permute-start(bf16[144,256]{1,0:T(8,128)(2,1)S(1)} %get-tuple-element.14), channel_id=1, source_target_pairs={{0,12},{4,0},{8,4},{12,8},{1,13},{5,1},{9,5},{13,9},{2,14},{6,2},{... | collective-permute-start | bytes 221192 | tf_op jit(solution)/shard_map/ppermute | solution.py:276
  2.6 5.2 %collective-permute-start.1 = (bf16[144,256]{1,0:T(8,128)(2,1)S(1)}, bf16[144,256]{1,0:T(8,128)(2,1)S(1)}, u32[]{:S(2)}, u32[]{:S(2)}) collective-permute-start(bf16[144,256]{1,0:T(8,128)(2,1)S(1)} %get-tuple-element.15), channel_id=1, source_target_pairs={{0,8},{4,12},{8,0},{12,4},{1,9},{5,13},{9,1},{13,5},{2,10},{6,14},... | collective-permute-start | bytes 221192 | tf_op jit(solution)/shard_map/ppermute | solution.py:276
  3.3 4.6 %collective-permute-start.2 = (bf16[144,256]{1,0:T(8,128)(2,1)S(1)}, bf16[144,256]{1,0:T(8,128)(2,1)S(1)}, u32[]{:S(2)}, u32[]{:S(2)}) collective-permute-start(bf16[144,256]{1,0:T(8,128)(2,1)S(1)} %get-tuple-element.16), channel_id=1, source_target_pairs={{0,4},{4,8},{8,12},{12,0},{1,5},{5,9},{9,13},{13,1},{2,6},{6,10},{... | collective-permute-start | bytes 221192 | tf_op jit(solution)/shard_map/ppermute | solution.py:276
  10.8 3.7 %collective-permute-start.3 = (f32[16,128]{1,0:T(8,128)S(1)}, f32[16,128]{1,0:T(8,128)S(1)}, u32[]{:S(2)}, u32[]{:S(2)}) collective-permute-start(f32[16,128]{1,0:T(8,128)S(1)} %get-tuple-element.19), channel_id=1, source_target_pairs={{0,1},{1,0},{2,3},{3,2},{4,5},{5,4},{6,7},{7,6},{8,9},{9,8},{10,11... | collective-permute-start | bytes 24584 | tf_op jit(solution)/shard_map/ppermute | solution.py:295
  12.4 3.7 %collective-permute-start.4 = (f32[16,128]{1,0:T(8,128)S(1)}, f32[16,128]{1,0:T(8,128)S(1)}, u32[]{:S(2)}, u32[]{:S(2)}) collective-permute-start(f32[16,128]{1,0:T(8,128)S(1)} %get-tuple-element.20), channel_id=1, source_target_pairs={{0,4},{1,2},{2,1},{3,7},{4,0},{5,6},{6,5},{7,3},{8,12},{9,10},{10,... | collective-permute-start | bytes 24584 | tf_op jit(solution)/shard_map/ppermute | solution.py:296

commit v3 on v2

--- a/solution.py
+++ b/solution.py
@@ -148,7 +148,8 @@
 
 
 def series_kernel(dates_here, slots, *refs):
-    *block_refs, wide_ref, looked_ref, first_ref, second_ref, ring_ref, pair_ref = refs
+    *block_refs, wide_ref, looked_ref, first_ref, second_ref, ring_ref, pair_ref, sum_ref = refs
+    block_refs = block_refs[:1] + block_refs[:0:-1]
     owners = len(block_refs)
     dates = owners * dates_here
     reach = dates // 2
@@ -208,19 +209,21 @@
                 pair_ref[half_row, :, part * columns : (part + 1) * columns],
                 preferred_element_type=F32,
             )
-            summed = summed[:tall] + summed[tall:]
-            looked = jnp.dot(
-                jnp.concatenate(halves(summed), axis=0), look, preferred_element_type=F32
-            )
-            looked = looked[:tall] + looked[tall:]
-            index = part * (rows // 2) + half_row
-            looked_ref[index * tall : (index + 1) * tall, :] = looked
-            to_right = jnp.where(
-                lane == index, pltpu.roll(looked, (index - looks) % LANES, 1), to_right
-            )
-            to_left = jnp.where(
-                lane == index, pltpu.roll(looked, (index - looks - 1) % LANES, 1), to_left
-            )
+            high, low = halves(summed[:tall] + summed[tall:])
+            at = (part * (rows // 2) + half_row) * tall
+            sum_ref[0, at : at + tall, :] = high
+            sum_ref[1, at : at + tall, :] = low
+    looked = jnp.dot(sum_ref[0], look, preferred_element_type=F32)
+    looked = looked + jnp.dot(sum_ref[1], look, preferred_element_type=F32)
+    looked_ref[...] = looked
+    for index in range(rows):
+        one = looked[index * tall : (index + 1) * tall]
+        to_right = jnp.where(
+            lane == index, pltpu.roll(one, (index - looks) % LANES, 1), to_right
+        )
+        to_left = jnp.where(
+            lane == index, pltpu.roll(one, (index - looks - 1) % LANES, 1), to_left
+        )
     even = lax.rem(lax.axis_index("col"), 2) == 0
     first_ref[...] = jnp.where(even, to_right, to_left)
     second_ref[...] = jnp.where(even, to_left, to_right)
@@ -271,7 +274,7 @@
     extent = round_up(dates + reach, 8)
 
     blocks, wide = cut(scenes, pair_dates.T, pair_count, inverse, owners)
-    for step in reversed(range(1, owners)):
+    for step in range(1, owners):
         moves = [(owner, (owner - step) % owners) for owner in range(owners)]
         blocks[step] = lax.ppermute(blocks[step], "date", moves)
 
@@ -288,9 +291,10 @@
         scratch_shapes=[
             pltpu.VMEM((parts, columns // LANES, 2 * half_rows * extent, LANES), F32),
             pltpu.VMEM((half_rows, 2 * reach * dates, parts * columns), BF16),
+            pltpu.VMEM((2, parts * half_rows * tall, columns), BF16),
         ],
         compiler_params=pltpu.CompilerParams(vmem_limit_bytes=40 << 20),
-    )(*[held(block) for block in blocks], held(wide))
+    )(*[held(block) for block in blocks[:1] + blocks[:0:-1]], held(wide))
 
     first = lax.ppermute(first, ("date", "col"), column_swap(0, owners, count))
     second = lax.ppermute(second, ("date", "col"), column_swap(1, owners, count))

time: 17 us -> 15 us (0.88)
  the two profiles are of different devices: /device:TPU:16 before, /device:TPU:18 now
where the time goes in v3:
time: 15 us; the launch traced here: 14.8 us
  waiting for transfers between devices  6.82 us (45%)
  starting transfers between devices  3.69 us (25%)
  Pallas kernels  3.65 us (24%)
  between operations  0.68 us (5%)
    ppermute x3, waiting for transfers between devices, per_device(): blocks[step] = lax.ppermute(blocks[step], 'date', moves)  3.17 us
    ppermute x1, waiting for transfers between devices, per_device(): first = lax.ppermute(first, ('date', 'col'), column_swap(0, owners, count))  2.07 us
    ppermute x3, starting transfers between devices, per_device(): blocks[step] = lax.ppermute(blocks[step], 'date', moves)  2.05 us
    pallas_call x1, Pallas kernels, per_device(): pl.pallas_call(functools.partial(series_kernel, dates_here, pair_dates.sh...  1.84 us
    ppermute x1, starting transfers between devices, per_device(): first = lax.ppermute(first, ('date', 'col'), column_swap(0, owners, count))  1.64 us
    ppermute x1, waiting for transfers between devices, per_device(): lax.ppermute(second, ('date', 'col'), column_swap(1, owners, count))  1.58 us
    pallas_call x1, Pallas kernels, cut(): pl.pallas_call(cut_kernel, out_shape=[pltpu.VMEM((height + NOTE_ROWS, col...  1 us
    pallas_call x1, Pallas kernels, per_device(): pl.pallas_call(finish_kernel, out_shape=jax.ShapeDtypeStruct((inverse.sha...  0.81 us
  transfers between devices with their start and end apart: 5, of which 4 were waited for; matrix products, arithmetic and copies ran while one was open for 0% of the time, Pallas kernels for 0%

profile of v3, /device:TPU:18, one launch (start us, length us, event | category | flops | bytes accessed | tf_op | source)
XLA Modules:
  0.0 14.8 jit_solution(15670707028366128690)
XLA Ops:
  0.7 1.0 %shard_map.46 = (bf16[144,256]{1,0:T(8,128)(2,1)S(1)}, bf16[144,256]{1,0:T(8,128)(2,1)S(1)}, bf16[144,256]{1,0:T(8,128)(2,1)S(1)}, bf16[144,256]{1,0:T(8,128)(2,1)S(1)}, f32[16,128]{1,0:T(8,128)S(1)}) custom-call(s32[1]{0:T(128)S(6)} %copy.5.count_ref, bf16[4,2,64,256]{3,2,1,0:T(8,128)(2,1)} %scenes_ref.1, s32[2,24]{1,0:T(2,128)} %bitcast.1, ...), custom_call_target="tpu_custom_call" | custom-call | tf_op jit(solution)/shard_map/pallas_call | solution.py:75
  1.7 0.1 collective-permute-start
  1.7 0.6 %collective-permute-start.1 = (bf16[144,256]{1,0:T(8,128)(2,1)S(1)}, bf16[144,256]{1,0:T(8,128)(2,1)S(1)}, u32[]{:S(2)}, u32[]{:S(2)}) collective-permute-start(bf16[144,256]{1,0:T(8,128)(2,1)S(1)} %get-tuple-element.15), channel_id=1, source_target_pairs={{0,8},{4,12},{8,0},{12,4},{1,9},{5,13},{9,1},{13,5},{2,10},{6,14},... | collective-permute-start | bytes 221192 | tf_op jit(solution)/shard_map/ppermute | solution.py:279
  2.3 1.4 %collective-permute-start.2 = (bf16[144,256]{1,0:T(8,128)(2,1)S(1)}, bf16[144,256]{1,0:T(8,128)(2,1)S(1)}, u32[]{:S(2)}, u32[]{:S(2)}) collective-permute-start(bf16[144,256]{1,0:T(8,128)(2,1)S(1)} %get-tuple-element.16), channel_id=1, source_target_pairs={{0,12},{4,0},{8,4},{12,8},{1,13},{5,1},{9,5},{13,9},{2,14},{6,2},{... | collective-permute-start | bytes 221192 | tf_op jit(solution)/shard_map/ppermute | solution.py:279
  3.7 2.0 %collective-permute-done.refs_1_ = bf16[144,256]{1,0:T(8,128)(2,1)S(1)} collective-permute-done((bf16[144,256]{1,0:T(8,128)(2,1)S(1)}, bf16[144,256]{1,0:T(8,128)(2,1)S(1)}, u32[]{:S(2)}, u32[]{:S(2)}) %collective-permute-start) | collective-permute-done | bytes 73760 | tf_op jit(solution)/shard_map/ppermute | solution.py:279
  5.7 1.2 %collective-permute-done.1.refs_2_ = bf16[144,256]{1,0:T(8,128)(2,1)S(1)} collective-permute-done((bf16[144,256]{1,0:T(8,128)(2,1)S(1)}, bf16[144,256]{1,0:T(8,128)(2,1)S(1)}, u32[]{:S(2)}, u32[]{:S(2)}) %collective-permute-start.1) | collective-permute-done | bytes 73760 | tf_op jit(solution)/shard_map/ppermute | solution.py:279
  6.9 0.0 collective-permute-done.2.refs_3_
  6.9 1.8 %shard_map.47 = (f32[256,128]{1,0:T(8,128)S(1)}, f32[16,128]{1,0:T(8,128)S(1)}, f32[16,128]{1,0:T(8,128)S(1)}) custom-call(bf16[144,256]{1,0:T(8,128)(2,1)S(1)} %get-tuple-element.13.refs_0_, bf16[144,256]{1,0:T(8,128)(2,1)S(1)} %collective-permute-done.refs_1_, bf16[144,256]{1,0:T(8,128)(2,1)S(1)} %collective-permute-done.1.refs_2_, ...), custom_call_target="tpu_custom_call" | custom-call | tf_op jit(solution)/shard_map/pallas_call | solution.py:282
  8.7 1.6 %collective-permute-start.3 = (f32[16,128]{1,0:T(8,128)S(1)}, f32[16,128]{1,0:T(8,128)S(1)}, u32[]{:S(2)}, u32[]{:S(2)}) collective-permute-start(f32[16,128]{1,0:T(8,128)S(1)} %get-tuple-element.19), channel_id=1, source_target_pairs={{0,1},{1,0},{2,3},{3,2},{4,5},{5,4},{6,7},{7,6},{8,9},{9,8},{10,11... | collective-permute-start | bytes 24584 | tf_op jit(solution)/shard_map/ppermute | solution.py:299
  10.4 0.0 collective-permute-start.4
  10.4 2.1 %collective-permute-done.3.first_ref = f32[16,128]{1,0:T(8,128)S(1)} collective-permute-done((f32[16,128]{1,0:T(8,128)S(1)}, f32[16,128]{1,0:T(8,128)S(1)}, u32[]{:S(2)}, u32[]{:S(2)}) %collective-permute-start.3) | collective-permute-done | bytes 8224 | tf_op jit(solution)/shard_map/ppermute | solution.py:299
  12.4 1.6 %collective-permute-done.4.second_ref = f32[16,128]{1,0:T(8,128)S(1)} collective-permute-done((f32[16,128]{1,0:T(8,128)S(1)}, f32[16,128]{1,0:T(8,128)S(1)}, u32[]{:S(2)}, u32[]{:S(2)}) %collective-permute-start.4) | collective-permute-done | bytes 8224 | tf_op jit(solution)/shard_map/ppermute | solution.py:300
  14.0 0.8 %shard_map.48 = f32[15,2,8,32]{3,2,1,0:T(8,128)} custom-call(f32[256,128]{1,0:T(8,128)S(1)} %get-tuple-element.18.looked_ref, f32[16,128]{1,0:T(8,128)S(1)} %collective-permute-done.3.first_ref, f32[16,128]{1,0:T(8,128)S(1)} %collective-permute-done.4.second_ref), custom_call_target="tpu_custom_call" | custom-call | tf_op jit(solution)/shard_map/pallas_call | solution.py:301
Async XLA Ops:
  1.7 4.0 %collective-permute-start = (bf16[144,256]{1,0:T(8,128)(2,1)S(1)}, bf16[144,256]{1,0:T(8,128)(2,1)S(1)}, u32[]{:S(2)}, u32[]{:S(2)}) collective-permute-start(bf16[144,256]{1,0:T(8,128)(2,1)S(1)} %get-tuple-element.14), channel_id=1, source_target_pairs={{0,4},{4,8},{8,12},{12,0},{1,5},{5,9},{9,13},{13,1},{2,6},{6,10},{... | collective-permute-start | bytes 221192 | tf_op jit(solution)/shard_map/ppermute | solution.py:279
  1.7 5.2 %collective-permute-start.1 = (bf16[144,256]{1,0:T(8,128)(2,1)S(1)}, bf16[144,256]{1,0:T(8,128)(2,1)S(1)}, u32[]{:S(2)}, u32[]{:S(2)}) collective-permute-start(bf16[144,256]{1,0:T(8,128)(2,1)S(1)} %get-tuple-element.15), channel_id=1, source_target_pairs={{0,8},{4,12},{8,0},{12,4},{1,9},{5,13},{9,1},{13,5},{2,10},{6,14},... | collective-permute-start | bytes 221192 | tf_op jit(solution)/shard_map/ppermute | solution.py:279
  2.3 4.6 %collective-permute-start.2 = (bf16[144,256]{1,0:T(8,128)(2,1)S(1)}, bf16[144,256]{1,0:T(8,128)(2,1)S(1)}, u32[]{:S(2)}, u32[]{:S(2)}) collective-permute-start(bf16[144,256]{1,0:T(8,128)(2,1)S(1)} %get-tuple-element.16), channel_id=1, source_target_pairs={{0,12},{4,0},{8,4},{12,8},{1,13},{5,1},{9,5},{13,9},{2,14},{6,2},{... | collective-permute-start | bytes 221192 | tf_op jit(solution)/shard_map/ppermute | solution.py:279
  8.7 3.7 %collective-permute-start.3 = (f32[16,128]{1,0:T(8,128)S(1)}, f32[16,128]{1,0:T(8,128)S(1)}, u32[]{:S(2)}, u32[]{:S(2)}) collective-permute-start(f32[16,128]{1,0:T(8,128)S(1)} %get-tuple-element.19), channel_id=1, source_target_pairs={{0,1},{1,0},{2,3},{3,2},{4,5},{5,4},{6,7},{7,6},{8,9},{9,8},{10,11... | collective-permute-start | bytes 24584 | tf_op jit(solution)/shard_map/ppermute | solution.py:299
  10.4 3.7 %collective-permute-start.4 = (f32[16,128]{1,0:T(8,128)S(1)}, f32[16,128]{1,0:T(8,128)S(1)}, u32[]{:S(2)}, u32[]{:S(2)}) collective-permute-start(f32[16,128]{1,0:T(8,128)S(1)} %get-tuple-element.20), channel_id=1, source_target_pairs={{0,4},{1,2},{2,1},{3,7},{4,0},{5,6},{6,5},{7,3},{8,12},{9,10},{10,... | collective-permute-start | bytes 24584 | tf_op jit(solution)/shard_map/ppermute | solution.py:300

commit v4 on v2

v4 whole, which is shorter than its diff:
```python
import functools

import jax
import jax.numpy as jnp
from jax import lax
from jax.experimental import pallas as pl
from jax.experimental.pallas import tpu as pltpu
from jax.sharding import PartitionSpec as P

F32, BF16 = jnp.float32, jnp.bfloat16
LANES = 128
NOTE_ROWS = 16
GROUP = 8
IN_VMEM = pl.BlockSpec(memory_space=pltpu.VMEM)
IN_SMEM = pl.BlockSpec(memory_space=pltpu.SMEM)


def round_up(value, step):
    return -(-value // step) * step


def held(array):
    return pltpu.with_memory_space_constraint(array, pltpu.VMEM)


def iota(shape, axis):
    return lax.broadcasted_iota(jnp.int32, shape, axis)


def halves(value):
    high = value.astype(BF16)
    return high, (value - high.astype(F32)).astype(BF16)


def note_of(pair_dates, count):
    slots = pair_dates.shape[1]
    dates = jnp.concatenate([pair_dates.astype(F32), jnp.zeros((2, LANES - slots), F32)], axis=1)
    row, lane = iota((NOTE_ROWS, LANES), 0), iota((NOTE_ROWS, LANES), 1)
    note = jnp.where((row == 2) & (lane < jnp.minimum(count, slots)), 1.0, 0.0)
    for side in range(2):
        note = jnp.where(row == side, dates[side : side + 1], note)
    return note.astype(BF16)


def cut_kernel(count_ref, scenes_ref, dates_ref, inverse_ref, *outs):
    *block_refs, wide_ref = outs
    owners = len(block_refs)
    me = lax.axis_index("date")
    rows = scenes_ref.shape[2] // owners
    note = note_of(dates_ref[...], count_ref[0])
    for step, block_ref in enumerate(block_refs):
        first = pl.multiple_of(lax.rem(me + owners - step, owners) * rows, rows)
        cells = scenes_ref[:, :, pl.ds(first, rows), :]
        height = block_ref.shape[0] - NOTE_ROWS
        block_ref[:height] = cells.reshape(height, block_ref.shape[1])
        block_ref[height:, :LANES] = note
    wide_ref[...] = jnp.zeros_like(wide_ref)
    wide_ref[: inverse_ref.shape[0], : inverse_ref.shape[1]] = inverse_ref[...]


def note_kernel(count_ref, dates_ref, inverse_ref, note_ref, wide_ref):
    note_ref[...] = jnp.zeros_like(note_ref)
    note_ref[:, :LANES] = note_of(dates_ref[...], count_ref[0])
    wide_ref[...] = jnp.zeros_like(wide_ref)
    wide_ref[: inverse_ref.shape[0], : inverse_ref.shape[1]] = inverse_ref[...]


def cut(scenes, pair_dates, pair_count, inverse, owners):
    dates_here, parts, all_rows, columns = scenes.shape
    rows = all_rows // owners
    height = dates_here * parts * rows
    wide = pltpu.VMEM(
        (round_up(inverse.shape[0], 16), round_up(inverse.shape[1], LANES)), F32
    )
    if rows % 16 == 0:
        *blocks, wide = pl.pallas_call(
            cut_kernel,
            out_shape=[pltpu.VMEM((height + NOTE_ROWS, columns), BF16)] * owners + [wide],
            in_specs=[IN_SMEM] + [IN_VMEM] * 3,
            out_specs=[IN_VMEM] * (owners + 1),
        )(pair_count, scenes, pair_dates, inverse)
        return blocks, wide
    note, wide = pl.pallas_call(
        note_kernel,
        out_shape=[pltpu.VMEM((NOTE_ROWS, columns), BF16), wide],
        in_specs=[IN_SMEM] + [IN_VMEM] * 2,
        out_specs=[IN_VMEM] * 2,
    )(pair_count, pair_dates, inverse)
    me = lax.axis_index("date")
    apart = scenes.reshape(dates_here * parts, owners, rows, columns)
    blocks = []
    for step in range(owners):
        cells = lax.dynamic_index_in_dim(apart, lax.rem(me + owners - step, owners), 1, False)
        blocks.append(jnp.concatenate([cells.reshape(height, columns), note], axis=0))
    return blocks, wide


def pair_places(first, second, dates):
    groups = dates // GROUP

    def group_of(date):
        return jnp.floor(date * (1.0 / GROUP))

    first_group, second_group = group_of(first), group_of(second)
    first_seat, second_seat = first - GROUP * first_group, second - GROUP * second_group
    ahead = second_seat - first_seat
    ahead = jnp.where(ahead < 0.0, ahead + GROUP, ahead)
    behind = jnp.where(ahead > 0.0, GROUP - ahead, 0.0)
    near = ahead <= GROUP // 2
    inside = first_group * (GROUP * GROUP // 2)
    inside = inside + jnp.where(
        near, (ahead - 1.0) * GROUP + first_seat, (behind - 1.0) * GROUP + second_seat
    )
    upward = first_group < second_group
    low, high = jnp.minimum(first_group, second_group), jnp.maximum(first_group, second_group)
    between = low * (2 * groups - 1.0 - low) * 0.5 + high - low - 1.0
    across = groups * (GROUP * GROUP // 2) + between * (GROUP * GROUP)
    across = across + jnp.where(
        upward, ahead * GROUP + first_seat, behind * GROUP + second_seat
    )
    same = first_group == second_group
    sign = jnp.where(same, jnp.where(near, 1.0, -1.0), jnp.where(upward, 1.0, -1.0))
    return jnp.where(same, inside, across), sign


def pair_weights(block_refs, wide, dates_here, slots):
    owners = len(block_refs)
    dates = owners * dates_here
    me = lax.axis_index("date")
    lanes = wide.shape[1]
    ring = jnp.zeros((8, lanes), F32)
    for step, block_ref in enumerate(block_refs):
        height = block_ref.shape[0]
        note = block_ref[height - NOTE_ROWS : height, :LANES].astype(F32)[:8]
        if lanes > LANES:
            note = jnp.concatenate([note, jnp.zeros((8, lanes - LANES), F32)], axis=1)
        ring = ring + pltpu.roll(note, lax.rem(me + step, owners) * slots, 1)
    start = lax.rem(me + owners - 1, owners) * dates_here
    start = jnp.full((1, lanes), start, jnp.int32).astype(F32)

    def wrapped(value):
        return jnp.where(value < 0.0, value + dates, value)

    place, sign = pair_places(wrapped(ring[0:1] - start), wrapped(ring[1:2] - start), dates)
    place = jnp.where(ring[2:3] > 0.5, place, -1.0)
    pairs = pair_rows(dates)
    chosen = jnp.where(iota((pairs, lanes), 0).astype(F32) == place, 1.0, 0.0).astype(BF16)
    scaled = wide * (1.0 / 128.0)
    signed = scaled * sign
    stacked = jnp.concatenate([*halves(scaled), *halves(signed)], axis=0)
    spread = lax.dot_general(
        stacked, chosen, (((1,), (1,)), ((), ())), preferred_element_type=F32
    )
    tall = wide.shape[0]
    weights = []
    for part in range(2):
        summed = spread[2 * part * tall : (2 * part + 1) * tall]
        summed = summed + spread[(2 * part + 1) * tall : (2 * part + 2) * tall]
        high, low = halves(summed)
        weights.append(
            jnp.concatenate(
                [jnp.concatenate([high, high], axis=1), jnp.concatenate([low, low], axis=1)], axis=0
            )
        )
    return weights


def pair_rows(dates):
    groups = dates // GROUP
    return GROUP * GROUP // 2 * groups + GROUP * GROUP * (groups * (groups - 1) // 2)


def pair_units(dates):
    groups = dates // GROUP
    half = GROUP // 2
    units = [(group, group, range(1, half + 1)) for group in range(groups)]
    for low in range(groups):
        for high in range(low + 1, groups):
            units += [(low, high, range(at, at + half)) for at in range(0, GROUP, half)]
    return units


def comb_of(columns):
    looks = columns // 8
    column, lane = iota((columns, columns), 0), iota((columns, columns), 1)
    here = (column // 8 == lane % looks) & (column % 8 == lane // looks)
    return jnp.where(here, 1.0, 0.0).astype(BF16)


def spread_block(block_ref, comb, dates_here, seat, rows_ref):
    height = block_ref.shape[0] - NOTE_ROWS
    rows = height // (2 * dates_here)
    combed = jnp.dot(block_ref[:height], comb, preferred_element_type=F32)
    for own in range(dates_here):
        for part in range(2):
            at = (own * 2 + part) * rows
            for side in range(rows_ref.shape[1]):
                rows_ref[part, side, pl.ds(seat + own, rows, stride=GROUP), :] = combed[
                    at : at + rows, side * LANES : (side + 1) * LANES
                ]


def pack_group(rows_ref, looks, half_rows, store):
    pack = LANES // looks
    lane = iota((GROUP, LANES), 1)
    for part in range(2):
        for odd in range(2):
            for tile in range(-(-half_rows // pack)):
                for side in range(rows_ref.shape[1]):
                    cells = []
                    for near in range(pack):
                        half_row = tile * pack + near
                        at = (2 * half_row + odd) * GROUP
                        if half_row < half_rows:
                            cells.append(rows_ref[part, side, at : at + GROUP, :])
                        else:
                            cells.append(jnp.zeros((GROUP, LANES), F32))
                    bit = pack // 2
                    while bit:
                        clear = (lane // looks) & bit == 0
                        for near in range(pack):
                            if not near & bit:
                                one, two = cells[near], cells[near + bit]
                                cells[near] = jnp.where(
                                    clear, one, pltpu.roll(two, bit * looks, 1)
                                )
                                cells[near + bit] = jnp.where(
                                    clear, pltpu.roll(one, LANES - bit * looks, 1), two
                                )
                        bit //= 2
                    for near in range(pack):
                        store(part, odd, side * pack + near, tile, cells[near])


def unit_products(tiles, looks, turns, mine_of, turned_of, store):
    lane = iota((GROUP, LANES), 1) % looks
    at_first, at_last = lane == 0, lane == looks - 1
    rims = [None] * (2 * len(turns))
    for tile in range(tiles):

        def product(place):
            mine = [[mine_of(part, odd, place, tile) for odd in range(2)] for part in range(2)]
            values = []
            for turn in turns:
                other = [
                    [turned_of(part, odd, place, tile, turn, mine) for odd in range(2)]
                    for part in range(2)
                ]
                real = (mine[0][0] * other[0][0] + mine[1][0] * other[1][0]) + (
                    mine[0][1] * other[0][1] + mine[1][1] * other[1][1]
                )
                imaginary = (mine[1][0] * other[0][0] - mine[0][0] * other[1][0]) + (
                    mine[1][1] * other[0][1] - mine[0][1] * other[1][1]
                )
                values += [real, imaginary]
            return values

        def running(places):
            total = product(places[0])
            ramp = total
            for place in places[1:]:
                total = [one + two for one, two in zip(total, product(place))]
                share = [0.5 * one for one in total] if place is places[-1] else total
                ramp = [one + two for one, two in zip(ramp, share)]
            return total, ramp

        early, to_left = running((0, 1, 2, 3))
        late, to_right = running((7, 6, 5, 4))
        values = []
        for index in range(len(early)):
            before = pltpu.roll(to_right[index], 1, 1)
            after = pltpu.roll(to_left[index], LANES - 1, 1)
            value = 8.0 * (early[index] + late[index]) - to_left[index] - to_right[index]
            value = value + jnp.where(at_first, 0.0, before) + jnp.where(at_last, 0.0, after)
            values.append(value)
            edge = jnp.where(at_first, before, jnp.where(at_last, after, 0.0))
            if tile:
                edge = rims[index] + pltpu.roll(edge, 2 * tile, 1)
            rims[index] = edge
        for part in range(2):
            store(part, tile, jnp.concatenate(values[part::2], axis=0))
    for part in range(2):
        store(part, tiles, jnp.concatenate(rims[part::2], axis=0))


def turn_here(part, odd, place, tile, turn, mine):
    return pltpu.roll(mine[part][odd], GROUP - turn, 0)


def early_kernel(dates_here, *refs):
    *block_refs, ring_ref, pair_ref, rows_ref = refs
    columns = block_refs[0].shape[1]
    looks = columns // 8
    tiles = ring_ref.shape[3]
    half_rows = rows_ref.shape[2] // GROUP // 2
    comb = comb_of(columns)
    for index, block_ref in enumerate(block_refs):
        spread_block(block_ref, comb, dates_here, index * dates_here, rows_ref)

    def keep(part, odd, place, tile, cells):
        ring_ref[part, odd, place, tile] = cells

    pack_group(rows_ref, looks, half_rows, keep)

    def store(part, tile, value):
        across = slice(tile * LANES, (tile + 1) * LANES)
        high, low = halves(value)
        pair_ref[part, 0, :, across] = high
        pair_ref[part, 1, :, across] = low

    unit_products(
        tiles,
        looks,
        range(1, GROUP // 2 + 1),
        lambda part, odd, place, tile: ring_ref[part, odd, place, tile],
        turn_here,
        store,
    )


def series_kernel(dates_here, slots, *refs):
    *refs, looked_ref, edge_ref, rows_ref, ring_ref, far_ref, pair_ref = refs
    *block_refs, wide_ref, first_ref, first_pair_ref = refs
    block_refs = block_refs[::-1]
    owners = len(block_refs)
    dates = owners * dates_here
    groups = dates // GROUP
    pairs = pair_rows(dates)
    columns = block_refs[0].shape[1]
    looks = columns // 8
    tiles = ring_ref.shape[4]
    half_rows = rows_ref.shape[2] // GROUP // 2
    tall = wide_ref.shape[0]
    together = GROUP // dates_here

    comb = comb_of(columns)
    for group in range(1, groups):
        for index in range(together):
            block_ref = block_refs[group * together + index - 1]
            spread_block(block_ref, comb, dates_here, index * dates_here, rows_ref)

        def keep(part, odd, place, tile, cells):
            ring_ref[group - 1, part, odd, place, tile] = cells
            for copy in range(2):
                at = pl.ds(2 * copy * GROUP + odd, GROUP, stride=2)
                far_ref[group - 1, part, place, tile, at, :] = cells

        pack_group(rows_ref, looks, half_rows, keep)

    weights = pair_weights(block_refs, wide_ref[...], dates_here, slots)

    across = first_pair_ref.shape[3]
    for part in range(2):
        for half in range(2):
            at = half * pairs
            pair_ref[part, at : at + first_pair_ref.shape[2], :across] = first_pair_ref[part, half]
    for unit, (low, high, turns) in enumerate(pair_units(dates)):
        if high == 0:
            continue

        def mine_of(part, odd, place, tile):
            if low == 0:
                return first_ref[part, odd, place, tile]
            return ring_ref[low - 1, part, odd, place, tile]

        def turn_far(part, odd, place, tile, turn, mine):
            at = pl.ds(2 * turn + odd, GROUP, stride=2)
            return far_ref[high - 1, part, place, tile, at, :]

        def store(part, tile, value):
            count = value.shape[0]
            across = slice(tile * LANES, (tile + 1) * LANES)
            bits = halves(value)
            for half in range(2):
                at = half * pairs + unit * count
                pair_ref[part, at : at + count, across] = bits[half]

        turned_of = turn_here if low == high else turn_far
        unit_products(tiles, looks, turns, mine_of, turned_of, store)
    message = jnp.zeros((tall, LANES), F32)
    for part in range(2):
        summed = jnp.dot(weights[part], pair_ref[part], preferred_element_type=F32)
        summed = summed[:tall] + summed[tall:]
        looked_ref[part] = summed[:, : tiles * LANES]
        edge = summed[:, tiles * LANES :]
        message = message + (pltpu.roll(edge, 2 * tiles, 1) if part else edge)
    edge_ref[...] = message


def finish_kernel(looked_ref, second_ref, first_ref, out_ref, sum_ref):
    times, parts, half_rows, looks = out_ref.shape
    tall = first_ref.shape[0]
    pack = LANES // looks
    tiles = looked_ref.shape[2] // LANES
    here, last = lax.axis_index("col"), lax.axis_size("col") - 1
    even = lax.rem(here, 2) == 0
    first, second = first_ref[...], second_ref[...]
    nothing = jnp.zeros_like(first)
    from_right = jnp.where(here == last, nothing, jnp.where(even, first, second))
    from_left = jnp.where(here == 0, nothing, jnp.where(even, second, first))
    lane = iota((tall, LANES), 1) % looks
    for part in range(parts):
        for tile in range(tiles):
            shift = 2 * (tile + tiles * part)
            value = looked_ref[part, :, tile * LANES : (tile + 1) * LANES]
            right = pltpu.roll(from_right, (looks - shift) % LANES, 1)
            left = pltpu.roll(from_left, (-looks - shift) % LANES, 1)
            value = value + jnp.where(lane == looks - 1, right, 0.0)
            value = value + jnp.where(lane == 0, left, 0.0)
            for near in range(min(pack, half_rows - tile * pack)):
                at = (part * half_rows + tile * pack + near) * tall
                sum_ref[at : at + tall, :] = pltpu.roll(value, -near * looks % LANES, 1)
    for time in range(times):
        for part in range(parts):
            rows = sum_ref[pl.ds(part * half_rows * tall + time, half_rows, stride=tall), :]
            out_ref[time, part] = rows[:, :looks]


def column_swap(first, owners, count):
    moves = []
    for owner in range(owners):
        for column in range(count):
            partner = column + 1 if (column - first) % 2 == 0 else column - 1
            to = owner
            if not 0 <= partner < count:
                partner = column
                to = owner ^ 1 if owners % 2 == 0 else owner
            moves.append((owner * count + column, to * count + partner))
    return moves


def per_device(scenes, pair_dates, pair_count, inverse):
    owners, count = lax.axis_size("date"), lax.axis_size("col")
    dates_here, parts, all_rows, columns = scenes.shape
    half_rows = all_rows // owners // 2
    dates = owners * dates_here
    pairs = pair_rows(dates)
    looks = columns // 8
    tiles = -(-half_rows // (LANES // looks))

    blocks, wide = cut(scenes, pair_dates.T, pair_count, inverse, owners)
    for step in range(1, owners):
        moves = [(owner, (owner - step) % owners) for owner in range(owners)]
        blocks[step] = lax.ppermute(blocks[step], "date", moves)

    tall = wide.shape[0]
    rows = 2 * half_rows
    sides = columns // LANES
    order = [blocks[(place - 1) % owners] for place in range(owners)]
    order = [held(block) for block in order]
    by_arrival = [held(block) for block in blocks[:0:-1] + blocks[:1]]
    group_rows = pltpu.VMEM((parts, sides, rows * GROUP, LANES), F32)
    first_group, first_pairs = pl.pallas_call(
        functools.partial(early_kernel, dates_here),
        out_shape=[
            pltpu.VMEM((parts, 2, 8, tiles, GROUP, LANES), F32),
            pltpu.VMEM((parts, 2, GROUP * GROUP // 2, (tiles + 1) * LANES), BF16),
        ],
        in_specs=[IN_VMEM] * (GROUP // dates_here),
        out_specs=[IN_VMEM] * 2,
        scratch_shapes=[group_rows],
        compiler_params=pltpu.CompilerParams(vmem_limit_bytes=40 << 20),
    )(*order[: GROUP // dates_here])
    others = dates // GROUP - 1
    looked, edge = pl.pallas_call(
        functools.partial(series_kernel, dates_here, pair_dates.shape[0]),
        out_shape=[
            pltpu.VMEM((parts, tall, tiles * LANES), F32),
            pltpu.VMEM((tall, LANES), F32),
        ],
        in_specs=[IN_VMEM] * (owners + 3),
        out_specs=[IN_VMEM] * 2,
        scratch_shapes=[
            group_rows,
            pltpu.VMEM((others, parts, 2, 8, tiles, GROUP, LANES), F32),
            pltpu.VMEM((others, parts, 8, tiles, 4 * GROUP, LANES), F32),
            pltpu.VMEM((parts, 2 * pairs, (tiles + 1) * LANES), BF16),
        ],
        compiler_params=pltpu.CompilerParams(vmem_limit_bytes=40 << 20),
    )(*by_arrival, held(wide), held(first_group), held(first_pairs))

    first = lax.ppermute(edge, ("date", "col"), column_swap(0, owners, count))
    second = lax.ppermute(edge, ("date", "col"), column_swap(1, owners, count))
    return pl.pallas_call(
        finish_kernel,
        out_shape=jax.ShapeDtypeStruct(
            (inverse.shape[0], parts, half_rows, columns // 8), F32
        ),
        in_specs=[IN_VMEM] * 3,
        out_specs=IN_VMEM,
        scratch_shapes=[pltpu.VMEM((parts * half_rows * tall, LANES), F32)],
    )(held(looked), held(second), held(first))


def solution(mesh):
    placed = (P("date", None, "groups", "col"), P("date", None), P("date"), P())
    return jax.shard_map(
        per_device,
        mesh=mesh,
        in_specs=placed,
        out_specs=P(None, None, ("groups", "date"), "col"),
        check_vma=False,
    )
```

time: 17 us -> 14.4 us (0.85)
  the two profiles are of different devices: /device:TPU:16 before, /device:TPU:18 now
where the time goes in v4:
time: 14.4 us; the launch traced here: 14.2 us
  waiting for transfers between devices  6.15 us (43%)
  Pallas kernels  3.76 us (26%)
  starting transfers between devices  3.65 us (25%)
  between operations  0.68 us (5%)
    ppermute x3, waiting for transfers between devices, per_device(): blocks[step] = lax.ppermute(blocks[step], 'date', moves)  2.51 us
    ppermute x1, waiting for transfers between devices, per_device(): first = lax.ppermute(edge, ('date', 'col'), column_swap(0, owners, count))  2.07 us
    ppermute x3, starting transfers between devices, per_device(): blocks[step] = lax.ppermute(blocks[step], 'date', moves)  2.05 us
    ppermute x1, starting transfers between devices, per_device(): first = lax.ppermute(edge, ('date', 'col'), column_swap(0, owners, count))  1.6 us
    ppermute x1, waiting for transfers between devices, per_device(): second = lax.ppermute(edge, ('date', 'col'), column_swap(1, owners, count))  1.58 us
    pallas_call x1, Pallas kernels, per_device(): pl.pallas_call(functools.partial(series_kernel, dates_here, pair_dates.sh...  1.26 us
    pallas_call x1, Pallas kernels, cut(): pl.pallas_call(cut_kernel, out_shape=[pltpu.VMEM((height + NOTE_ROWS, col...  1 us
    pallas_call x1, Pallas kernels, per_device(): pl.pallas_call(finish_kernel, out_shape=jax.ShapeDtypeStruct((inverse.sha...  0.84 us
  transfers between devices with their start and end apart: 5, of which 4 were waited for; matrix products, arithmetic and copies ran while one was open for 0% of the time, Pallas kernels for 5%

profile of v4, /device:TPU:18, one launch (start us, length us, event | category | flops | bytes accessed | tf_op | source)
XLA Modules:
  0.0 14.2 jit_solution(5302957556036400244)
XLA Ops:
  0.7 1.0 %shard_map.46 = (bf16[144,256]{1,0:T(8,128)(2,1)S(1)}, bf16[144,256]{1,0:T(8,128)(2,1)S(1)}, bf16[144,256]{1,0:T(8,128)(2,1)S(1)}, bf16[144,256]{1,0:T(8,128)(2,1)S(1)}, f32[16,128]{1,0:T(8,128)S(1)}) custom-call(s32[1]{0:T(128)S(6)} %copy.5.count_ref, bf16[4,2,64,256]{3,2,1,0:T(8,128)(2,1)} %scenes_ref.1, s32[2,24]{1,0:T(2,128)} %bitcast.1, ...), custom_call_target="tpu_custom_call" | custom-call | tf_op jit(solution)/shard_map/pallas_call | solution.py:76
  1.7 0.1 collective-permute-start
  1.7 0.6 %collective-permute-start.1 = (bf16[144,256]{1,0:T(8,128)(2,1)S(1)}, bf16[144,256]{1,0:T(8,128)(2,1)S(1)}, u32[]{:S(2)}, u32[]{:S(2)}) collective-permute-start(bf16[144,256]{1,0:T(8,128)(2,1)S(1)} %get-tuple-element.15), channel_id=1, source_target_pairs={{0,8},{4,12},{8,0},{12,4},{1,9},{5,13},{9,1},{13,5},{2,10},{6,14},... | collective-permute-start | bytes 221192 | tf_op jit(solution)/shard_map/ppermute | solution.py:444
  2.3 1.4 %collective-permute-start.2 = (bf16[144,256]{1,0:T(8,128)(2,1)S(1)}, bf16[144,256]{1,0:T(8,128)(2,1)S(1)}, u32[]{:S(2)}, u32[]{:S(2)}) collective-permute-start(bf16[144,256]{1,0:T(8,128)(2,1)S(1)} %get-tuple-element.16), channel_id=1, source_target_pairs={{0,12},{4,0},{8,4},{12,8},{1,13},{5,1},{9,5},{13,9},{2,14},{6,2},{... | collective-permute-start | bytes 221192 | tf_op jit(solution)/shard_map/ppermute | solution.py:444
  3.7 2.0 %collective-permute-done.refs_0_ = bf16[144,256]{1,0:T(8,128)(2,1)S(1)} collective-permute-done((bf16[144,256]{1,0:T(8,128)(2,1)S(1)}, bf16[144,256]{1,0:T(8,128)(2,1)S(1)}, u32[]{:S(2)}, u32[]{:S(2)}) %collective-permute-start) | collective-permute-done | bytes 73760 | tf_op jit(solution)/shard_map/ppermute | solution.py:444
  5.7 0.7 %shard_map.47 = (f32[2,2,8,2,8,128]{5,4,3,2,1,0:T(8,128)S(1)}, bf16[2,2,32,384]{3,2,1,0:T(8,128)(2,1)S(1)}) custom-call(bf16[144,256]{1,0:T(8,128)(2,1)S(1)} %collective-permute-done.refs_0_, bf16[144,256]{1,0:T(8,128)(2,1)S(1)} %get-tuple-element.17.refs_1_.refs_3_), custom_call_target="tpu_custom_call" | custom-call | tf_op jit(solution)/shard_map/pallas_call | solution.py:453
  6.3 0.5 %collective-permute-done.1.refs_1_ = bf16[144,256]{1,0:T(8,128)(2,1)S(1)} collective-permute-done((bf16[144,256]{1,0:T(8,128)(2,1)S(1)}, bf16[144,256]{1,0:T(8,128)(2,1)S(1)}, u32[]{:S(2)}, u32[]{:S(2)}) %collective-permute-start.1) | collective-permute-done | bytes 73760 | tf_op jit(solution)/shard_map/ppermute | solution.py:444
  6.9 0.0 collective-permute-done.2.refs_2_
  6.9 1.3 %shard_map.48 = (f32[2,16,256]{2,1,0:T(8,128)S(1)}, f32[16,128]{1,0:T(8,128)S(1)}) custom-call(bf16[144,256]{1,0:T(8,128)(2,1)S(1)} %collective-permute-done.refs_0_, bf16[144,256]{1,0:T(8,128)(2,1)S(1)} %collective-permute-done.1.refs_1_, bf16[144,256]{1,0:T(8,128)(2,1)S(1)} %collective-permute-done.2.refs_2_, ...), custom_call_target="tpu_custom_call" | custom-call | tf_op jit(solution)/shard_map/pallas_call | solution.py:465
  8.1 1.6 %collective-permute-start.4 = (f32[16,128]{1,0:T(8,128)S(1)}, f32[16,128]{1,0:T(8,128)S(1)}, u32[]{:S(2)}, u32[]{:S(2)}) collective-permute-start(f32[16,128]{1,0:T(8,128)S(1)} %get-tuple-element.22), channel_id=1, source_target_pairs={{0,1},{1,0},{2,3},{3,2},{4,5},{5,4},{6,7},{7,6},{8,9},{9,8},{10,11... | collective-permute-start | bytes 24584 | tf_op jit(solution)/shard_map/ppermute | solution.py:482
  9.7 0.0 collective-permute-start.3
  9.7 2.1 %collective-permute-done.4.first_ref = f32[16,128]{1,0:T(8,128)S(1)} collective-permute-done((f32[16,128]{1,0:T(8,128)S(1)}, f32[16,128]{1,0:T(8,128)S(1)}, u32[]{:S(2)}, u32[]{:S(2)}) %collective-permute-start.4) | collective-permute-done | bytes 8224 | tf_op jit(solution)/shard_map/ppermute | solution.py:482
  11.8 1.6 %collective-permute-done.3.second_ref = f32[16,128]{1,0:T(8,128)S(1)} collective-permute-done((f32[16,128]{1,0:T(8,128)S(1)}, f32[16,128]{1,0:T(8,128)S(1)}, u32[]{:S(2)}, u32[]{:S(2)}) %collective-permute-start.3) | collective-permute-done | bytes 8224 | tf_op jit(solution)/shard_map/ppermute | solution.py:483
  13.4 0.8 %shard_map.49 = f32[15,2,8,32]{3,2,1,0:T(8,128)} custom-call(f32[2,16,256]{2,1,0:T(8,128)S(1)} %get-tuple-element.21.looked_ref, f32[16,128]{1,0:T(8,128)S(1)} %collective-permute-done.3.second_ref, f32[16,128]{1,0:T(8,128)S(1)} %collective-permute-done.4.first_ref), custom_call_target="tpu_custom_call" | custom-call | tf_op jit(solution)/shard_map/pallas_call | solution.py:484
Async XLA Ops:
  1.7 4.0 %collective-permute-start = (bf16[144,256]{1,0:T(8,128)(2,1)S(1)}, bf16[144,256]{1,0:T(8,128)(2,1)S(1)}, u32[]{:S(2)}, u32[]{:S(2)}) collective-permute-start(bf16[144,256]{1,0:T(8,128)(2,1)S(1)} %get-tuple-element.14), channel_id=1, source_target_pairs={{0,4},{4,8},{8,12},{12,0},{1,5},{5,9},{9,13},{13,1},{2,6},{6,10},{... | collective-permute-start | bytes 221192 | tf_op jit(solution)/shard_map/ppermute | solution.py:444
  1.7 5.2 %collective-permute-start.1 = (bf16[144,256]{1,0:T(8,128)(2,1)S(1)}, bf16[144,256]{1,0:T(8,128)(2,1)S(1)}, u32[]{:S(2)}, u32[]{:S(2)}) collective-permute-start(bf16[144,256]{1,0:T(8,128)(2,1)S(1)} %get-tuple-element.15), channel_id=1, source_target_pairs={{0,8},{4,12},{8,0},{12,4},{1,9},{5,13},{9,1},{13,5},{2,10},{6,14},... | collective-permute-start | bytes 221192 | tf_op jit(solution)/shard_map/ppermute | solution.py:444
  2.3 4.6 %collective-permute-start.2 = (bf16[144,256]{1,0:T(8,128)(2,1)S(1)}, bf16[144,256]{1,0:T(8,128)(2,1)S(1)}, u32[]{:S(2)}, u32[]{:S(2)}) collective-permute-start(bf16[144,256]{1,0:T(8,128)(2,1)S(1)} %get-tuple-element.16), channel_id=1, source_target_pairs={{0,12},{4,0},{8,4},{12,8},{1,13},{5,1},{9,5},{13,9},{2,14},{6,2},{... | collective-permute-start | bytes 221192 | tf_op jit(solution)/shard_map/ppermute | solution.py:444
  8.1 3.7 %collective-permute-start.4 = (f32[16,128]{1,0:T(8,128)S(1)}, f32[16,128]{1,0:T(8,128)S(1)}, u32[]{:S(2)}, u32[]{:S(2)}) collective-permute-start(f32[16,128]{1,0:T(8,128)S(1)} %get-tuple-element.22), channel_id=1, source_target_pairs={{0,1},{1,0},{2,3},{3,2},{4,5},{5,4},{6,7},{7,6},{8,9},{9,8},{10,11... | collective-permute-start | bytes 24584 | tf_op jit(solution)/shard_map/ppermute | solution.py:482
  9.7 3.7 %collective-permute-start.3 = (f32[16,128]{1,0:T(8,128)S(1)}, f32[16,128]{1,0:T(8,128)S(1)}, u32[]{:S(2)}, u32[]{:S(2)}) collective-permute-start(f32[16,128]{1,0:T(8,128)S(1)} %get-tuple-element.22), channel_id=1, source_target_pairs={{0,4},{1,2},{2,1},{3,7},{4,0},{5,6},{6,5},{7,3},{8,12},{9,10},{10,... | collective-permute-start | bytes 24584 | tf_op jit(solution)/shard_map/ppermute | solution.py:483

commit v5 on v4

--- a/solution.py
+++ b/solution.py
@@ -32,67 +32,66 @@
     return high, (value - high.astype(F32)).astype(BF16)
 
 
-def note_of(pair_dates, count):
-    slots = pair_dates.shape[1]
-    dates = jnp.concatenate([pair_dates.astype(F32), jnp.zeros((2, LANES - slots), F32)], axis=1)
+def comb_kernel(comb_ref, blank_ref):
+    comb_ref[...] = comb_of(comb_ref.shape[0])
+    blank_ref[...] = jnp.zeros_like(blank_ref)
+
+
+def note_kernel(count_ref, dates_ref, blank_ref, note_ref):
+    slots = dates_ref.shape[1]
+    dates = dates_ref[...].astype(F32)
+    dates = jnp.concatenate([dates, jnp.zeros((2, LANES - slots), F32)], axis=1)
     row, lane = iota((NOTE_ROWS, LANES), 0), iota((NOTE_ROWS, LANES), 1)
-    note = jnp.where((row == 2) & (lane < jnp.minimum(count, slots)), 1.0, 0.0)
+    note = jnp.where((row == 2) & (lane < jnp.minimum(count_ref[0], slots)), 1.0, 0.0)
     for side in range(2):
         note = jnp.where(row == side, dates[side : side + 1], note)
-    return note.astype(BF16)
-
-
-def cut_kernel(count_ref, scenes_ref, dates_ref, inverse_ref, *outs):
-    *block_refs, wide_ref = outs
+    note_ref[...] = blank_ref[...]
+    note_ref[:, :LANES] = note.astype(BF16)
+
+
+def cut_kernel(scenes_ref, note_ref, *block_refs):
     owners = len(block_refs)
     me = lax.axis_index("date")
     rows = scenes_ref.shape[2] // owners
-    note = note_of(dates_ref[...], count_ref[0])
     for step, block_ref in enumerate(block_refs):
         first = pl.multiple_of(lax.rem(me + owners - step, owners) * rows, rows)
         cells = scenes_ref[:, :, pl.ds(first, rows), :]
         height = block_ref.shape[0] - NOTE_ROWS
         block_ref[:height] = cells.reshape(height, block_ref.shape[1])
-        block_ref[height:, :LANES] = note
-    wide_ref[...] = jnp.zeros_like(wide_ref)
-    wide_ref[: inverse_ref.shape[0], : inverse_ref.shape[1]] = inverse_ref[...]
-
-
-def note_kernel(count_ref, dates_ref, inverse_ref, note_ref, wide_ref):
-    note_ref[...] = jnp.zeros_like(note_ref)
-    note_ref[:, :LANES] = note_of(dates_ref[...], count_ref[0])
-    wide_ref[...] = jnp.zeros_like(wide_ref)
-    wide_ref[: inverse_ref.shape[0], : inverse_ref.shape[1]] = inverse_ref[...]
-
-
-def cut(scenes, pair_dates, pair_count, inverse, owners):
+        block_ref[height:] = note_ref[...]
+
+
+def cut(scenes, pair_dates, pair_count, owners):
     dates_here, parts, all_rows, columns = scenes.shape
     rows = all_rows // owners
     height = dates_here * parts * rows
-    wide = pltpu.VMEM(
-        (round_up(inverse.shape[0], 16), round_up(inverse.shape[1], LANES)), F32
-    )
+    comb, blank = pl.pallas_call(
+        comb_kernel,
+        out_shape=[pltpu.VMEM((columns, columns), BF16), pltpu.VMEM((NOTE_ROWS, columns), BF16)],
+        out_specs=[IN_VMEM] * 2,
+        cost_estimate=pl.CostEstimate(flops=10**9, bytes_accessed=10**7, transcendentals=0),
+    )()
+    note = pl.pallas_call(
+        note_kernel,
+        out_shape=pltpu.VMEM((NOTE_ROWS, columns), BF16),
+        in_specs=[IN_SMEM] + [IN_VMEM] * 2,
+        out_specs=IN_VMEM,
+    )(pair_count, held(pair_dates), held(blank))
     if rows % 16 == 0:
-        *blocks, wide = pl.pallas_call(
+        blocks = pl.pallas_call(
             cut_kernel,
-            out_shape=[pltpu.VMEM((height + NOTE_ROWS, columns), BF16)] * owners + [wide],
-            in_specs=[IN_SMEM] + [IN_VMEM] * 3,
-            out_specs=[IN_VMEM] * (owners + 1),
-        )(pair_count, scenes, pair_dates, inverse)
-        return blocks, wide
-    note, wide = pl.pallas_call(
-        note_kernel,
-        out_shape=[pltpu.VMEM((NOTE_ROWS, columns), BF16), wide],
-        in_specs=[IN_SMEM] + [IN_VMEM] * 2,
-        out_specs=[IN_VMEM] * 2,
-    )(pair_count, pair_dates, inverse)
+            out_shape=[pltpu.VMEM((height + NOTE_ROWS, columns), BF16)] * owners,
+            in_specs=[IN_VMEM] * 2,
+            out_specs=[IN_VMEM] * owners,
+        )(held(scenes), held(note))
+        return list(blocks), comb
     me = lax.axis_index("date")
     apart = scenes.reshape(dates_here * parts, owners, rows, columns)
     blocks = []
     for step in range(owners):
         cells = lax.dynamic_index_in_dim(apart, lax.rem(me + owners - step, owners), 1, False)
         blocks.append(jnp.concatenate([cells.reshape(height, columns), note], axis=0))
-    return blocks, wide
+    return blocks, comb
 
 
 def pair_places(first, second, dates):
@@ -235,7 +234,6 @@
 def unit_products(tiles, looks, turns, mine_of, turned_of, store):
     lane = iota((GROUP, LANES), 1) % looks
     at_first, at_last = lane == 0, lane == looks - 1
-    rims = [None] * (2 * len(turns))
     for tile in range(tiles):
 
         def product(place):
@@ -273,29 +271,43 @@
             value = 8.0 * (early[index] + late[index]) - to_left[index] - to_right[index]
             value = value + jnp.where(at_first, 0.0, before) + jnp.where(at_last, 0.0, after)
             values.append(value)
-            edge = jnp.where(at_first, before, jnp.where(at_last, after, 0.0))
-            if tile:
-                edge = rims[index] + pltpu.roll(edge, 2 * tile, 1)
-            rims[index] = edge
         for part in range(2):
             store(part, tile, jnp.concatenate(values[part::2], axis=0))
-    for part in range(2):
-        store(part, tiles, jnp.concatenate(rims[part::2], axis=0))
 
 
 def turn_here(part, odd, place, tile, turn, mine):
     return pltpu.roll(mine[part][odd], GROUP - turn, 0)
 
 
+def seam_of(block_ref, dates_here, seat, seam_ref):
+    height = block_ref.shape[0] - NOTE_ROWS
+    columns = block_ref.shape[1]
+    rows = height // (2 * dates_here)
+    column, lane = iota((columns, LANES), 0), iota((columns, LANES), 1) % 8
+    wanted = jnp.where(lane < 4, lane, columns - 8 + lane)
+    pick = jnp.where(column == wanted, 1.0, 0.0).astype(BF16)
+    cells = jnp.dot(block_ref[:height], pick, preferred_element_type=F32)
+    row, lane = iota((height, LANES), 0), iota((height, LANES), 1)
+    cells = jnp.where(row % rows == lane // 8, cells, 0.0).astype(BF16)
+    line, row = iota((16, height), 0), iota((16, height), 1) // rows
+    gather = jnp.where((line < 2 * dates_here) & (row == line % dates_here * 2 + line // dates_here), 1.0, 0.0)
+    lines = jnp.dot(gather.astype(BF16), cells, preferred_element_type=F32)
+    for part in range(2):
+        seam_ref[part, seat : seat + dates_here, :] = lines[
+            part * dates_here : (part + 1) * dates_here
+        ]
+
+
 def early_kernel(dates_here, *refs):
-    *block_refs, ring_ref, pair_ref, rows_ref = refs
+    comb_ref, *block_refs, ring_ref, pair_ref, seam_ref, rows_ref = refs
     columns = block_refs[0].shape[1]
     looks = columns // 8
     tiles = ring_ref.shape[3]
     half_rows = rows_ref.shape[2] // GROUP // 2
-    comb = comb_of(columns)
+    comb = comb_ref[...]
     for index, block_ref in enumerate(block_refs):
         spread_block(block_ref, comb, dates_here, index * dates_here, rows_ref)
+        seam_of(block_ref, dates_here, index * dates_here, seam_ref)
 
     def keep(part, odd, place, tile, cells):
         ring_ref[part, odd, place, tile] = cells
@@ -318,25 +330,73 @@
     )
 
 
-def series_kernel(dates_here, slots, *refs):
-    *refs, looked_ref, edge_ref, rows_ref, ring_ref, far_ref, pair_ref = refs
-    *block_refs, wide_ref, first_ref, first_pair_ref = refs
+def edge_kernel(dates_here, slots, *refs):
+    *refs, weights_ref, message_ref, wide_ref, seams_ref, pair_ref = refs
+    *block_refs, inverse_ref, seam_ref = refs
     block_refs = block_refs[::-1]
     owners = len(block_refs)
     dates = owners * dates_here
     groups = dates // GROUP
     pairs = pair_rows(dates)
+    together = GROUP // dates_here
+    tall = wide_ref.shape[0]
+
+    for group in range(1, groups):
+        for index in range(together):
+            block_ref = block_refs[group * together + index - 1]
+            seam_of(block_ref, dates_here, index * dates_here, seams_ref.at[group - 1])
+    wide_ref[...] = jnp.zeros_like(wide_ref)
+    wide_ref[: inverse_ref.shape[0], : inverse_ref.shape[1]] = inverse_ref[...]
+    weights = pair_weights(block_refs, wide_ref[...], dates_here, slots)
+    for part in range(2):
+        weights_ref[part] = weights[part]
+
+    lane = iota((GROUP, LANES), 1) % 8
+    ramp = jnp.where(lane < 4, 3.5 - lane.astype(F32), lane.astype(F32) - 3.5)
+    for unit, (low, high, turns) in enumerate(pair_units(dates)):
+        mine = [(seams_ref[low - 1, part] if low else seam_ref[part]) * ramp for part in range(2)]
+        theirs = [seams_ref[high - 1, part] if high else seam_ref[part] for part in range(2)]
+        values = []
+        for turn in turns:
+            other = [pltpu.roll(cells, GROUP - turn, 0) if turn else cells for cells in theirs]
+            values.append(mine[0] * other[0] + mine[1] * other[1])
+            values.append(mine[1] * other[0] - mine[0] * other[1])
+        for part in range(2):
+            value = jnp.concatenate(values[part::2], axis=0)
+            count = value.shape[0]
+            bits = halves(value)
+            for half in range(2):
+                at = half * pairs + unit * count
+                pair_ref[part, at : at + count, :] = bits[half]
+    sums = []
+    for part in range(2):
+        summed = jnp.dot(weights[part], pair_ref[part], preferred_element_type=F32)
+        summed = summed[:tall] + summed[tall:]
+        for shift in (1, 2, 8):
+            summed = summed + pltpu.roll(summed, LANES - shift, 1)
+        sums.append(summed)
+    lane = iota((tall, LANES), 1)
+    message_ref[...] = jnp.where(lane % 4 == 1, pltpu.roll(sums[1], 1, 1), sums[0])
+
+
+def series_kernel(dates_here, *refs):
+    *refs, looked_ref, rows_ref, ring_ref, far_ref, pair_ref = refs
+    *block_refs, comb_ref, weights_ref, first_ref, first_pair_ref = refs
+    block_refs = block_refs[::-1]
+    groups = 1 + ring_ref.shape[0]
+    dates = groups * GROUP
+    pairs = pair_rows(dates)
     columns = block_refs[0].shape[1]
     looks = columns // 8
     tiles = ring_ref.shape[4]
     half_rows = rows_ref.shape[2] // GROUP // 2
-    tall = wide_ref.shape[0]
+    tall = looked_ref.shape[1]
     together = GROUP // dates_here
 
-    comb = comb_of(columns)
+    comb = comb_ref[...]
     for group in range(1, groups):
         for index in range(together):
-            block_ref = block_refs[group * together + index - 1]
+            block_ref = block_refs[(group - 1) * together + index]
             spread_block(block_ref, comb, dates_here, index * dates_here, rows_ref)
 
         def keep(part, odd, place, tile, cells):
@@ -347,13 +407,10 @@
 
         pack_group(rows_ref, looks, half_rows, keep)
 
-    weights = pair_weights(block_refs, wide_ref[...], dates_here, slots)
-
-    across = first_pair_ref.shape[3]
     for part in range(2):
         for half in range(2):
             at = half * pairs
-            pair_ref[part, at : at + first_pair_ref.shape[2], :across] = first_pair_ref[part, half]
+            pair_ref[part, at : at + first_pair_ref.shape[2], :] = first_pair_ref[part, half]
     for unit, (low, high, turns) in enumerate(pair_units(dates)):
         if high == 0:
             continue
@@ -377,39 +434,34 @@
 
         turned_of = turn_here if low == high else turn_far
         unit_products(tiles, looks, turns, mine_of, turned_of, store)
-    message = jnp.zeros((tall, LANES), F32)
-    for part in range(2):
-        summed = jnp.dot(weights[part], pair_ref[part], preferred_element_type=F32)
-        summed = summed[:tall] + summed[tall:]
-        looked_ref[part] = summed[:, : tiles * LANES]
-        edge = summed[:, tiles * LANES :]
-        message = message + (pltpu.roll(edge, 2 * tiles, 1) if part else edge)
-    edge_ref[...] = message
+    for part in range(2):
+        summed = jnp.dot(weights_ref[part], pair_ref[part], preferred_element_type=F32)
+        looked_ref[part] = summed[:tall] + summed[tall:]
 
 
 def finish_kernel(looked_ref, second_ref, first_ref, out_ref, sum_ref):
     times, parts, half_rows, looks = out_ref.shape
     tall = first_ref.shape[0]
     pack = LANES // looks
-    tiles = looked_ref.shape[2] // LANES
     here, last = lax.axis_index("col"), lax.axis_size("col") - 1
     even = lax.rem(here, 2) == 0
     first, second = first_ref[...], second_ref[...]
     nothing = jnp.zeros_like(first)
     from_right = jnp.where(here == last, nothing, jnp.where(even, first, second))
     from_left = jnp.where(here == 0, nothing, jnp.where(even, second, first))
-    lane = iota((tall, LANES), 1) % looks
+    lane = iota((tall, LANES), 1)
     for part in range(parts):
-        for tile in range(tiles):
-            shift = 2 * (tile + tiles * part)
+        for half_row in range(half_rows):
+            tile, near = half_row // pack, half_row % pack
             value = looked_ref[part, :, tile * LANES : (tile + 1) * LANES]
-            right = pltpu.roll(from_right, (looks - shift) % LANES, 1)
-            left = pltpu.roll(from_left, (-looks - shift) % LANES, 1)
+            value = pltpu.roll(value, -near * looks % LANES, 1)
+            at = 16 * half_row + part
+            right = pltpu.roll(from_right, (looks - 1 - at) % LANES, 1)
+            left = pltpu.roll(from_left, (-4 - at) % LANES, 1)
             value = value + jnp.where(lane == looks - 1, right, 0.0)
             value = value + jnp.where(lane == 0, left, 0.0)
-            for near in range(min(pack, half_rows - tile * pack)):
-                at = (part * half_rows + tile * pack + near) * tall
-                sum_ref[at : at + tall, :] = pltpu.roll(value, -near * looks % LANES, 1)
+            at = (part * half_rows + half_row) * tall
+            sum_ref[at : at + tall, :] = value
     for time in range(times):
         for part in range(parts):
             rows = sum_ref[pl.ds(part * half_rows * tall + time, half_rows, stride=tall), :]
@@ -438,46 +490,63 @@
     looks = columns // 8
     tiles = -(-half_rows // (LANES // looks))
 
-    blocks, wide = cut(scenes, pair_dates.T, pair_count, inverse, owners)
+    blocks, comb = cut(scenes, pair_dates.T, pair_count, owners)
     for step in range(1, owners):
         moves = [(owner, (owner - step) % owners) for owner in range(owners)]
         blocks[step] = lax.ppermute(blocks[step], "date", moves)
 
-    tall = wide.shape[0]
+    tall = round_up(inverse.shape[0], 16)
     rows = 2 * half_rows
     sides = columns // LANES
     order = [blocks[(place - 1) % owners] for place in range(owners)]
     order = [held(block) for block in order]
     by_arrival = [held(block) for block in blocks[:0:-1] + blocks[:1]]
     group_rows = pltpu.VMEM((parts, sides, rows * GROUP, LANES), F32)
-    first_group, first_pairs = pl.pallas_call(
+    first_group, first_pairs, first_seam = pl.pallas_call(
         functools.partial(early_kernel, dates_here),
         out_shape=[
             pltpu.VMEM((parts, 2, 8, tiles, GROUP, LANES), F32),
-            pltpu.VMEM((parts, 2, GROUP * GROUP // 2, (tiles + 1) * LANES), BF16),
+            pltpu.VMEM((parts, 2, GROUP * GROUP // 2, tiles * LANES), BF16),
+            pltpu.VMEM((parts, GROUP, LANES), F32),
         ],
-        in_specs=[IN_VMEM] * (GROUP // dates_here),
-        out_specs=[IN_VMEM] * 2,
+        in_specs=[IN_VMEM] * (GROUP // dates_here + 1),
+        out_specs=[IN_VMEM] * 3,
         scratch_shapes=[group_rows],
         compiler_params=pltpu.CompilerParams(vmem_limit_bytes=40 << 20),
-    )(*order[: GROUP // dates_here])
+    )(held(comb), *order[: GROUP // dates_here])
     others = dates // GROUP - 1
-    looked, edge = pl.pallas_call(
-        functools.partial(series_kernel, dates_here, pair_dates.shape[0]),
+    weights, edge = pl.pallas_call(
+        functools.partial(edge_kernel, dates_here, pair_dates.shape[0]),
         out_shape=[
-            pltpu.VMEM((parts, tall, tiles * LANES), F32),
+            pltpu.VMEM((parts, 2 * tall, 2 * pairs), BF16),
             pltpu.VMEM((tall, LANES), F32),
         ],
-        in_specs=[IN_VMEM] * (owners + 3),
+        in_specs=[IN_VMEM] * (owners + 2),
         out_specs=[IN_VMEM] * 2,
+        scratch_shapes=[
+            pltpu.VMEM((tall, round_up(inverse.shape[1], LANES)), F32),
+            pltpu.VMEM((others, parts, GROUP, LANES), F32),
+            pltpu.VMEM((parts, 2 * pairs, LANES), BF16),
+        ],
+        compiler_params=pltpu.CompilerParams(vmem_limit_bytes=40 << 20),
+    )(*by_arrival, held(inverse), held(first_seam))
+    late = [held(block) for block in order[GROUP // dates_here :]][::-1]
+    looked = pl.pallas_call(
+        functools.partial(series_kernel, dates_here),
+        out_shape=pltpu.VMEM((parts, tall, tiles * LANES), F32),
+        in_specs=[IN_VMEM] * (len(late) + 4),
+        out_specs=IN_VMEM,
         scratch_shapes=[
             group_rows,
             pltpu.VMEM((others, parts, 2, 8, tiles, GROUP, LANES), F32),
             pltpu.VMEM((others, parts, 8, tiles, 4 * GROUP, LANES), F32),
-            pltpu.VMEM((parts, 2 * pairs, (tiles + 1) * LANES), BF16),
+            pltpu.VMEM((parts, 2 * pairs, tiles * LANES), BF16),
         ],
         compiler_params=pltpu.CompilerParams(vmem_limit_bytes=40 << 20),
-    )(*by_arrival, held(wide), held(first_group), held(first_pairs))
+        cost_estimate=pl.CostEstimate(
+            flops=2 * parts * pairs * columns * rows * 8, bytes_accessed=1 << 20, transcendentals=0
+        ),
+    )(*late, held(comb), held(weights), held(first_group), held(first_pairs))
 
     first = lax.ppermute(edge, ("date", "col"), column_swap(0, owners, count))
     second = lax.ppermute(edge, ("date", "col"), column_swap(1, owners, count))

time: 14.4 us -> 13.9 us (0.965)
  waiting for transfers between devices: 6.15 us -> 5.06 us
  local copies, waits for them, and re-layouts: 0 us -> 0.68 us
  Pallas kernels: 3.76 us -> 3.58 us
    ppermute x1, waiting for transfers between devices: 2.07 us -> 0.97 us  [per_device(): first = lax.ppermute(edge, ('date', 'col'), column_swap(0, owners, count))]
    pallas_call x1, Pallas kernels: 1 us -> 0.03 us  [cut(): pl.pallas_call(cut_kernel, out_shape=[pltpu.VMEM((height + NOTE_ROWS, col...]
    pallas_call x1 -> x4, Pallas kernels: 1.26 us -> 2.06 us  [the longest x1 1.1 us: per_device(): pl.pallas_call(functools.partial(series_kernel, dates_here), out_shape=pl...]
    unnamed x0 -> x6, local copies, waits for them, and re-layouts: none -> 0.68 us
  transfers between devices with their start and end apart: 5 -> 5, of which waited for: 4 -> 4; matrix products, arithmetic and copies ran while one was open for 0% -> 0% of each run, Pallas kernels for 5% -> 13%
where the time goes in v5:
time: 13.9 us; the launch traced here: 13.7 us
  waiting for transfers between devices  5.06 us (36%)
  starting transfers between devices  3.64 us (26%)
  Pallas kernels  3.58 us (26%)
  between operations  0.72 us (5%)
  local copies, waits for them, and re-layouts  0.68 us (5%)
    ppermute x3, waiting for transfers between devices, per_device(): blocks[step] = lax.ppermute(blocks[step], 'date', moves)  2.52 us
    ppermute x3, starting transfers between devices, per_device(): blocks[step] = lax.ppermute(blocks[step], 'date', moves)  2.05 us
    ppermute x1, starting transfers between devices, per_device(): first = lax.ppermute(edge, ('date', 'col'), column_swap(0, owners, count))  1.59 us
    ppermute x1, waiting for transfers between devices, per_device(): second = lax.ppermute(edge, ('date', 'col'), column_swap(1, owners, count))  1.58 us
    pallas_call x1, Pallas kernels, per_device(): pl.pallas_call(functools.partial(series_kernel, dates_here), out_shape=pl...  1.1 us
    ppermute x1, waiting for transfers between devices, per_device(): first = lax.ppermute(edge, ('date', 'col'), column_swap(0, owners, count))  0.97 us
    pallas_call x1, Pallas kernels, per_device(): pl.pallas_call(functools.partial(edge_kernel, dates_here, pair_dates.shap...  0.89 us
    pallas_call x1, Pallas kernels, per_device(): pl.pallas_call(finish_kernel, out_shape=jax.ShapeDtypeStruct((inverse.sha...  0.84 us
  transfers between devices with their start and end apart: 5, of which 4 were waited for; matrix products, arithmetic and copies ran while one was open for 0% of the time, Pallas kernels for 13%

profile of v5, /device:TPU:18, one launch (start us, length us, event | category | flops | bytes accessed | tf_op | source)
XLA Modules:
  0.0 13.7 jit_solution(8147485485869925362)
XLA Ops:
  0.0 0.0 copy-start
  0.0 0.1 shard_map.46
  0.7 0.0 copy-start.2
  0.8 0.7 %copy-done.2 = s32[24,2]{0,1:T(2,128)S(1)} copy-done((s32[24,2]{0,1:T(2,128)S(1)}, s32[24,2]{0,1:T(2,128)}, u32[]{:S(2)}) %copy-start.2) | copy-done | bytes 216
  1.4 0.0 copy-done
  1.5 0.1 collective-permute-start.2
  1.5 0.6 %collective-permute-start = (bf16[144,256]{1,0:T(8,128)(2,1)S(1)}, bf16[144,256]{1,0:T(8,128)(2,1)S(1)}, u32[]{:S(2)}, u32[]{:S(2)}) collective-permute-start(bf16[144,256]{1,0:T(8,128)(2,1)S(1)} %get-tuple-element.17), channel_id=1, source_target_pairs={{0,8},{4,12},{8,0},{12,4},{1,9},{5,13},{9,1},{13,5},{2,10},{6,14},... | collective-permute-start | bytes 221192 | tf_op jit(solution)/shard_map/ppermute | solution.py:496
  2.1 1.4 %collective-permute-start.1 = (bf16[144,256]{1,0:T(8,128)(2,1)S(1)}, bf16[144,256]{1,0:T(8,128)(2,1)S(1)}, u32[]{:S(2)}, u32[]{:S(2)}) collective-permute-start(bf16[144,256]{1,0:T(8,128)(2,1)S(1)} %get-tuple-element.18), channel_id=1, source_target_pairs={{0,12},{4,0},{8,4},{12,8},{1,13},{5,1},{9,5},{13,9},{2,14},{6,2},{... | collective-permute-start | bytes 221192 | tf_op jit(solution)/shard_map/ppermute | solution.py:496
  3.5 2.0 %collective-permute-done.2.refs_1_.refs_0_ = bf16[144,256]{1,0:T(8,128)(2,1)S(1)} collective-permute-done((bf16[144,256]{1,0:T(8,128)(2,1)S(1)}, bf16[144,256]{1,0:T(8,128)(2,1)S(1)}, u32[]{:S(2)}, u32[]{:S(2)}) %collective-permute-start.2) | collective-permute-done | bytes 73760 | tf_op jit(solution)/shard_map/ppermute | solution.py:496
  5.5 0.0 copy-start.1
  5.5 0.7 %shard_map.49 = (f32[2,2,8,2,8,128]{5,4,3,2,1,0:T(8,128)S(1)}, bf16[2,2,32,256]{3,2,1,0:T(8,128)(2,1)S(1)}, f32[2,8,128]{2,1,0:T(8,128)S(1)}) custom-call(bf16[256,256]{1,0:T(8,128)(2,1)S(1)} %get-tuple-element.19.refs_0_.refs_2_, bf16[144,256]{1,0:T(8,128)(2,1)S(1)} %collective-permute-done.2.refs_1_.refs_0_, ...), custom_call_target="tpu_custom_call" | custom-call | tf_op jit(solution)/shard_map/pallas_call | solution.py:505
  6.1 0.6 %collective-permute-done.refs_1_.refs_0_ = bf16[144,256]{1,0:T(8,128)(2,1)S(1)} collective-permute-done((bf16[144,256]{1,0:T(8,128)(2,1)S(1)}, bf16[144,256]{1,0:T(8,128)(2,1)S(1)}, u32[]{:S(2)}, u32[]{:S(2)}) %collective-permute-start) | collective-permute-done | bytes 73760 | tf_op jit(solution)/shard_map/ppermute | solution.py:496
  6.7 0.0 collective-permute-done.1.refs_2_.refs_1_
  6.7 0.0 copy-done.1
  6.7 0.9 %shard_map.50 = (bf16[2,32,256]{2,1,0:T(8,128)(2,1)S(1)}, f32[16,128]{1,0:T(8,128)S(1)}) custom-call(bf16[144,256]{1,0:T(8,128)(2,1)S(1)} %collective-permute-done.2.refs_1_.refs_0_, bf16[144,256]{1,0:T(8,128)(2,1)S(1)} %collective-permute-done.refs_1_.refs_0_, bf16[144,256]{1,0:T(8,128)(2,1)S(1)} %collective-permute-done.1.refs_2_.refs_1_, ...), custom_call_target="tpu_custom_call" | custom-call | tf_op jit(solution)/shard_map/pallas_call | solution.py:518
  7.6 1.6 %collective-permute-start.4 = (f32[16,128]{1,0:T(8,128)S(1)}, f32[16,128]{1,0:T(8,128)S(1)}, u32[]{:S(2)}, u32[]{:S(2)}) collective-permute-start(f32[16,128]{1,0:T(8,128)S(1)} %get-tuple-element.26), channel_id=1, source_target_pairs={{0,1},{1,0},{2,3},{3,2},{4,5},{5,4},{6,7},{7,6},{8,9},{9,8},{10,11... | collective-permute-start | bytes 24584 | tf_op jit(solution)/shard_map/ppermute | solution.py:551
  9.2 0.0 collective-permute-start.3
  9.2 1.1 %shard_map.51.looked_ref = f32[2,16,256]{2,1,0:T(8,128)S(1)} custom-call(bf16[144,256]{1,0:T(8,128)(2,1)S(1)} %collective-permute-done.refs_1_.refs_0_, bf16[144,256]{1,0:T(8,128)(2,1)S(1)} %collective-permute-done.1.refs_2_.refs_1_, bf16[256,256]{1,0:T(8,128)(2,1)S(1)} %get-tuple-element.19.refs_0_.refs_2_, ...), custom_call_target="tpu_custom_call" | custom-call | flops 16777216 | bytes 1048576 | tf_op jit(solution)/shard_map/pallas_call | solution.py:534
  10.3 1.0 %collective-permute-done.4.first_ref = f32[16,128]{1,0:T(8,128)S(1)} collective-permute-done((f32[16,128]{1,0:T(8,128)S(1)}, f32[16,128]{1,0:T(8,128)S(1)}, u32[]{:S(2)}, u32[]{:S(2)}) %collective-permute-start.4) | collective-permute-done | bytes 8224 | tf_op jit(solution)/shard_map/ppermute | solution.py:551
  11.3 1.6 %collective-permute-done.3.second_ref = f32[16,128]{1,0:T(8,128)S(1)} collective-permute-done((f32[16,128]{1,0:T(8,128)S(1)}, f32[16,128]{1,0:T(8,128)S(1)}, u32[]{:S(2)}, u32[]{:S(2)}) %collective-permute-start.3) | collective-permute-done | bytes 8224 | tf_op jit(solution)/shard_map/ppermute | solution.py:552
  12.8 0.8 %shard_map.52 = f32[15,2,8,32]{3,2,1,0:T(8,128)} custom-call(f32[2,16,256]{2,1,0:T(8,128)S(1)} %shard_map.51.looked_ref, f32[16,128]{1,0:T(8,128)S(1)} %collective-permute-done.3.second_ref, f32[16,128]{1,0:T(8,128)S(1)} %collective-permute-done.4.first_ref), custom_call_target="tpu_custom_call" | custom-call | tf_op jit(solution)/shard_map/pallas_call | solution.py:553
  (2 shorter events, 0.0 us)
Async XLA Ops:
  0.0 1.4 %copy-start = (bf16[4,2,64,256]{3,2,1,0:T(8,128)(2,1)S(1)}, bf16[4,2,64,256]{3,2,1,0:T(8,128)(2,1)}, u32[]{:S(2)}) copy-start(bf16[4,2,64,256]{3,2,1,0:T(8,128)(2,1)} %scenes_ref.1) | copy-start | bytes 786436
  0.7 0.7 %copy-start.2 = (s32[24,2]{0,1:T(2,128)S(1)}, s32[24,2]{0,1:T(2,128)}, u32[]{:S(2)}) copy-start(s32[24,2]{0,1:T(2,128)} %param.5) | copy-start | bytes 580
  1.5 4.0 %collective-permute-start.2 = (bf16[144,256]{1,0:T(8,128)(2,1)S(1)}, bf16[144,256]{1,0:T(8,128)(2,1)S(1)}, u32[]{:S(2)}, u32[]{:S(2)}) collective-permute-start(bf16[144,256]{1,0:T(8,128)(2,1)S(1)} %get-tuple-element.20), channel_id=1, source_target_pairs={{0,4},{4,8},{8,12},{12,0},{1,5},{5,9},{9,13},{13,1},{2,6},{6,10},{... | collective-permute-start | bytes 221192 | tf_op jit(solution)/shard_map/ppermute | solution.py:496
  1.5 5.2 %collective-permute-start = (bf16[144,256]{1,0:T(8,128)(2,1)S(1)}, bf16[144,256]{1,0:T(8,128)(2,1)S(1)}, u32[]{:S(2)}, u32[]{:S(2)}) collective-permute-start(bf16[144,256]{1,0:T(8,128)(2,1)S(1)} %get-tuple-element.17), channel_id=1, source_target_pairs={{0,8},{4,12},{8,0},{12,4},{1,9},{5,13},{9,1},{13,5},{2,10},{6,14},... | collective-permute-start | bytes 221192 | tf_op jit(solution)/shard_map/ppermute | solution.py:496
  2.1 4.6 %collective-permute-start.1 = (bf16[144,256]{1,0:T(8,128)(2,1)S(1)}, bf16[144,256]{1,0:T(8,128)(2,1)S(1)}, u32[]{:S(2)}, u32[]{:S(2)}) collective-permute-start(bf16[144,256]{1,0:T(8,128)(2,1)S(1)} %get-tuple-element.18), channel_id=1, source_target_pairs={{0,12},{4,0},{8,4},{12,8},{1,13},{5,1},{9,5},{13,9},{2,14},{6,2},{... | collective-permute-start | bytes 221192 | tf_op jit(solution)/shard_map/ppermute | solution.py:496
  5.5 1.2 %copy-start.1 = (f32[15,96]{1,0:T(8,128)S(1)}, f32[15,96]{1,0:T(8,128)}, u32[]{:S(2)}) copy-start(f32[15,96]{1,0:T(8,128)} %refs_4_.1) | copy-start | bytes 17284
  7.6 3.7 %collective-permute-start.4 = (f32[16,128]{1,0:T(8,128)S(1)}, f32[16,128]{1,0:T(8,128)S(1)}, u32[]{:S(2)}, u32[]{:S(2)}) collective-permute-start(f32[16,128]{1,0:T(8,128)S(1)} %get-tuple-element.26), channel_id=1, source_target_pairs={{0,1},{1,0},{2,3},{3,2},{4,5},{5,4},{6,7},{7,6},{8,9},{9,8},{10,11... | collective-permute-start | bytes 24584 | tf_op jit(solution)/shard_map/ppermute | solution.py:551
  9.2 3.7 %collective-permute-start.3 = (f32[16,128]{1,0:T(8,128)S(1)}, f32[16,128]{1,0:T(8,128)S(1)}, u32[]{:S(2)}, u32[]{:S(2)}) collective-permute-start(f32[16,128]{1,0:T(8,128)S(1)} %get-tuple-element.26), channel_id=1, source_target_pairs={{0,4},{1,2},{2,1},{3,7},{4,0},{5,6},{6,5},{7,3},{8,12},{9,10},{10,... | collective-permute-start | bytes 24584 | tf_op jit(solution)/shard_map/ppermute | solution.py:552

commit v6 on v5

--- a/solution.py
+++ b/solution.py
@@ -9,8 +9,10 @@
 
 F32, BF16 = jnp.float32, jnp.bfloat16
 LANES = 128
-NOTE_ROWS = 16
+NOTE = 8
+NOTE_ROWS = 2 * NOTE
 GROUP = 8
+ANYWHERE = pl.BlockSpec(memory_space=pl.ANY)
 IN_VMEM = pl.BlockSpec(memory_space=pltpu.VMEM)
 IN_SMEM = pl.BlockSpec(memory_space=pltpu.SMEM)
 
@@ -32,66 +34,129 @@
     return high, (value - high.astype(F32)).astype(BF16)
 
 
-def comb_kernel(comb_ref, blank_ref):
-    comb_ref[...] = comb_of(comb_ref.shape[0])
+def blank_kernel(blank_ref):
     blank_ref[...] = jnp.zeros_like(blank_ref)
 
 
-def note_kernel(count_ref, dates_ref, blank_ref, note_ref):
-    slots = dates_ref.shape[1]
-    dates = dates_ref[...].astype(F32)
-    dates = jnp.concatenate([dates, jnp.zeros((2, LANES - slots), F32)], axis=1)
-    row, lane = iota((NOTE_ROWS, LANES), 0), iota((NOTE_ROWS, LANES), 1)
-    note = jnp.where((row == 2) & (lane < jnp.minimum(count_ref[0], slots)), 1.0, 0.0)
-    for side in range(2):
-        note = jnp.where(row == side, dates[side : side + 1], note)
-    note_ref[...] = blank_ref[...]
-    note_ref[:, :LANES] = note.astype(BF16)
-
-
-def cut_kernel(scenes_ref, note_ref, *block_refs):
+def comb_of(columns):
+    looks = columns // 8
+    column, lane = iota((columns, columns), 0), iota((columns, columns), 1)
+    here = (column // 8 == lane % looks) & (column % 8 == lane // looks)
+    return jnp.where(here, 1.0, 0.0).astype(BF16)
+
+
+def fold_of(shape, looks, half_rows):
+    cell, target = iota(shape, 0), iota(shape, 1)
+    right = cell < LANES
+    cell = cell % LANES
+    half_row = cell // 16
+    here = right & (cell % 8 < 4) & (target == half_row * looks + looks - 1)
+    here = here | ~right & (cell % 8 >= 4) & (target == half_row * looks)
+    return jnp.where(here & (half_row < half_rows), 1.0, 0.0).astype(BF16)
+
+
+def live_kernel(slots, count_ref, blank_ref, live_ref):
+    row, lane = iota(live_ref.shape, 0), iota(live_ref.shape, 1)
+    live = (row == 2) & (lane < jnp.minimum(count_ref[0], slots))
+    live_ref[...] = jnp.where(live, 1.0, blank_ref[...])
+
+
+def seam_kernel(scenes_ref, dates_ref, live_ref, seams_ref, note_ref, fetched_ref, semaphore):
+    fetch = pltpu.make_async_copy(dates_ref, fetched_ref, semaphore)
+    fetch.start()
+    dates_here, parts, all_rows, columns = scenes_ref.shape
+    owners = seams_ref.shape[0]
+    rows = all_rows // owners
+    height = dates_here * parts * all_rows
+    column, lane = iota((columns, LANES), 0), iota((columns, LANES), 1) % 8
+    wanted = jnp.where(lane < 4, lane, columns - 8 + lane)
+    pick = jnp.where(column == wanted, 1.0, 0.0).astype(BF16)
+    cells = scenes_ref[...].reshape(height, columns)
+    cells = jnp.dot(cells, pick, preferred_element_type=F32)
+    row, lane = iota((height, LANES), 0), iota((height, LANES), 1)
+    cells = jnp.where(row % rows == lane // 8, cells, 0.0).astype(BF16)
+    line, row = iota((owners * NOTE, height), 0), iota((owners * NOTE, height), 1) // rows
+    place = line % NOTE
+    wanted = (place % dates_here * parts + place // dates_here) * owners + line // NOTE
+    gather = jnp.where((place < parts * dates_here) & (row == wanted), 1.0, 0.0).astype(BF16)
+    lines = jnp.dot(gather, cells, preferred_element_type=F32)
+    for owner in range(owners):
+        seams_ref[owner] = lines[owner * NOTE : (owner + 1) * NOTE]
+    note_ref[...] = live_ref[...]
+    fetch.wait()
+    note_ref[:2, : dates_ref.shape[1]] = fetched_ref[...].astype(F32)
+
+
+def twin_of(owner, owners):
+    return owner + 1 - 2 * (owner % 2) if owners % 2 == 0 else owner
+
+
+def cut_kernel(scenes_ref, note_ref, seams_ref, *block_refs):
     owners = len(block_refs)
     me = lax.axis_index("date")
     rows = scenes_ref.shape[2] // owners
+    sides = scenes_ref.shape[3] // LANES
     for step, block_ref in enumerate(block_refs):
-        first = pl.multiple_of(lax.rem(me + owners - step, owners) * rows, rows)
-        cells = scenes_ref[:, :, pl.ds(first, rows), :]
-        height = block_ref.shape[0] - NOTE_ROWS
-        block_ref[:height] = cells.reshape(height, block_ref.shape[1])
-        block_ref[height:] = note_ref[...]
+        owner = lax.rem(me + owners - step, owners)
+        first = pl.multiple_of(owner * rows, rows)
+        height = (block_ref.shape[0] - NOTE_ROWS) // sides
+        for side in range(sides):
+            cells = scenes_ref[:, :, pl.ds(first, rows), side * LANES : (side + 1) * LANES]
+            block_ref[side * height : (side + 1) * height] = cells.reshape(height, LANES)
+        seam = seams_ref[twin_of(owner, owners)]
+        block_ref[sides * height :] = jnp.concatenate([note_ref[...], seam], axis=0).astype(BF16)
+
+
+def cells_of(block_ref, sides):
+    height = (block_ref.shape[0] - NOTE_ROWS) // sides
+    return jnp.concatenate(
+        [block_ref[side * height : (side + 1) * height] for side in range(sides)], axis=1
+    )
 
 
 def cut(scenes, pair_dates, pair_count, owners):
     dates_here, parts, all_rows, columns = scenes.shape
     rows = all_rows // owners
+    sides = columns // LANES
     height = dates_here * parts * rows
-    comb, blank = pl.pallas_call(
-        comb_kernel,
-        out_shape=[pltpu.VMEM((columns, columns), BF16), pltpu.VMEM((NOTE_ROWS, columns), BF16)],
-        out_specs=[IN_VMEM] * 2,
+    blank = pl.pallas_call(
+        blank_kernel,
+        out_shape=pltpu.VMEM((NOTE, LANES), F32),
+        out_specs=IN_VMEM,
         cost_estimate=pl.CostEstimate(flops=10**9, bytes_accessed=10**7, transcendentals=0),
     )()
-    note = pl.pallas_call(
-        note_kernel,
-        out_shape=pltpu.VMEM((NOTE_ROWS, columns), BF16),
-        in_specs=[IN_SMEM] + [IN_VMEM] * 2,
+    live = pl.pallas_call(
+        functools.partial(live_kernel, pair_dates.shape[1]),
+        out_shape=pltpu.VMEM((NOTE, LANES), F32),
+        in_specs=[IN_SMEM, IN_VMEM],
         out_specs=IN_VMEM,
-    )(pair_count, held(pair_dates), held(blank))
+    )(pair_count, held(blank))
+    seams, note = pl.pallas_call(
+        seam_kernel,
+        out_shape=[pltpu.VMEM((owners, NOTE, LANES), F32), pltpu.VMEM((NOTE, LANES), F32)],
+        in_specs=[IN_VMEM, ANYWHERE, IN_VMEM],
+        out_specs=[IN_VMEM] * 2,
+        scratch_shapes=[pltpu.VMEM(pair_dates.shape, jnp.int32), pltpu.SemaphoreType.DMA],
+    )(held(scenes), pair_dates, held(live))
     if rows % 16 == 0:
         blocks = pl.pallas_call(
             cut_kernel,
-            out_shape=[pltpu.VMEM((height + NOTE_ROWS, columns), BF16)] * owners,
-            in_specs=[IN_VMEM] * 2,
+            out_shape=[pltpu.VMEM((sides * height + NOTE_ROWS, LANES), BF16)] * owners,
+            in_specs=[IN_VMEM] * 3,
             out_specs=[IN_VMEM] * owners,
-        )(held(scenes), held(note))
-        return list(blocks), comb
+        )(held(scenes), held(note), held(seams))
+        return list(blocks)
     me = lax.axis_index("date")
     apart = scenes.reshape(dates_here * parts, owners, rows, columns)
     blocks = []
     for step in range(owners):
-        cells = lax.dynamic_index_in_dim(apart, lax.rem(me + owners - step, owners), 1, False)
-        blocks.append(jnp.concatenate([cells.reshape(height, columns), note], axis=0))
-    return blocks, comb
+        owner = lax.rem(me + owners - step, owners)
+        cells = lax.dynamic_index_in_dim(apart, owner, 1, False).reshape(height, columns)
+        strips = [cells[:, side * LANES : (side + 1) * LANES] for side in range(sides)]
+        seam = lax.dynamic_index_in_dim(seams, twin_of(owner, owners), 0, False)
+        strips += [note.astype(BF16), seam.astype(BF16)]
+        blocks.append(jnp.concatenate(strips, axis=0))
+    return blocks
 
 
 def pair_places(first, second, dates):
@@ -122,46 +187,34 @@
     return jnp.where(same, inside, across), sign
 
 
-def pair_weights(block_refs, wide, dates_here, slots):
-    owners = len(block_refs)
+def inverse_of(wide, step, owners, slots):
+    lanes = wide.shape[1]
+    owner = lax.rem(lax.axis_index("date") + step, owners)
+    moved = pltpu.roll(wide, lax.rem(lanes - owner * slots, lanes), 1)
+    return moved[:, :LANES] * (1.0 / 128.0)
+
+
+def slot_weights(block_ref, inverse, owners, dates_here):
     dates = owners * dates_here
-    me = lax.axis_index("date")
-    lanes = wide.shape[1]
-    ring = jnp.zeros((8, lanes), F32)
-    for step, block_ref in enumerate(block_refs):
-        height = block_ref.shape[0]
-        note = block_ref[height - NOTE_ROWS : height, :LANES].astype(F32)[:8]
-        if lanes > LANES:
-            note = jnp.concatenate([note, jnp.zeros((8, lanes - LANES), F32)], axis=1)
-        ring = ring + pltpu.roll(note, lax.rem(me + step, owners) * slots, 1)
-    start = lax.rem(me + owners - 1, owners) * dates_here
-    start = jnp.full((1, lanes), start, jnp.int32).astype(F32)
+    start = lax.rem(lax.axis_index("date") + owners - 1, owners) * dates_here
+    start = jnp.full((1, LANES), start, jnp.int32).astype(F32)
+    height = block_ref.shape[0]
+    note = block_ref[height - NOTE_ROWS : height].astype(F32)
 
     def wrapped(value):
         return jnp.where(value < 0.0, value + dates, value)
 
-    place, sign = pair_places(wrapped(ring[0:1] - start), wrapped(ring[1:2] - start), dates)
-    place = jnp.where(ring[2:3] > 0.5, place, -1.0)
+    place, sign = pair_places(wrapped(note[0:1] - start), wrapped(note[1:2] - start), dates)
+    place = jnp.where(note[2:3] > 0.5, place, -1.0)
     pairs = pair_rows(dates)
-    chosen = jnp.where(iota((pairs, lanes), 0).astype(F32) == place, 1.0, 0.0).astype(BF16)
-    scaled = wide * (1.0 / 128.0)
-    signed = scaled * sign
-    stacked = jnp.concatenate([*halves(scaled), *halves(signed)], axis=0)
+    chosen = jnp.where(iota((pairs, LANES), 0).astype(F32) == place, 1.0, 0.0).astype(BF16)
+    stacked = jnp.concatenate([*halves(inverse), *halves(inverse * sign)], axis=0)
     spread = lax.dot_general(
         stacked, chosen, (((1,), (1,)), ((), ())), preferred_element_type=F32
     )
-    tall = wide.shape[0]
-    weights = []
-    for part in range(2):
-        summed = spread[2 * part * tall : (2 * part + 1) * tall]
-        summed = summed + spread[(2 * part + 1) * tall : (2 * part + 2) * tall]
-        high, low = halves(summed)
-        weights.append(
-            jnp.concatenate(
-                [jnp.concatenate([high, high], axis=1), jnp.concatenate([low, low], axis=1)], axis=0
-            )
-        )
-    return weights
+    tall = inverse.shape[0]
+    parts = [spread[at * tall : (at + 1) * tall] for at in range(4)]
+    return parts[0] + parts[1], parts[2] + parts[3]
 
 
 def pair_rows(dates):
@@ -179,21 +232,14 @@
     return units
 
 
-def comb_of(columns):
-    looks = columns // 8
-    column, lane = iota((columns, columns), 0), iota((columns, columns), 1)
-    here = (column // 8 == lane % looks) & (column % 8 == lane // looks)
-    return jnp.where(here, 1.0, 0.0).astype(BF16)
-
-
 def spread_block(block_ref, comb, dates_here, seat, rows_ref):
-    height = block_ref.shape[0] - NOTE_ROWS
-    rows = height // (2 * dates_here)
-    combed = jnp.dot(block_ref[:height], comb, preferred_element_type=F32)
+    sides = rows_ref.shape[1]
+    combed = jnp.dot(cells_of(block_ref, sides), comb, preferred_element_type=F32)
+    rows = combed.shape[0] // (2 * dates_here)
     for own in range(dates_here):
         for part in range(2):
             at = (own * 2 + part) * rows
-            for side in range(rows_ref.shape[1]):
+            for side in range(sides):
                 rows_ref[part, side, pl.ds(seat + own, rows, stride=GROUP), :] = combed[
                     at : at + rows, side * LANES : (side + 1) * LANES
                 ]
@@ -280,31 +326,22 @@
 
 
 def seam_of(block_ref, dates_here, seat, seam_ref):
-    height = block_ref.shape[0] - NOTE_ROWS
-    columns = block_ref.shape[1]
-    rows = height // (2 * dates_here)
-    column, lane = iota((columns, LANES), 0), iota((columns, LANES), 1) % 8
-    wanted = jnp.where(lane < 4, lane, columns - 8 + lane)
-    pick = jnp.where(column == wanted, 1.0, 0.0).astype(BF16)
-    cells = jnp.dot(block_ref[:height], pick, preferred_element_type=F32)
-    row, lane = iota((height, LANES), 0), iota((height, LANES), 1)
-    cells = jnp.where(row % rows == lane // 8, cells, 0.0).astype(BF16)
-    line, row = iota((16, height), 0), iota((16, height), 1) // rows
-    gather = jnp.where((line < 2 * dates_here) & (row == line % dates_here * 2 + line // dates_here), 1.0, 0.0)
-    lines = jnp.dot(gather.astype(BF16), cells, preferred_element_type=F32)
+    height = block_ref.shape[0]
+    lines = block_ref[height - NOTE_ROWS : height].astype(F32)
     for part in range(2):
-        seam_ref[part, seat : seat + dates_here, :] = lines[
-            part * dates_here : (part + 1) * dates_here
-        ]
+        at = NOTE + part * dates_here
+        seam_ref[part, seat : seat + dates_here, :] = lines[at : at + dates_here]
 
 
 def early_kernel(dates_here, *refs):
-    comb_ref, *block_refs, ring_ref, pair_ref, seam_ref, rows_ref = refs
-    columns = block_refs[0].shape[1]
+    *block_refs, comb_ref, fold_ref, ring_ref, pair_ref, seam_ref, rows_ref = refs
+    columns = comb_ref.shape[0]
     looks = columns // 8
     tiles = ring_ref.shape[3]
     half_rows = rows_ref.shape[2] // GROUP // 2
-    comb = comb_ref[...]
+    comb = comb_of(columns)
+    comb_ref[...] = comb
+    fold_ref[...] = fold_of(fold_ref.shape, looks, half_rows)
     for index, block_ref in enumerate(block_refs):
         spread_block(block_ref, comb, dates_here, index * dates_here, rows_ref)
         seam_of(block_ref, dates_here, index * dates_here, seam_ref)
@@ -330,25 +367,47 @@
     )
 
 
-def edge_kernel(dates_here, slots, *refs):
-    *refs, weights_ref, message_ref, wide_ref, seams_ref, pair_ref = refs
-    *block_refs, inverse_ref, seam_ref = refs
-    block_refs = block_refs[::-1]
-    owners = len(block_refs)
-    dates = owners * dates_here
-    groups = dates // GROUP
-    pairs = pair_rows(dates)
-    together = GROUP // dates_here
-    tall = wide_ref.shape[0]
-
-    for group in range(1, groups):
-        for index in range(together):
-            block_ref = block_refs[group * together + index - 1]
-            seam_of(block_ref, dates_here, index * dates_here, seams_ref.at[group - 1])
+def place_of(step, owners, dates_here):
+    date = (step + 1) % owners * dates_here
+    return date // GROUP, date % GROUP
+
+
+def middle_kernel(dates_here, slots, steps, *refs):
+    *refs, rows_ref, seams_ref, partial_ref, rest_ref, wide_ref = refs
+    comb_ref, inverse_ref, *block_refs = refs
+    owners = len(block_refs) + 1
+    comb = comb_ref[...]
     wide_ref[...] = jnp.zeros_like(wide_ref)
     wide_ref[: inverse_ref.shape[0], : inverse_ref.shape[1]] = inverse_ref[...]
-    weights = pair_weights(block_refs, wide_ref[...], dates_here, slots)
+    wide = wide_ref[...]
+    sums = [0.0, 0.0]
+    for step, block_ref in zip(steps, block_refs):
+        group, seat = place_of(step, owners, dates_here)
+        if group:
+            spread_block(block_ref, comb, dates_here, seat, rows_ref.at[group - 1])
+            seam_of(block_ref, dates_here, seat, seams_ref.at[group - 1])
+        more = slot_weights(block_ref, inverse_of(wide, step, owners, slots), owners, dates_here)
+        sums = [one + two for one, two in zip(sums, more)]
     for part in range(2):
+        partial_ref[part] = sums[part]
+    rest_ref[...] = inverse_of(wide, 1, owners, slots)
+
+
+def edge_kernel(dates_here, owners, *refs):
+    block_ref, seam_ref, others_ref, partial_ref, rest_ref, *refs = refs
+    weights_ref, message_ref, seams_ref, pair_ref = refs
+    dates = owners * dates_here
+    pairs = pair_rows(dates)
+    tall = rest_ref.shape[0]
+
+    seams_ref[...] = others_ref[...]
+    group, seat = place_of(1, owners, dates_here)
+    seam_of(block_ref, dates_here, seat, seams_ref.at[group - 1])
+    weights = []
+    for part, more in enumerate(slot_weights(block_ref, rest_ref[...], owners, dates_here)):
+        high, low = halves(partial_ref[part] + more)
+        wide = [jnp.concatenate([half, half], axis=1) for half in (high, low)]
+        weights.append(jnp.concatenate(wide, axis=0))
         weights_ref[part] = weights[part]
 
     lane = iota((GROUP, LANES), 1) % 8
@@ -368,36 +427,27 @@
             for half in range(2):
                 at = half * pairs + unit * count
                 pair_ref[part, at : at + count, :] = bits[half]
-    sums = []
     for part in range(2):
         summed = jnp.dot(weights[part], pair_ref[part], preferred_element_type=F32)
-        summed = summed[:tall] + summed[tall:]
-        for shift in (1, 2, 8):
-            summed = summed + pltpu.roll(summed, LANES - shift, 1)
-        sums.append(summed)
-    lane = iota((tall, LANES), 1)
-    message_ref[...] = jnp.where(lane % 4 == 1, pltpu.roll(sums[1], 1, 1), sums[0])
+        message_ref[part * tall : (part + 1) * tall] = summed[:tall] + summed[tall:]
 
 
 def series_kernel(dates_here, *refs):
     *refs, looked_ref, rows_ref, ring_ref, far_ref, pair_ref = refs
-    *block_refs, comb_ref, weights_ref, first_ref, first_pair_ref = refs
-    block_refs = block_refs[::-1]
+    block_ref, comb_ref, weights_ref, first_ref, first_pair_ref, others_ref = refs
     groups = 1 + ring_ref.shape[0]
     dates = groups * GROUP
     pairs = pair_rows(dates)
-    columns = block_refs[0].shape[1]
+    columns = comb_ref.shape[0]
     looks = columns // 8
     tiles = ring_ref.shape[4]
-    half_rows = rows_ref.shape[2] // GROUP // 2
+    half_rows = rows_ref.shape[3] // GROUP // 2
     tall = looked_ref.shape[1]
-    together = GROUP // dates_here
-
-    comb = comb_ref[...]
+
+    rows_ref[...] = others_ref[...]
+    last_group, seat = place_of(1, dates // dates_here, dates_here)
+    spread_block(block_ref, comb_ref[...], dates_here, seat, rows_ref.at[last_group - 1])
     for group in range(1, groups):
-        for index in range(together):
-            block_ref = block_refs[(group - 1) * together + index]
-            spread_block(block_ref, comb, dates_here, index * dates_here, rows_ref)
 
         def keep(part, odd, place, tile, cells):
             ring_ref[group - 1, part, odd, place, tile] = cells
@@ -405,7 +455,7 @@
                 at = pl.ds(2 * copy * GROUP + odd, GROUP, stride=2)
                 far_ref[group - 1, part, place, tile, at, :] = cells
 
-        pack_group(rows_ref, looks, half_rows, keep)
+        pack_group(rows_ref.at[group - 1], looks, half_rows, keep)
 
     for part in range(2):
         for half in range(2):
@@ -439,9 +489,9 @@
         looked_ref[part] = summed[:tall] + summed[tall:]
 
 
-def finish_kernel(looked_ref, second_ref, first_ref, out_ref, sum_ref):
+def finish_kernel(looked_ref, fold_ref, second_ref, first_ref, out_ref, sum_ref):
     times, parts, half_rows, looks = out_ref.shape
-    tall = first_ref.shape[0]
+    tall = looked_ref.shape[1]
     pack = LANES // looks
     here, last = lax.axis_index("col"), lax.axis_size("col") - 1
     even = lax.rem(here, 2) == 0
@@ -449,19 +499,16 @@
     nothing = jnp.zeros_like(first)
     from_right = jnp.where(here == last, nothing, jnp.where(even, first, second))
     from_left = jnp.where(here == 0, nothing, jnp.where(even, second, first))
-    lane = iota((tall, LANES), 1)
+    edges = jnp.concatenate(halves(jnp.concatenate([from_right, from_left], axis=1)), axis=0)
+    edges = jnp.dot(edges, fold_ref[...], preferred_element_type=F32)
+    edges = edges[: parts * tall] + edges[parts * tall :]
     for part in range(parts):
+        value = looked_ref[part] + edges[part * tall : (part + 1) * tall]
         for half_row in range(half_rows):
             tile, near = half_row // pack, half_row % pack
-            value = looked_ref[part, :, tile * LANES : (tile + 1) * LANES]
-            value = pltpu.roll(value, -near * looks % LANES, 1)
-            at = 16 * half_row + part
-            right = pltpu.roll(from_right, (looks - 1 - at) % LANES, 1)
-            left = pltpu.roll(from_left, (-4 - at) % LANES, 1)
-            value = value + jnp.where(lane == looks - 1, right, 0.0)
-            value = value + jnp.where(lane == 0, left, 0.0)
+            one = value[:, tile * LANES : (tile + 1) * LANES]
             at = (part * half_rows + half_row) * tall
-            sum_ref[at : at + tall, :] = value
+            sum_ref[at : at + tall, :] = pltpu.roll(one, -near * looks % LANES, 1)
     for time in range(times):
         for part in range(parts):
             rows = sum_ref[pl.ds(part * half_rows * tall + time, half_rows, stride=tall), :]
@@ -473,11 +520,8 @@
     for owner in range(owners):
         for column in range(count):
             partner = column + 1 if (column - first) % 2 == 0 else column - 1
-            to = owner
-            if not 0 <= partner < count:
-                partner = column
-                to = owner ^ 1 if owners % 2 == 0 else owner
-            moves.append((owner * count + column, to * count + partner))
+            partner = partner if 0 <= partner < count else column
+            moves.append((owner * count + column, twin_of(owner, owners) * count + partner))
     return moves
 
 
@@ -490,7 +534,7 @@
     looks = columns // 8
     tiles = -(-half_rows // (LANES // looks))
 
-    blocks, comb = cut(scenes, pair_dates.T, pair_count, owners)
+    blocks = cut(scenes, pair_dates.T, pair_count, owners)
     for step in range(1, owners):
         moves = [(owner, (owner - step) % owners) for owner in range(owners)]
         blocks[step] = lax.ppermute(blocks[step], "date", moves)
@@ -500,41 +544,55 @@
     sides = columns // LANES
     order = [blocks[(place - 1) % owners] for place in range(owners)]
     order = [held(block) for block in order]
-    by_arrival = [held(block) for block in blocks[:0:-1] + blocks[:1]]
     group_rows = pltpu.VMEM((parts, sides, rows * GROUP, LANES), F32)
-    first_group, first_pairs, first_seam = pl.pallas_call(
+    comb, fold, first_group, first_pairs, first_seam = pl.pallas_call(
         functools.partial(early_kernel, dates_here),
         out_shape=[
+            pltpu.VMEM((columns, columns), BF16),
+            pltpu.VMEM((2 * LANES, tiles * LANES), BF16),
             pltpu.VMEM((parts, 2, 8, tiles, GROUP, LANES), F32),
             pltpu.VMEM((parts, 2, GROUP * GROUP // 2, tiles * LANES), BF16),
             pltpu.VMEM((parts, GROUP, LANES), F32),
         ],
-        in_specs=[IN_VMEM] * (GROUP // dates_here + 1),
-        out_specs=[IN_VMEM] * 3,
+        in_specs=[IN_VMEM] * (GROUP // dates_here),
+        out_specs=[IN_VMEM] * 5,
         scratch_shapes=[group_rows],
         compiler_params=pltpu.CompilerParams(vmem_limit_bytes=40 << 20),
-    )(held(comb), *order[: GROUP // dates_here])
+    )(*order[: GROUP // dates_here])
     others = dates // GROUP - 1
+    steps = [*range(owners - 1, 1, -1), 0]
+    group_rows = pltpu.VMEM((others, *group_rows.shape), F32)
+    other_rows, other_seams, partial, rest = pl.pallas_call(
+        functools.partial(middle_kernel, dates_here, pair_dates.shape[0], steps),
+        out_shape=[
+            group_rows,
+            pltpu.VMEM((others, parts, GROUP, LANES), F32),
+            pltpu.VMEM((parts, tall, pairs), F32),
+            pltpu.VMEM((tall, LANES), F32),
+        ],
+        in_specs=[IN_VMEM] * (owners + 1),
+        out_specs=[IN_VMEM] * 4,
+        scratch_shapes=[pltpu.VMEM((tall, round_up(inverse.shape[1], LANES)), F32)],
+        compiler_params=pltpu.CompilerParams(vmem_limit_bytes=40 << 20),
+    )(held(comb), held(inverse), *[held(blocks[step]) for step in steps])
     weights, edge = pl.pallas_call(
-        functools.partial(edge_kernel, dates_here, pair_dates.shape[0]),
+        functools.partial(edge_kernel, dates_here, owners),
         out_shape=[
             pltpu.VMEM((parts, 2 * tall, 2 * pairs), BF16),
-            pltpu.VMEM((tall, LANES), F32),
+            pltpu.VMEM((parts * tall, LANES), F32),
         ],
-        in_specs=[IN_VMEM] * (owners + 2),
+        in_specs=[IN_VMEM] * 5,
         out_specs=[IN_VMEM] * 2,
         scratch_shapes=[
-            pltpu.VMEM((tall, round_up(inverse.shape[1], LANES)), F32),
             pltpu.VMEM((others, parts, GROUP, LANES), F32),
             pltpu.VMEM((parts, 2 * pairs, LANES), BF16),
         ],
         compiler_params=pltpu.CompilerParams(vmem_limit_bytes=40 << 20),
-    )(*by_arrival, held(inverse), held(first_seam))
-    late = [held(block) for block in order[GROUP // dates_here :]][::-1]
+    )(*[held(array) for array in (blocks[1], first_seam, other_seams, partial, rest)])
     looked = pl.pallas_call(
         functools.partial(series_kernel, dates_here),
         out_shape=pltpu.VMEM((parts, tall, tiles * LANES), F32),
-        in_specs=[IN_VMEM] * (len(late) + 4),
+        in_specs=[IN_VMEM] * 6,
         out_specs=IN_VMEM,
         scratch_shapes=[
             group_rows,
@@ -546,7 +604,7 @@
         cost_estimate=pl.CostEstimate(
             flops=2 * parts * pairs * columns * rows * 8, bytes_accessed=1 << 20, transcendentals=0
         ),
-    )(*late, held(comb), held(weights), held(first_group), held(first_pairs))
+    )(*[held(one) for one in (blocks[1], comb, weights, first_group, first_pairs, other_rows)])
 
     first = lax.ppermute(edge, ("date", "col"), column_swap(0, owners, count))
     second = lax.ppermute(edge, ("date", "col"), column_swap(1, owners, count))
@@ -555,10 +613,10 @@
         out_shape=jax.ShapeDtypeStruct(
             (inverse.shape[0], parts, half_rows, columns // 8), F32
         ),
-        in_specs=[IN_VMEM] * 3,
+        in_specs=[IN_VMEM] * 4,
         out_specs=IN_VMEM,
         scratch_shapes=[pltpu.VMEM((parts * half_rows * tall, LANES), F32)],
-    )(held(looked), held(second), held(first))
+    )(held(looked), held(fold), held(second), held(first))
 
 
 def solution(mesh):

time: 13.9 us -> 13.9 us (level)
  the two profiles are of different devices: /device:TPU:18 before, /device:TPU:17 now
where the time goes in v6:
time: 13.9 us; the launch traced here: 13.7 us
  waiting for transfers between devices  5.21 us (37%)
  Pallas kernels  4.14 us (30%)
  starting transfers between devices  3.35 us (24%)
  between operations  0.74 us (5%)
  local copies, waits for them, and re-layouts  0.26 us (2%)
    ppermute x3, waiting for transfers between devices, per_device(): blocks[step] = lax.ppermute(blocks[step], 'date', moves)  2.75 us
    ppermute x3, starting transfers between devices, per_device(): blocks[step] = lax.ppermute(blocks[step], 'date', moves)  2.3 us
    ppermute x1, waiting for transfers between devices, per_device(): second = lax.ppermute(edge, ('date', 'col'), column_swap(1, owners, count))  1.43 us
    pallas_call x1, Pallas kernels, per_device(): pl.pallas_call(functools.partial(series_kernel, dates_here), out_shape=pl...  1.15 us
    ppermute x1, starting transfers between devices, per_device(): first = lax.ppermute(edge, ('date', 'col'), column_swap(0, owners, count))  1.05 us
    ppermute x1, waiting for transfers between devices, per_device(): first = lax.ppermute(edge, ('date', 'col'), column_swap(0, owners, count))  1.03 us
    pallas_call x1, Pallas kernels, per_device(): pl.pallas_call(finish_kernel, out_shape=jax.ShapeDtypeStruct((inverse.sha...  0.91 us
    pallas_call x1, Pallas kernels, cut(): pl.pallas_call(seam_kernel, out_shape=[pltpu.VMEM((owners, NOTE, LANES),...  0.73 us
  transfers between devices with their start and end apart: 5, of which 5 were waited for; matrix products, arithmetic and copies ran while one was open for 0% of the time, Pallas kernels for 15%

profile of v6, /device:TPU:17, one launch (start us, length us, event | category | flops | bytes accessed | tf_op | source)
XLA Modules:
  0.0 13.7 jit_solution(1769062341630416719)
XLA Ops:
  0.0 0.0 copy-start
  0.7 0.3 %copy-done = bf16[4,2,64,256]{3,2,1,0:T(8,128)(2,1)S(1)} copy-done((bf16[4,2,64,256]{3,2,1,0:T(8,128)(2,1)S(1)}, bf16[4,2,64,256]{3,2,1,0:T(8,128)(2,1)}, u32[]{:S(2)}) %copy-start) | copy-done | bytes 262168
  1.0 0.7 %shard_map.48 = (f32[4,8,128]{2,1,0:T(8,128)S(1)}, f32[8,128]{1,0:T(8,128)S(1)}) custom-call(bf16[4,2,64,256]{3,2,1,0:T(8,128)(2,1)S(1)} %copy-done, s32[2,24]{1,0:T(2,128)} %bitcast.1, f32[8,128]{1,0:T(8,128)S(1)} %shard_map.47.live_ref), custom_call_target="tpu_custom_call" | custom-call | tf_op jit(solution)/shard_map/pallas_call | solution.py:134
  1.7 0.1 shard_map.49
  1.8 1.8 %collective-permute-start.1 = (bf16[272,128]{1,0:T(8,128)(2,1)S(1)}, bf16[272,128]{1,0:T(8,128)(2,1)S(1)}, u32[]{:S(2)}, u32[]{:S(2)}) collective-permute-start(bf16[272,128]{1,0:T(8,128)(2,1)S(1)} %get-tuple-element.25), channel_id=1, source_target_pairs={{0,4},{4,8},{8,12},{12,0},{1,5},{5,9},{9,13},{13,1},{2,6},{6,10},{... | collective-permute-start | bytes 208904 | tf_op jit(solution)/shard_map/ppermute | solution.py:540
  3.6 0.3 %collective-permute-start.2 = (bf16[272,128]{1,0:T(8,128)(2,1)S(1)}, bf16[272,128]{1,0:T(8,128)(2,1)S(1)}, u32[]{:S(2)}, u32[]{:S(2)}) collective-permute-start(bf16[272,128]{1,0:T(8,128)(2,1)S(1)} %get-tuple-element.29), channel_id=1, source_target_pairs={{0,8},{4,12},{8,0},{12,4},{1,9},{5,13},{9,1},{13,5},{2,10},{6,14},... | collective-permute-start | bytes 208904 | tf_op jit(solution)/shard_map/ppermute | solution.py:540
  3.9 0.2 %collective-permute-start = (bf16[272,128]{1,0:T(8,128)(2,1)S(1)}, bf16[272,128]{1,0:T(8,128)(2,1)S(1)}, u32[]{:S(2)}, u32[]{:S(2)}) collective-permute-start(bf16[272,128]{1,0:T(8,128)(2,1)S(1)} %get-tuple-element.24), channel_id=1, source_target_pairs={{0,12},{4,0},{8,4},{12,8},{1,13},{5,1},{9,5},{13,9},{2,14},{6,2},{... | collective-permute-start | bytes 208904 | tf_op jit(solution)/shard_map/ppermute | solution.py:540
  4.1 0.9 %collective-permute-done.1.refs_0_.refs_2_ = bf16[272,128]{1,0:T(8,128)(2,1)S(1)} collective-permute-done((bf16[272,128]{1,0:T(8,128)(2,1)S(1)}, bf16[272,128]{1,0:T(8,128)(2,1)S(1)}, u32[]{:S(2)}, u32[]{:S(2)}) %collective-permute-start.1) | collective-permute-done | bytes 69664 | tf_op jit(solution)/shard_map/ppermute | solution.py:540
  5.0 0.0 copy-start.1
  5.0 0.7 %shard_map.50 = (bf16[256,256]{1,0:T(8,128)(2,1)S(1)}, bf16[256,256]{1,0:T(8,128)(2,1)S(1)}, f32[2,2,8,2,8,128]{5,4,3,2,1,0:T(8,128)S(1)}, bf16[2,2,32,256]{3,2,1,0:T(8,128)(2,1)S(1)}, f32[2,8,128]{2,1,0:T(8,128)S(1)}) custom-call(bf16[272,128]{1,0:T(8,128)(2,1)S(1)} %collective-permute-done.1.refs_0_.refs_2_, ...), custom_call_target="tpu_custom_call" | custom-call | tf_op jit(solution)/shard_map/pallas_call | solution.py:548
  5.7 1.6 %collective-permute-done.2.refs_3_ = bf16[272,128]{1,0:T(8,128)(2,1)S(1)} collective-permute-done((bf16[272,128]{1,0:T(8,128)(2,1)S(1)}, bf16[272,128]{1,0:T(8,128)(2,1)S(1)}, u32[]{:S(2)}, u32[]{:S(2)}) %collective-permute-start.2) | collective-permute-done | bytes 69664 | tf_op jit(solution)/shard_map/ppermute | solution.py:540
  7.3 0.0 copy-done.1
  7.3 0.2 %shard_map.51 = (f32[1,2,2,128,128]{4,3,2,1,0:T(8,128)S(1)}, f32[1,2,8,128]{3,2,1,0:T(8,128)S(1)}, f32[2,16,128]{2,1,0:T(8,128)S(1)}, f32[16,128]{1,0:T(8,128)S(1)}) custom-call(bf16[256,256]{1,0:T(8,128)(2,1)S(1)} %get-tuple-element.27.refs_0_.refs_1_, f32[15,96]{1,0:T(8,128)S(1)} %copy-done.1, bf16[272,128]{1,0:T(8,128)(2,1)S(1)} %collective-permute-done.1.refs_0_.refs_2_, ...), custom_call_target="tpu_custom_call" | custom-call | tf_op jit(solution)/shard_map/pallas_call | solution.py:565
  7.5 0.3 %collective-permute-done.refs_0_ = bf16[272,128]{1,0:T(8,128)(2,1)S(1)} collective-permute-done((bf16[272,128]{1,0:T(8,128)(2,1)S(1)}, bf16[272,128]{1,0:T(8,128)(2,1)S(1)}, u32[]{:S(2)}, u32[]{:S(2)}) %collective-permute-start) | collective-permute-done | bytes 69664 | tf_op jit(solution)/shard_map/ppermute | solution.py:540
  7.8 0.3 %shard_map.52 = (bf16[2,32,256]{2,1,0:T(8,128)(2,1)S(1)}, f32[32,128]{1,0:T(8,128)S(1)}) custom-call(bf16[272,128]{1,0:T(8,128)(2,1)S(1)} %collective-permute-done.refs_0_, f32[2,8,128]{2,1,0:T(8,128)S(1)} %get-tuple-element.28.refs_1_, f32[1,2,8,128]{3,2,1,0:T(8,128)S(1)} %get-tuple-element.30.refs_2_, f32[2,16,128]{2,1,0:T(8,128)S(1)} %get-tuple-element.31.refs_3_, ...), custom_call_target="tpu_custom_call" | custom-call | tf_op jit(solution)/shard_map/pallas_call | solution.py:578
  8.1 1.0 %collective-permute-start.4 = (f32[32,128]{1,0:T(8,128)S(1)}, f32[32,128]{1,0:T(8,128)S(1)}, u32[]{:S(2)}, u32[]{:S(2)}) collective-permute-start(f32[32,128]{1,0:T(8,128)S(1)} %get-tuple-element.38), channel_id=1, source_target_pairs={{0,5},{1,4},{2,7},{3,6},{4,1},{5,0},{6,3},{7,2},{8,13},{9,12},{10,... | collective-permute-start | bytes 49160 | tf_op jit(solution)/shard_map/ppermute | solution.py:609
  9.2 0.0 collective-permute-start.3
  9.2 1.1 %shard_map.53.looked_ref = f32[2,16,256]{2,1,0:T(8,128)S(1)} custom-call(bf16[272,128]{1,0:T(8,128)(2,1)S(1)} %collective-permute-done.refs_0_, bf16[256,256]{1,0:T(8,128)(2,1)S(1)} %get-tuple-element.27.refs_0_.refs_1_, bf16[2,32,256]{2,1,0:T(8,128)(2,1)S(1)} %get-tuple-element.33.refs_2_, f32[2,2,8,2,8,128]{5,4,3,2,1,0:T(8,128)S(1)} %get-tuple-element.34.refs_3_, ...), custom_call_target="tpu_custom_call" | custom-call | flops 16777216 | bytes 1048576 | tf_op jit(solution)/shard_map/pallas_call | solution.py:592
  10.3 1.0 %collective-permute-done.4.first_ref = f32[32,128]{1,0:T(8,128)S(1)} collective-permute-done((f32[32,128]{1,0:T(8,128)S(1)}, f32[32,128]{1,0:T(8,128)S(1)}, u32[]{:S(2)}, u32[]{:S(2)}) %collective-permute-start.4) | collective-permute-done | bytes 16416 | tf_op jit(solution)/shard_map/ppermute | solution.py:609
  11.4 1.4 %collective-permute-done.3.second_ref = f32[32,128]{1,0:T(8,128)S(1)} collective-permute-done((f32[32,128]{1,0:T(8,128)S(1)}, f32[32,128]{1,0:T(8,128)S(1)}, u32[]{:S(2)}, u32[]{:S(2)}) %collective-permute-start.3) | collective-permute-done | bytes 16416 | tf_op jit(solution)/shard_map/ppermute | solution.py:610
  12.8 0.9 %shard_map.54 = f32[15,2,8,32]{3,2,1,0:T(8,128)} custom-call(f32[2,16,256]{2,1,0:T(8,128)S(1)} %shard_map.53.looked_ref, bf16[256,256]{1,0:T(8,128)(2,1)S(1)} %get-tuple-element.37.fold_ref, f32[32,128]{1,0:T(8,128)S(1)} %collective-permute-done.3.second_ref, f32[32,128]{1,0:T(8,128)S(1)} %collective-permute-done.4.first_ref), custom_call_target="tpu_custom_call" | custom-call | tf_op jit(solution)/shard_map/pallas_call | solution.py:611
  (2 shorter events, 0.0 us)
Async XLA Ops:
  0.0 1.0 %copy-start = (bf16[4,2,64,256]{3,2,1,0:T(8,128)(2,1)S(1)}, bf16[4,2,64,256]{3,2,1,0:T(8,128)(2,1)}, u32[]{:S(2)}) copy-start(bf16[4,2,64,256]{3,2,1,0:T(8,128)(2,1)} %scenes_ref.3) | copy-start | bytes 786436
  1.8 3.2 %collective-permute-start.1 = (bf16[272,128]{1,0:T(8,128)(2,1)S(1)}, bf16[272,128]{1,0:T(8,128)(2,1)S(1)}, u32[]{:S(2)}, u32[]{:S(2)}) collective-permute-start(bf16[272,128]{1,0:T(8,128)(2,1)S(1)} %get-tuple-element.25), channel_id=1, source_target_pairs={{0,4},{4,8},{8,12},{12,0},{1,5},{5,9},{9,13},{13,1},{2,6},{6,10},{... | collective-permute-start | bytes 208904 | tf_op jit(solution)/shard_map/ppermute | solution.py:540
  3.6 3.7 %collective-permute-start.2 = (bf16[272,128]{1,0:T(8,128)(2,1)S(1)}, bf16[272,128]{1,0:T(8,128)(2,1)S(1)}, u32[]{:S(2)}, u32[]{:S(2)}) collective-permute-start(bf16[272,128]{1,0:T(8,128)(2,1)S(1)} %get-tuple-element.29), channel_id=1, source_target_pairs={{0,8},{4,12},{8,0},{12,4},{1,9},{5,13},{9,1},{13,5},{2,10},{6,14},... | collective-permute-start | bytes 208904 | tf_op jit(solution)/shard_map/ppermute | solution.py:540
  3.9 3.9 %collective-permute-start = (bf16[272,128]{1,0:T(8,128)(2,1)S(1)}, bf16[272,128]{1,0:T(8,128)(2,1)S(1)}, u32[]{:S(2)}, u32[]{:S(2)}) collective-permute-start(bf16[272,128]{1,0:T(8,128)(2,1)S(1)} %get-tuple-element.24), channel_id=1, source_target_pairs={{0,12},{4,0},{8,4},{12,8},{1,13},{5,1},{9,5},{13,9},{2,14},{6,2},{... | collective-permute-start | bytes 208904 | tf_op jit(solution)/shard_map/ppermute | solution.py:540
  5.0 2.3 %copy-start.1 = (f32[15,96]{1,0:T(8,128)S(1)}, f32[15,96]{1,0:T(8,128)}, u32[]{:S(2)}) copy-start(f32[15,96]{1,0:T(8,128)} %refs_1_.1) | copy-start | bytes 17284
  8.1 3.2 %collective-permute-start.4 = (f32[32,128]{1,0:T(8,128)S(1)}, f32[32,128]{1,0:T(8,128)S(1)}, u32[]{:S(2)}, u32[]{:S(2)}) collective-permute-start(f32[32,128]{1,0:T(8,128)S(1)} %get-tuple-element.38), channel_id=1, source_target_pairs={{0,5},{1,4},{2,7},{3,6},{4,1},{5,0},{6,3},{7,2},{8,13},{9,12},{10,... | collective-permute-start | bytes 49160 | tf_op jit(solution)/shard_map/ppermute | solution.py:609
  9.2 3.6 %collective-permute-start.3 = (f32[32,128]{1,0:T(8,128)S(1)}, f32[32,128]{1,0:T(8,128)S(1)}, u32[]{:S(2)}, u32[]{:S(2)}) collective-permute-start(f32[32,128]{1,0:T(8,128)S(1)} %get-tuple-element.38), channel_id=1, source_target_pairs={{0,4},{1,6},{2,5},{3,7},{4,0},{5,2},{6,1},{7,3},{8,12},{9,14},{10,... | collective-permute-start | bytes 49160 | tf_op jit(solution)/shard_map/ppermute | solution.py:610

commit v7 on v6

--- a/solution.py
+++ b/solution.py
@@ -50,41 +50,44 @@
     right = cell < LANES
     cell = cell % LANES
     half_row = cell // 16
-    here = right & (cell % 8 < 4) & (target == half_row * looks + looks - 1)
-    here = here | ~right & (cell % 8 >= 4) & (target == half_row * looks)
+    here = right & (target == half_row * looks + looks - 1)
+    here = here | ~right & (target == half_row * looks)
     return jnp.where(here & (half_row < half_rows), 1.0, 0.0).astype(BF16)
 
 
-def live_kernel(slots, count_ref, blank_ref, live_ref):
-    row, lane = iota(live_ref.shape, 0), iota(live_ref.shape, 1)
-    live = (row == 2) & (lane < jnp.minimum(count_ref[0], slots))
-    live_ref[...] = jnp.where(live, 1.0, blank_ref[...])
-
-
-def seam_kernel(scenes_ref, dates_ref, live_ref, seams_ref, note_ref, fetched_ref, semaphore):
+def note_kernel(rows, count_ref, dates_ref, blank_ref, *refs):
+    note_ref, pick_ref, own_ref, gather_ref, fetched_ref, semaphore = refs
     fetch = pltpu.make_async_copy(dates_ref, fetched_ref, semaphore)
     fetch.start()
+    columns, (all_rows, lanes), (lines, height) = pick_ref.shape[0], own_ref.shape, gather_ref.shape
+    column, lane = iota((columns, lanes), 0), iota((columns, lanes), 1) % 8
+    wanted = jnp.where(lane < 4, lane, columns - 8 + lane)
+    pick_ref[...] = jnp.where(column == wanted, 1.0, 0.0).astype(BF16)
+    row, lane = iota((all_rows, lanes), 0), iota((all_rows, lanes), 1)
+    own_ref[...] = jnp.where(row % rows == lane // 8, 1.0, 0.0)
+    owners, images = all_rows // rows, height // all_rows
+    line, row = iota((lines, height), 0), iota((lines, height), 1) // rows
+    place = line % NOTE
+    wanted = (place % (images // 2) * 2 + place // (images // 2)) * owners + line // NOTE
+    gather_ref[...] = jnp.where((place < images) & (row == wanted), 1.0, 0.0).astype(BF16)
+    row, lane = iota(note_ref.shape, 0), iota(note_ref.shape, 1)
+    slots = dates_ref.shape[1]
+    live = (row == 2) & (lane < jnp.minimum(count_ref[0], slots))
+    note_ref[...] = jnp.where(live, 1.0, blank_ref[...])
+    fetch.wait()
+    note_ref[:2, :slots] = fetched_ref[...].astype(F32)
+
+
+def seam_kernel(scenes_ref, pick_ref, own_ref, gather_ref, seams_ref):
     dates_here, parts, all_rows, columns = scenes_ref.shape
-    owners = seams_ref.shape[0]
-    rows = all_rows // owners
     height = dates_here * parts * all_rows
-    column, lane = iota((columns, LANES), 0), iota((columns, LANES), 1) % 8
-    wanted = jnp.where(lane < 4, lane, columns - 8 + lane)
-    pick = jnp.where(column == wanted, 1.0, 0.0).astype(BF16)
     cells = scenes_ref[...].reshape(height, columns)
-    cells = jnp.dot(cells, pick, preferred_element_type=F32)
-    row, lane = iota((height, LANES), 0), iota((height, LANES), 1)
-    cells = jnp.where(row % rows == lane // 8, cells, 0.0).astype(BF16)
-    line, row = iota((owners * NOTE, height), 0), iota((owners * NOTE, height), 1) // rows
-    place = line % NOTE
-    wanted = (place % dates_here * parts + place // dates_here) * owners + line // NOTE
-    gather = jnp.where((place < parts * dates_here) & (row == wanted), 1.0, 0.0).astype(BF16)
-    lines = jnp.dot(gather, cells, preferred_element_type=F32)
-    for owner in range(owners):
+    cells = jnp.dot(cells, pick_ref[...], preferred_element_type=F32)
+    cells = cells.reshape(dates_here * parts, all_rows, LANES) * own_ref[...][None]
+    cells = cells.reshape(height, LANES).astype(BF16)
+    lines = jnp.dot(gather_ref[...], cells, preferred_element_type=F32)
+    for owner in range(seams_ref.shape[0]):
         seams_ref[owner] = lines[owner * NOTE : (owner + 1) * NOTE]
-    note_ref[...] = live_ref[...]
-    fetch.wait()
-    note_ref[:2, : dates_ref.shape[1]] = fetched_ref[...].astype(F32)
 
 
 def twin_of(owner, owners):
@@ -125,19 +128,24 @@
         out_specs=IN_VMEM,
         cost_estimate=pl.CostEstimate(flops=10**9, bytes_accessed=10**7, transcendentals=0),
     )()
-    live = pl.pallas_call(
-        functools.partial(live_kernel, pair_dates.shape[1]),
-        out_shape=pltpu.VMEM((NOTE, LANES), F32),
-        in_specs=[IN_SMEM, IN_VMEM],
+    note, pick, own, gather = pl.pallas_call(
+        functools.partial(note_kernel, rows),
+        out_shape=[
+            pltpu.VMEM((NOTE, LANES), F32),
+            pltpu.VMEM((columns, LANES), BF16),
+            pltpu.VMEM((all_rows, LANES), F32),
+            pltpu.VMEM((owners * NOTE, dates_here * parts * all_rows), BF16),
+        ],
+        in_specs=[IN_SMEM, ANYWHERE, IN_VMEM],
+        out_specs=[IN_VMEM] * 4,
+        scratch_shapes=[pltpu.VMEM(pair_dates.shape, jnp.int32), pltpu.SemaphoreType.DMA],
+    )(pair_count, pair_dates, held(blank))
+    seams = pl.pallas_call(
+        seam_kernel,
+        out_shape=pltpu.VMEM((owners, NOTE, LANES), F32),
+        in_specs=[IN_VMEM] * 4,
         out_specs=IN_VMEM,
-    )(pair_count, held(blank))
-    seams, note = pl.pallas_call(
-        seam_kernel,
-        out_shape=[pltpu.VMEM((owners, NOTE, LANES), F32), pltpu.VMEM((NOTE, LANES), F32)],
-        in_specs=[IN_VMEM, ANYWHERE, IN_VMEM],
-        out_specs=[IN_VMEM] * 2,
-        scratch_shapes=[pltpu.VMEM(pair_dates.shape, jnp.int32), pltpu.SemaphoreType.DMA],
-    )(held(scenes), pair_dates, held(live))
+    )(held(scenes), held(pick), held(own), held(gather))
     if rows % 16 == 0:
         blocks = pl.pallas_call(
             cut_kernel,
@@ -395,7 +403,7 @@
 
 def edge_kernel(dates_here, owners, *refs):
     block_ref, seam_ref, others_ref, partial_ref, rest_ref, *refs = refs
-    weights_ref, message_ref, seams_ref, pair_ref = refs
+    weights_ref, *message_refs, seams_ref, pair_ref = refs
     dates = owners * dates_here
     pairs = pair_rows(dates)
     tall = rest_ref.shape[0]
@@ -427,9 +435,16 @@
             for half in range(2):
                 at = half * pairs + unit * count
                 pair_ref[part, at : at + count, :] = bits[half]
+    sums = []
     for part in range(2):
         summed = jnp.dot(weights[part], pair_ref[part], preferred_element_type=F32)
-        message_ref[part * tall : (part + 1) * tall] = summed[:tall] + summed[tall:]
+        sums.append(summed[:tall] + summed[tall:])
+    head = iota((tall, LANES), 1) % 8 < 4
+    to_left = jnp.where(head, sums[0], pltpu.roll(sums[1], 4, 1))
+    to_right = jnp.where(head, pltpu.roll(sums[0], LANES - 4, 1), sums[1])
+    here = lax.rem(lax.axis_index("col"), len(message_refs))
+    for swap, message_ref in enumerate(message_refs):
+        message_ref[...] = jnp.where(here == swap, to_right, to_left)
 
 
 def series_kernel(dates_here, *refs):
@@ -489,38 +504,52 @@
         looked_ref[part] = summed[:tall] + summed[tall:]
 
 
-def finish_kernel(looked_ref, fold_ref, second_ref, first_ref, out_ref, sum_ref):
-    times, parts, half_rows, looks = out_ref.shape
+def finish_kernel(looked_ref, fold_ref, *refs):
+    *message_refs, out_ref, sum_ref, done_ref, semaphores = refs
+    parts, times, half_rows, looks = done_ref.shape
     tall = looked_ref.shape[1]
     pack = LANES // looks
     here, last = lax.axis_index("col"), lax.axis_size("col") - 1
-    even = lax.rem(here, 2) == 0
-    first, second = first_ref[...], second_ref[...]
-    nothing = jnp.zeros_like(first)
-    from_right = jnp.where(here == last, nothing, jnp.where(even, first, second))
-    from_left = jnp.where(here == 0, nothing, jnp.where(even, second, first))
-    edges = jnp.concatenate(halves(jnp.concatenate([from_right, from_left], axis=1)), axis=0)
+    swaps = len(message_refs)
+    from_right = from_left = jnp.zeros((tall, LANES), F32)
+    for swap, message_ref in enumerate(message_refs):
+        message = message_ref[...]
+        from_right = jnp.where((here != last) & (here % swaps == swap), message, from_right)
+        from_left = jnp.where((here != 0) & ((here - 1) % swaps == swap), message, from_left)
+    edges = jnp.concatenate([from_right, from_left], axis=1)
+    head = iota(edges.shape, 1) % 8 < 4
+    edges = [jnp.where(head, edges, 0.0), jnp.where(head, 0.0, edges)]
+    edges = jnp.concatenate(halves(jnp.concatenate(edges, axis=0)), axis=0)
     edges = jnp.dot(edges, fold_ref[...], preferred_element_type=F32)
     edges = edges[: parts * tall] + edges[parts * tall :]
+    sent = []
     for part in range(parts):
         value = looked_ref[part] + edges[part * tall : (part + 1) * tall]
         for half_row in range(half_rows):
             tile, near = half_row // pack, half_row % pack
             one = value[:, tile * LANES : (tile + 1) * LANES]
-            at = (part * half_rows + half_row) * tall
-            sum_ref[at : at + tall, :] = pltpu.roll(one, -near * looks % LANES, 1)
-    for time in range(times):
-        for part in range(parts):
-            rows = sum_ref[pl.ds(part * half_rows * tall + time, half_rows, stride=tall), :]
-            out_ref[time, part] = rows[:, :looks]
-
-
-def column_swap(first, owners, count):
+            at = half_row * tall
+            sum_ref[part, at : at + tall, :] = pltpu.roll(one, -near * looks % LANES, 1)
+        for time in range(times):
+            rows = sum_ref[part, pl.ds(time, half_rows, stride=tall), :]
+            done_ref[part, time] = rows[:, :looks]
+        sent.append(
+            pltpu.make_async_copy(done_ref.at[part], out_ref.at[:, part], semaphores.at[part])
+        )
+        sent[part].start()
+    for copy in sent:
+        copy.wait()
+
+
+def column_swap(swap, swaps, owners, count):
     moves = []
     for owner in range(owners):
         for column in range(count):
-            partner = column + 1 if (column - first) % 2 == 0 else column - 1
-            partner = partner if 0 <= partner < count else column
+            partner = column
+            if column % swaps == swap and column + 1 < count:
+                partner = column + 1
+            elif column and (column - 1) % swaps == swap:
+                partner = column - 1
             moves.append((owner * count + column, twin_of(owner, owners) * count + partner))
     return moves
 
@@ -575,14 +604,15 @@
         scratch_shapes=[pltpu.VMEM((tall, round_up(inverse.shape[1], LANES)), F32)],
         compiler_params=pltpu.CompilerParams(vmem_limit_bytes=40 << 20),
     )(held(comb), held(inverse), *[held(blocks[step]) for step in steps])
-    weights, edge = pl.pallas_call(
+    swaps = min(3, count - 1)
+    weights, *messages = pl.pallas_call(
         functools.partial(edge_kernel, dates_here, owners),
         out_shape=[
             pltpu.VMEM((parts, 2 * tall, 2 * pairs), BF16),
-            pltpu.VMEM((parts * tall, LANES), F32),
+            *[pltpu.VMEM((tall, LANES), F32)] * swaps,
         ],
         in_specs=[IN_VMEM] * 5,
-        out_specs=[IN_VMEM] * 2,
+        out_specs=[IN_VMEM] * (swaps + 1),
         scratch_shapes=[
             pltpu.VMEM((others, parts, GROUP, LANES), F32),
             pltpu.VMEM((parts, 2 * pairs, LANES), BF16),
@@ -606,17 +636,22 @@
         ),
     )(*[held(one) for one in (blocks[1], comb, weights, first_group, first_pairs, other_rows)])
 
-    first = lax.ppermute(edge, ("date", "col"), column_swap(0, owners, count))
-    second = lax.ppermute(edge, ("date", "col"), column_swap(1, owners, count))
+    for swap in range(swaps):
+        moves = column_swap(swap, swaps, owners, count)
+        messages[swap] = held(lax.ppermute(messages[swap], ("date", "col"), moves))
     return pl.pallas_call(
         finish_kernel,
         out_shape=jax.ShapeDtypeStruct(
             (inverse.shape[0], parts, half_rows, columns // 8), F32
         ),
-        in_specs=[IN_VMEM] * 4,
-        out_specs=IN_VMEM,
-        scratch_shapes=[pltpu.VMEM((parts * half_rows * tall, LANES), F32)],
-    )(held(looked), held(fold), held(second), held(first))
+        in_specs=[IN_VMEM] * (swaps + 2),
+        out_specs=ANYWHERE,
+        scratch_shapes=[
+            pltpu.VMEM((parts, half_rows * tall, LANES), F32),
+            pltpu.VMEM((parts, inverse.shape[0], half_rows, columns // 8), F32),
+            pltpu.SemaphoreType.DMA((parts,)),
+        ],
+    )(held(looked), held(fold), *messages)
 
 
 def solution(mesh):

time: 13.9 us -> 13.5 us (0.971)
  the two profiles are of different devices: /device:TPU:17 before, /device:TPU:0 now
where the time goes in v7:
time: 13.5 us; the launch traced here: 13.3 us
  starting transfers between devices  6.99 us (52%)
  Pallas kernels  4.51 us (33%)
  waiting for transfers between devices  1.1 us (8%)
  between operations  0.75 us (6%)
    ppermute x3, starting transfers between devices, per_device(): blocks[step] = lax.ppermute(blocks[step], 'date', moves)  4.45 us
    ppermute x3, starting transfers between devices, per_device(): messages[swap] = held(lax.ppermute(messages[swap], ('date', 'col'), moves))  2.53 us
    pallas_call x1, Pallas kernels, per_device(): pl.pallas_call(functools.partial(series_kernel, dates_here), out_shape=pl...  1.15 us
    ppermute x3, waiting for transfers between devices, per_device(): blocks[step] = lax.ppermute(blocks[step], 'date', moves)  1.08 us
    pallas_call x1, Pallas kernels, per_device(): pl.pallas_call(finish_kernel, out_shape=jax.ShapeDtypeStruct((inverse.sha...  0.91 us
    pallas_call x1, Pallas kernels, per_device(): pl.pallas_call(functools.partial(early_kernel, dates_here), out_shape=[pl...  0.7 us
    pallas_call x1, Pallas kernels, cut(): pl.pallas_call(functools.partial(note_kernel, rows), out_shape=[pltpu.VME...  0.69 us
    pallas_call x1, Pallas kernels, per_device(): pl.pallas_call(functools.partial(edge_kernel, dates_here, owners), out_sh...  0.39 us
  transfers between devices with their start and end apart: 6, of which 2 were waited for; matrix products, arithmetic and copies ran while one was open for 0% of the time, Pallas kernels for 16%

profile of v7, /device:TPU:0, one launch (start us, length us, event | category | flops | bytes accessed | tf_op | source)
XLA Modules:
  0.0 13.3 jit_solution(4222778015701369203)
XLA Ops:
  0.0 0.0 copy-start
  0.7 0.7 %shard_map.47 = (f32[8,128]{1,0:T(8,128)S(1)}, bf16[256,128]{1,0:T(8,128)(2,1)S(1)}, f32[64,128]{1,0:T(8,128)S(1)}, bf16[32,512]{1,0:T(8,128)(2,1)S(1)}) custom-call(s32[1]{0:T(128)S(6)} %copy.5.count_ref, s32[2,24]{1,0:T(2,128)} %bitcast.1, f32[8,128]{1,0:T(8,128)S(1)} %shard_map.46.blank_ref), custom_call_target="tpu_custom_call" | custom-call | tf_op jit(solution)/shard_map/pallas_call | solution.py:131
  1.4 0.0 copy-done
  1.4 0.4 %shard_map.48.seams_ref = f32[4,8,128]{2,1,0:T(8,128)S(1)} custom-call(bf16[4,2,64,256]{3,2,1,0:T(8,128)(2,1)S(1)} %copy-done, bf16[256,128]{1,0:T(8,128)(2,1)S(1)} %get-tuple-element.27.pick_ref, f32[64,128]{1,0:T(8,128)S(1)} %get-tuple-element.28.own_ref, bf16[32,512]{1,0:T(8,128)(2,1)S(1)} %get-tuple-element.29.gather_ref), custom_call_target="tpu_custom_call" | custom-call | tf_op jit(solution)/shard_map/pallas_call | solution.py:143
  1.8 0.1 shard_map.49
  1.8 0.5 %collective-permute-start.1 = (bf16[272,128]{1,0:T(8,128)(2,1)S(1)}, bf16[272,128]{1,0:T(8,128)(2,1)S(1)}, u32[]{:S(2)}, u32[]{:S(2)}) collective-permute-start(bf16[272,128]{1,0:T(8,128)(2,1)S(1)} %get-tuple-element.31), channel_id=1, source_target_pairs={{0,4},{4,8},{8,12},{12,0},{1,5},{5,9},{9,13},{13,1},{2,6},{6,10},{... | collective-permute-start | bytes 208904 | tf_op jit(solution)/shard_map/ppermute | solution.py:569
  2.4 2.6 %collective-permute-start.2 = (bf16[272,128]{1,0:T(8,128)(2,1)S(1)}, bf16[272,128]{1,0:T(8,128)(2,1)S(1)}, u32[]{:S(2)}, u32[]{:S(2)}) collective-permute-start(bf16[272,128]{1,0:T(8,128)(2,1)S(1)} %get-tuple-element.35), channel_id=1, source_target_pairs={{0,8},{4,12},{8,0},{12,4},{1,9},{5,13},{9,1},{13,5},{2,10},{6,14},... | collective-permute-start | bytes 208904 | tf_op jit(solution)/shard_map/ppermute | solution.py:569
  4.9 1.4 %collective-permute-start = (bf16[272,128]{1,0:T(8,128)(2,1)S(1)}, bf16[272,128]{1,0:T(8,128)(2,1)S(1)}, u32[]{:S(2)}, u32[]{:S(2)}) collective-permute-start(bf16[272,128]{1,0:T(8,128)(2,1)S(1)} %get-tuple-element.30), channel_id=1, source_target_pairs={{0,12},{4,0},{8,4},{12,8},{1,13},{5,1},{9,5},{13,9},{2,14},{6,2},{... | collective-permute-start | bytes 208904 | tf_op jit(solution)/shard_map/ppermute | solution.py:569
  6.3 0.0 collective-permute-done.1.refs_0_.refs_2_
  6.3 0.0 copy-start.1
  6.3 0.7 %shard_map.50 = (bf16[256,256]{1,0:T(8,128)(2,1)S(1)}, bf16[256,256]{1,0:T(8,128)(2,1)S(1)}, f32[2,2,8,2,8,128]{5,4,3,2,1,0:T(8,128)S(1)}, bf16[2,2,32,256]{3,2,1,0:T(8,128)(2,1)S(1)}, f32[2,8,128]{2,1,0:T(8,128)S(1)}) custom-call(bf16[272,128]{1,0:T(8,128)(2,1)S(1)} %collective-permute-done.1.refs_0_.refs_2_, ...), custom_call_target="tpu_custom_call" | custom-call | tf_op jit(solution)/shard_map/pallas_call | solution.py:577
  7.0 0.4 %collective-permute-done.2.refs_3_ = bf16[272,128]{1,0:T(8,128)(2,1)S(1)} collective-permute-done((bf16[272,128]{1,0:T(8,128)(2,1)S(1)}, bf16[272,128]{1,0:T(8,128)(2,1)S(1)}, u32[]{:S(2)}, u32[]{:S(2)}) %collective-permute-start.2) | collective-permute-done | bytes 69664 | tf_op jit(solution)/shard_map/ppermute | solution.py:569
  7.4 0.0 copy-done.1
  7.4 0.2 %shard_map.51 = (f32[1,2,2,128,128]{4,3,2,1,0:T(8,128)S(1)}, f32[1,2,8,128]{3,2,1,0:T(8,128)S(1)}, f32[2,16,128]{2,1,0:T(8,128)S(1)}, f32[16,128]{1,0:T(8,128)S(1)}) custom-call(bf16[256,256]{1,0:T(8,128)(2,1)S(1)} %get-tuple-element.33.refs_0_.refs_1_, f32[15,96]{1,0:T(8,128)S(1)} %copy-done.1, bf16[272,128]{1,0:T(8,128)(2,1)S(1)} %collective-permute-done.1.refs_0_.refs_2_, ...), custom_call_target="tpu_custom_call" | custom-call | tf_op jit(solution)/shard_map/pallas_call | solution.py:594
  7.7 0.6 %collective-permute-done.refs_0_ = bf16[272,128]{1,0:T(8,128)(2,1)S(1)} collective-permute-done((bf16[272,128]{1,0:T(8,128)(2,1)S(1)}, bf16[272,128]{1,0:T(8,128)(2,1)S(1)}, u32[]{:S(2)}, u32[]{:S(2)}) %collective-permute-start) | collective-permute-done | bytes 69664 | tf_op jit(solution)/shard_map/ppermute | solution.py:569
  8.3 0.4 %shard_map.52 = (bf16[2,32,256]{2,1,0:T(8,128)(2,1)S(1)}, f32[16,128]{1,0:T(8,128)S(1)}, f32[16,128]{1,0:T(8,128)S(1)}, f32[16,128]{1,0:T(8,128)S(1)}) custom-call(bf16[272,128]{1,0:T(8,128)(2,1)S(1)} %collective-permute-done.refs_0_, f32[2,8,128]{2,1,0:T(8,128)S(1)} %get-tuple-element.34.refs_1_, f32[1,2,8,128]{3,2,1,0:T(8,128)S(1)} %get-tuple-element.36.refs_2_, ...), custom_call_target="tpu_custom_call" | custom-call | tf_op jit(solution)/shard_map/pallas_call | solution.py:608
  8.7 2.0 %collective-permute-start.3 = (f32[16,128]{1,0:T(8,128)S(1)}, f32[16,128]{1,0:T(8,128)S(1)}, u32[]{:S(2)}, u32[]{:S(2)}) collective-permute-start(f32[16,128]{1,0:T(8,128)S(1)} %get-tuple-element.44), channel_id=1, source_target_pairs={{0,5},{1,4},{2,6},{3,7},{4,1},{5,0},{6,2},{7,3},{8,13},{9,12},{10,... | collective-permute-start | bytes 24584 | tf_op jit(solution)/shard_map/ppermute | solution.py:641
  10.7 0.0 collective-permute-start.4
  10.7 0.5 %collective-permute-start.5 = (f32[16,128]{1,0:T(8,128)S(1)}, f32[16,128]{1,0:T(8,128)S(1)}, u32[]{:S(2)}, u32[]{:S(2)}) collective-permute-start(f32[16,128]{1,0:T(8,128)S(1)} %get-tuple-element.46), channel_id=1, source_target_pairs={{0,4},{1,5},{2,7},{3,6},{4,0},{5,1},{6,3},{7,2},{8,12},{9,13},{10,... | collective-permute-start | bytes 24584 | tf_op jit(solution)/shard_map/ppermute | solution.py:641
  11.3 1.1 %shard_map.53.looked_ref = f32[2,16,256]{2,1,0:T(8,128)S(1)} custom-call(bf16[272,128]{1,0:T(8,128)(2,1)S(1)} %collective-permute-done.refs_0_, bf16[256,256]{1,0:T(8,128)(2,1)S(1)} %get-tuple-element.33.refs_0_.refs_1_, bf16[2,32,256]{2,1,0:T(8,128)(2,1)S(1)} %get-tuple-element.39.refs_2_, f32[2,2,8,2,8,128]{5,4,3,2,1,0:T(8,128)S(1)} %get-tuple-element.40.refs_3_, ...), custom_call_target="tpu_custom_call" | custom-call | flops 16777216 | bytes 1048576 | tf_op jit(solution)/shard_map/pallas_call | solution.py:622
  12.4 0.0 collective-permute-done.3.refs_0_
  12.4 0.0 collective-permute-done.4.refs_1_
  12.4 0.0 collective-permute-done.5.refs_2_
  12.4 0.9 %shard_map.54 = f32[15,2,8,32]{3,2,1,0:T(8,128)} custom-call(f32[2,16,256]{2,1,0:T(8,128)S(1)} %shard_map.53.looked_ref, bf16[256,256]{1,0:T(8,128)(2,1)S(1)} %get-tuple-element.43.fold_ref, f32[16,128]{1,0:T(8,128)S(1)} %collective-permute-done.3.refs_0_, f32[16,128]{1,0:T(8,128)S(1)} %collective-permute-done.4.refs_1_, ...), custom_call_target="tpu_custom_call" | custom-call | tf_op jit(solution)/shard_map/pallas_call | solution.py:642
  (1 shorter events, 0.0 us)
Async XLA Ops:
  0.0 1.4 %copy-start = (bf16[4,2,64,256]{3,2,1,0:T(8,128)(2,1)S(1)}, bf16[4,2,64,256]{3,2,1,0:T(8,128)(2,1)}, u32[]{:S(2)}) copy-start(bf16[4,2,64,256]{3,2,1,0:T(8,128)(2,1)} %scenes_ref.3) | copy-start | bytes 786436
  1.8 4.5 %collective-permute-start.1 = (bf16[272,128]{1,0:T(8,128)(2,1)S(1)}, bf16[272,128]{1,0:T(8,128)(2,1)S(1)}, u32[]{:S(2)}, u32[]{:S(2)}) collective-permute-start(bf16[272,128]{1,0:T(8,128)(2,1)S(1)} %get-tuple-element.31), channel_id=1, source_target_pairs={{0,4},{4,8},{8,12},{12,0},{1,5},{5,9},{9,13},{13,1},{2,6},{6,10},{... | collective-permute-start | bytes 208904 | tf_op jit(solution)/shard_map/ppermute | solution.py:569
  2.4 5.1 %collective-permute-start.2 = (bf16[272,128]{1,0:T(8,128)(2,1)S(1)}, bf16[272,128]{1,0:T(8,128)(2,1)S(1)}, u32[]{:S(2)}, u32[]{:S(2)}) collective-permute-start(bf16[272,128]{1,0:T(8,128)(2,1)S(1)} %get-tuple-element.35), channel_id=1, source_target_pairs={{0,8},{4,12},{8,0},{12,4},{1,9},{5,13},{9,1},{13,5},{2,10},{6,14},... | collective-permute-start | bytes 208904 | tf_op jit(solution)/shard_map/ppermute | solution.py:569
  4.9 3.4 %collective-permute-start = (bf16[272,128]{1,0:T(8,128)(2,1)S(1)}, bf16[272,128]{1,0:T(8,128)(2,1)S(1)}, u32[]{:S(2)}, u32[]{:S(2)}) collective-permute-start(bf16[272,128]{1,0:T(8,128)(2,1)S(1)} %get-tuple-element.30), channel_id=1, source_target_pairs={{0,12},{4,0},{8,4},{12,8},{1,13},{5,1},{9,5},{13,9},{2,14},{6,2},{... | collective-permute-start | bytes 208904 | tf_op jit(solution)/shard_map/ppermute | solution.py:569
  6.3 1.1 %copy-start.1 = (f32[15,96]{1,0:T(8,128)S(1)}, f32[15,96]{1,0:T(8,128)}, u32[]{:S(2)}) copy-start(f32[15,96]{1,0:T(8,128)} %refs_1_.1) | copy-start | bytes 17284
  8.7 3.7 %collective-permute-start.3 = (f32[16,128]{1,0:T(8,128)S(1)}, f32[16,128]{1,0:T(8,128)S(1)}, u32[]{:S(2)}, u32[]{:S(2)}) collective-permute-start(f32[16,128]{1,0:T(8,128)S(1)} %get-tuple-element.44), channel_id=1, source_target_pairs={{0,5},{1,4},{2,6},{3,7},{4,1},{5,0},{6,2},{7,3},{8,13},{9,12},{10,... | collective-permute-start | bytes 24584 | tf_op jit(solution)/shard_map/ppermute | solution.py:641
  10.7 1.7 %collective-permute-start.4 = (f32[16,128]{1,0:T(8,128)S(1)}, f32[16,128]{1,0:T(8,128)S(1)}, u32[]{:S(2)}, u32[]{:S(2)}) collective-permute-start(f32[16,128]{1,0:T(8,128)S(1)} %get-tuple-element.45), channel_id=1, source_target_pairs={{0,4},{1,6},{2,5},{3,7},{4,0},{5,2},{6,1},{7,3},{8,12},{9,14},{10,... | collective-permute-start | bytes 24584 | tf_op jit(solution)/shard_map/ppermute | solution.py:641
  10.7 1.7 %collective-permute-start.5 = (f32[16,128]{1,0:T(8,128)S(1)}, f32[16,128]{1,0:T(8,128)S(1)}, u32[]{:S(2)}, u32[]{:S(2)}) collective-permute-start(f32[16,128]{1,0:T(8,128)S(1)} %get-tuple-element.46), channel_id=1, source_target_pairs={{0,4},{1,5},{2,7},{3,6},{4,0},{5,1},{6,3},{7,2},{8,12},{9,13},{10,... | collective-permute-start | bytes 24584 | tf_op jit(solution)/shard_map/ppermute | solution.py:641

commit v8 on v7

--- a/solution.py
+++ b/solution.py
@@ -55,10 +55,7 @@
     return jnp.where(here & (half_row < half_rows), 1.0, 0.0).astype(BF16)
 
 
-def note_kernel(rows, count_ref, dates_ref, blank_ref, *refs):
-    note_ref, pick_ref, own_ref, gather_ref, fetched_ref, semaphore = refs
-    fetch = pltpu.make_async_copy(dates_ref, fetched_ref, semaphore)
-    fetch.start()
+def live_kernel(rows, slots, count_ref, blank_ref, live_ref, pick_ref, own_ref, gather_ref):
     columns, (all_rows, lanes), (lines, height) = pick_ref.shape[0], own_ref.shape, gather_ref.shape
     column, lane = iota((columns, lanes), 0), iota((columns, lanes), 1) % 8
     wanted = jnp.where(lane < 4, lane, columns - 8 + lane)
@@ -70,15 +67,15 @@
     place = line % NOTE
     wanted = (place % (images // 2) * 2 + place // (images // 2)) * owners + line // NOTE
     gather_ref[...] = jnp.where((place < images) & (row == wanted), 1.0, 0.0).astype(BF16)
-    row, lane = iota(note_ref.shape, 0), iota(note_ref.shape, 1)
-    slots = dates_ref.shape[1]
+    row, lane = iota(live_ref.shape, 0), iota(live_ref.shape, 1)
     live = (row == 2) & (lane < jnp.minimum(count_ref[0], slots))
-    note_ref[...] = jnp.where(live, 1.0, blank_ref[...])
-    fetch.wait()
-    note_ref[:2, :slots] = fetched_ref[...].astype(F32)
-
-
-def seam_kernel(scenes_ref, pick_ref, own_ref, gather_ref, seams_ref):
+    live_ref[...] = jnp.where(live, 1.0, blank_ref[...])
+
+
+def seam_kernel(scenes_ref, dates_ref, live_ref, pick_ref, own_ref, gather_ref, *refs):
+    seams_ref, note_ref, fetched_ref, semaphore = refs
+    fetch = pltpu.make_async_copy(dates_ref, fetched_ref, semaphore)
+    fetch.start()
     dates_here, parts, all_rows, columns = scenes_ref.shape
     height = dates_here * parts * all_rows
     cells = scenes_ref[...].reshape(height, columns)
@@ -88,6 +85,9 @@
     lines = jnp.dot(gather_ref[...], cells, preferred_element_type=F32)
     for owner in range(seams_ref.shape[0]):
         seams_ref[owner] = lines[owner * NOTE : (owner + 1) * NOTE]
+    note_ref[...] = live_ref[...]
+    fetch.wait()
+    note_ref[:2, : dates_ref.shape[1]] = fetched_ref[...].astype(F32)
 
 
 def twin_of(owner, owners):
@@ -128,24 +128,24 @@
         out_specs=IN_VMEM,
         cost_estimate=pl.CostEstimate(flops=10**9, bytes_accessed=10**7, transcendentals=0),
     )()
-    note, pick, own, gather = pl.pallas_call(
-        functools.partial(note_kernel, rows),
+    live, *constants = pl.pallas_call(
+        functools.partial(live_kernel, rows, pair_dates.shape[1]),
         out_shape=[
             pltpu.VMEM((NOTE, LANES), F32),
             pltpu.VMEM((columns, LANES), BF16),
             pltpu.VMEM((all_rows, LANES), F32),
             pltpu.VMEM((owners * NOTE, dates_here * parts * all_rows), BF16),
         ],
-        in_specs=[IN_SMEM, ANYWHERE, IN_VMEM],
+        in_specs=[IN_SMEM, IN_VMEM],
         out_specs=[IN_VMEM] * 4,
+    )(pair_count, held(blank))
+    seams, note = pl.pallas_call(
+        seam_kernel,
+        out_shape=[pltpu.VMEM((owners, NOTE, LANES), F32), pltpu.VMEM((NOTE, LANES), F32)],
+        in_specs=[IN_VMEM, ANYWHERE] + [IN_VMEM] * 4,
+        out_specs=[IN_VMEM] * 2,
         scratch_shapes=[pltpu.VMEM(pair_dates.shape, jnp.int32), pltpu.SemaphoreType.DMA],
-    )(pair_count, pair_dates, held(blank))
-    seams = pl.pallas_call(
-        seam_kernel,
-        out_shape=pltpu.VMEM((owners, NOTE, LANES), F32),
-        in_specs=[IN_VMEM] * 4,
-        out_specs=IN_VMEM,
-    )(held(scenes), held(pick), held(own), held(gather))
+    )(held(scenes), pair_dates, held(live), *[held(array) for array in constants])
     if rows % 16 == 0:
         blocks = pl.pallas_call(
             cut_kernel,
@@ -285,48 +285,47 @@
                         store(part, odd, side * pack + near, tile, cells[near])
 
 
-def unit_products(tiles, looks, turns, mine_of, turned_of, store):
+def unit_products(tile, looks, turns, mine_of, turned_of, store):
     lane = iota((GROUP, LANES), 1) % looks
     at_first, at_last = lane == 0, lane == looks - 1
-    for tile in range(tiles):
-
-        def product(place):
-            mine = [[mine_of(part, odd, place, tile) for odd in range(2)] for part in range(2)]
-            values = []
-            for turn in turns:
-                other = [
-                    [turned_of(part, odd, place, tile, turn, mine) for odd in range(2)]
-                    for part in range(2)
-                ]
-                real = (mine[0][0] * other[0][0] + mine[1][0] * other[1][0]) + (
-                    mine[0][1] * other[0][1] + mine[1][1] * other[1][1]
-                )
-                imaginary = (mine[1][0] * other[0][0] - mine[0][0] * other[1][0]) + (
-                    mine[1][1] * other[0][1] - mine[0][1] * other[1][1]
-                )
-                values += [real, imaginary]
-            return values
-
-        def running(places):
-            total = product(places[0])
-            ramp = total
-            for place in places[1:]:
-                total = [one + two for one, two in zip(total, product(place))]
-                share = [0.5 * one for one in total] if place is places[-1] else total
-                ramp = [one + two for one, two in zip(ramp, share)]
-            return total, ramp
-
-        early, to_left = running((0, 1, 2, 3))
-        late, to_right = running((7, 6, 5, 4))
+
+    def product(place):
+        mine = [[mine_of(part, odd, place, tile) for odd in range(2)] for part in range(2)]
         values = []
-        for index in range(len(early)):
-            before = pltpu.roll(to_right[index], 1, 1)
-            after = pltpu.roll(to_left[index], LANES - 1, 1)
-            value = 8.0 * (early[index] + late[index]) - to_left[index] - to_right[index]
-            value = value + jnp.where(at_first, 0.0, before) + jnp.where(at_last, 0.0, after)
-            values.append(value)
-        for part in range(2):
-            store(part, tile, jnp.concatenate(values[part::2], axis=0))
+        for turn in turns:
+            other = [
+                [turned_of(part, odd, place, tile, turn, mine) for odd in range(2)]
+                for part in range(2)
+            ]
+            real = (mine[0][0] * other[0][0] + mine[1][0] * other[1][0]) + (
+                mine[0][1] * other[0][1] + mine[1][1] * other[1][1]
+            )
+            imaginary = (mine[1][0] * other[0][0] - mine[0][0] * other[1][0]) + (
+                mine[1][1] * other[0][1] - mine[0][1] * other[1][1]
+            )
+            values += [real, imaginary]
+        return values
+
+    def running(places):
+        total = product(places[0])
+        ramp = total
+        for place in places[1:]:
+            total = [one + two for one, two in zip(total, product(place))]
+            share = [0.5 * one for one in total] if place is places[-1] else total
+            ramp = [one + two for one, two in zip(ramp, share)]
+        return total, ramp
+
+    early, to_left = running((0, 1, 2, 3))
+    late, to_right = running((7, 6, 5, 4))
+    values = []
+    for index in range(len(early)):
+        before = pltpu.roll(to_right[index], 1, 1)
+        after = pltpu.roll(to_left[index], LANES - 1, 1)
+        value = 8.0 * (early[index] + late[index]) - to_left[index] - to_right[index]
+        value = value + jnp.where(at_first, 0.0, before) + jnp.where(at_last, 0.0, after)
+        values.append(value)
+    for part in range(2):
+        store(part, tile, jnp.concatenate(values[part::2], axis=0))
 
 
 def turn_here(part, odd, place, tile, turn, mine):
@@ -365,14 +364,15 @@
         pair_ref[part, 0, :, across] = high
         pair_ref[part, 1, :, across] = low
 
-    unit_products(
-        tiles,
-        looks,
-        range(1, GROUP // 2 + 1),
-        lambda part, odd, place, tile: ring_ref[part, odd, place, tile],
-        turn_here,
-        store,
-    )
+    for tile in range(tiles):
+        unit_products(
+            tile,
+            looks,
+            range(1, GROUP // 2 + 1),
+            lambda part, odd, place, tile: ring_ref[part, odd, place, tile],
+            turn_here,
+            store,
+        )
 
 
 def place_of(step, owners, dates_here):
@@ -402,14 +402,16 @@
 
 
 def edge_kernel(dates_here, owners, *refs):
-    block_ref, seam_ref, others_ref, partial_ref, rest_ref, *refs = refs
-    weights_ref, *message_refs, seams_ref, pair_ref = refs
+    block_ref, seam_ref, others_ref, partial_ref, rest_ref, comb_ref, other_rows_ref, *refs = refs
+    weights_ref, ring_ref, far_ref, *message_refs, seams_ref, pair_ref, rows_ref = refs
     dates = owners * dates_here
     pairs = pair_rows(dates)
     tall = rest_ref.shape[0]
 
+    group, seat = place_of(1, owners, dates_here)
+    rows_ref[...] = other_rows_ref[...]
+    spread_block(block_ref, comb_ref[...], dates_here, seat, rows_ref.at[group - 1])
     seams_ref[...] = others_ref[...]
-    group, seat = place_of(1, owners, dates_here)
     seam_of(block_ref, dates_here, seat, seams_ref.at[group - 1])
     weights = []
     for part, more in enumerate(slot_weights(block_ref, rest_ref[...], owners, dates_here)):
@@ -435,6 +437,17 @@
             for half in range(2):
                 at = half * pairs + unit * count
                 pair_ref[part, at : at + count, :] = bits[half]
+    looks = comb_ref.shape[0] // 8
+    half_rows = rows_ref.shape[3] // GROUP // 2
+    for group in range(1, dates // GROUP):
+
+        def keep(part, odd, place, tile, cells):
+            ring_ref[group - 1, part, odd, place, tile] = cells
+            for copy in range(2):
+                at = pl.ds(2 * copy * GROUP + odd, GROUP, stride=2)
+                far_ref[group - 1, part, place, tile, at, :] = cells
+
+        pack_group(rows_ref.at[group - 1], looks, half_rows, keep)
     sums = []
     for part in range(2):
         summed = jnp.dot(weights[part], pair_ref[part], preferred_element_type=F32)
@@ -447,61 +460,48 @@
         message_ref[...] = jnp.where(here == swap, to_right, to_left)
 
 
-def series_kernel(dates_here, *refs):
-    *refs, looked_ref, rows_ref, ring_ref, far_ref, pair_ref = refs
-    block_ref, comb_ref, weights_ref, first_ref, first_pair_ref, others_ref = refs
+def series_kernel(looks, *refs):
+    weights_ref, first_ref, first_pair_ref, ring_ref, far_ref, looked_ref, pair_ref = refs
     groups = 1 + ring_ref.shape[0]
     dates = groups * GROUP
     pairs = pair_rows(dates)
-    columns = comb_ref.shape[0]
-    looks = columns // 8
     tiles = ring_ref.shape[4]
-    half_rows = rows_ref.shape[3] // GROUP // 2
     tall = looked_ref.shape[1]
-
-    rows_ref[...] = others_ref[...]
-    last_group, seat = place_of(1, dates // dates_here, dates_here)
-    spread_block(block_ref, comb_ref[...], dates_here, seat, rows_ref.at[last_group - 1])
-    for group in range(1, groups):
-
-        def keep(part, odd, place, tile, cells):
-            ring_ref[group - 1, part, odd, place, tile] = cells
-            for copy in range(2):
-                at = pl.ds(2 * copy * GROUP + odd, GROUP, stride=2)
-                far_ref[group - 1, part, place, tile, at, :] = cells
-
-        pack_group(rows_ref.at[group - 1], looks, half_rows, keep)
 
     for part in range(2):
         for half in range(2):
             at = half * pairs
             pair_ref[part, at : at + first_pair_ref.shape[2], :] = first_pair_ref[part, half]
-    for unit, (low, high, turns) in enumerate(pair_units(dates)):
-        if high == 0:
-            continue
-
-        def mine_of(part, odd, place, tile):
-            if low == 0:
-                return first_ref[part, odd, place, tile]
-            return ring_ref[low - 1, part, odd, place, tile]
-
-        def turn_far(part, odd, place, tile, turn, mine):
-            at = pl.ds(2 * turn + odd, GROUP, stride=2)
-            return far_ref[high - 1, part, place, tile, at, :]
-
-        def store(part, tile, value):
-            count = value.shape[0]
-            across = slice(tile * LANES, (tile + 1) * LANES)
-            bits = halves(value)
-            for half in range(2):
-                at = half * pairs + unit * count
-                pair_ref[part, at : at + count, across] = bits[half]
-
-        turned_of = turn_here if low == high else turn_far
-        unit_products(tiles, looks, turns, mine_of, turned_of, store)
-    for part in range(2):
-        summed = jnp.dot(weights_ref[part], pair_ref[part], preferred_element_type=F32)
-        looked_ref[part] = summed[:tall] + summed[tall:]
+    for tile in range(tiles):
+        for unit, (low, high, turns) in enumerate(pair_units(dates)):
+            if high == 0:
+                continue
+
+            def mine_of(part, odd, place, tile):
+                if low == 0:
+                    return first_ref[part, odd, place, tile]
+                return ring_ref[low - 1, part, odd, place, tile]
+
+            def turn_far(part, odd, place, tile, turn, mine):
+                at = pl.ds(2 * turn + odd, GROUP, stride=2)
+                return far_ref[high - 1, part, place, tile, at, :]
+
+            def store(part, tile, value):
+                count = value.shape[0]
+                across = slice(tile * LANES, (tile + 1) * LANES)
+                bits = halves(value)
+                for half in range(2):
+                    at = half * pairs + unit * count
+                    pair_ref[part, at : at + count, across] = bits[half]
+
+            turned_of = turn_here if low == high else turn_far
+            unit_products(tile, looks, turns, mine_of, turned_of, store)
+        across = slice(tile * LANES, (tile + 1) * LANES)
+        for part in range(2):
+            summed = jnp.dot(
+                weights_ref[part], pair_ref[part, :, across], preferred_element_type=F32
+            )
+            looked_ref[part, :, across] = summed[:tall] + summed[tall:]
 
 
 def finish_kernel(looked_ref, fold_ref, *refs):
@@ -605,36 +605,37 @@
         compiler_params=pltpu.CompilerParams(vmem_limit_bytes=40 << 20),
     )(held(comb), held(inverse), *[held(blocks[step]) for step in steps])
     swaps = min(3, count - 1)
-    weights, *messages = pl.pallas_call(
+    weights, ring, far, *messages = pl.pallas_call(
         functools.partial(edge_kernel, dates_here, owners),
         out_shape=[
             pltpu.VMEM((parts, 2 * tall, 2 * pairs), BF16),
+            pltpu.VMEM((others, parts, 2, 8, tiles, GROUP, LANES), F32),
+            pltpu.VMEM((others, parts, 8, tiles, 4 * GROUP, LANES), F32),
             *[pltpu.VMEM((tall, LANES), F32)] * swaps,
         ],
-        in_specs=[IN_VMEM] * 5,
-        out_specs=[IN_VMEM] * (swaps + 1),
+        in_specs=[IN_VMEM] * 7,
+        out_specs=[IN_VMEM] * (swaps + 3),
         scratch_shapes=[
             pltpu.VMEM((others, parts, GROUP, LANES), F32),
             pltpu.VMEM((parts, 2 * pairs, LANES), BF16),
+            group_rows,
         ],
         compiler_params=pltpu.CompilerParams(vmem_limit_bytes=40 << 20),
-    )(*[held(array) for array in (blocks[1], first_seam, other_seams, partial, rest)])
+    )(
+        *[held(one) for one in (blocks[1], first_seam, other_seams, partial, rest, comb)],
+        held(other_rows),
+    )
     looked = pl.pallas_call(
-        functools.partial(series_kernel, dates_here),
+        functools.partial(series_kernel, looks),
         out_shape=pltpu.VMEM((parts, tall, tiles * LANES), F32),
-        in_specs=[IN_VMEM] * 6,
+        in_specs=[IN_VMEM] * 5,
         out_specs=IN_VMEM,
-        scratch_shapes=[
-            group_rows,
-            pltpu.VMEM((others, parts, 2, 8, tiles, GROUP, LANES), F32),
-            pltpu.VMEM((others, parts, 8, tiles, 4 * GROUP, LANES), F32),
-            pltpu.VMEM((parts, 2 * pairs, tiles * LANES), BF16),
-        ],
+        scratch_shapes=[pltpu.VMEM((parts, 2 * pairs, tiles * LANES), BF16)],
         compiler_params=pltpu.CompilerParams(vmem_limit_bytes=40 << 20),
         cost_estimate=pl.CostEstimate(
             flops=2 * parts * pairs * columns * rows * 8, bytes_accessed=1 << 20, transcendentals=0
         ),
-    )(*[held(one) for one in (blocks[1], comb, weights, first_group, first_pairs, other_rows)])
+    )(*[held(one) for one in (weights, first_group, first_pairs, ring, far)])
 
     for swap in range(swaps):
         moves = column_swap(swap, swaps, owners, count)

time: 13.5 us -> 13.2 us (0.978)
  Pallas kernels: 4.51 us -> 3.85 us
  local copies, waits for them, and re-layouts: 0.01 us -> 0.23 us
    pallas_call x3, Pallas kernels: 2.19 us -> 1.52 us  [the longest x1 0.77 us: per_device(): pl.pallas_call(functools.partial(series_kernel, looks), out_shape=pltpu.V...]
    unnamed x4, local copies, waits for them, and re-layouts: 0.01 us -> 0.23 us
  transfers between devices with their start and end apart: 6 -> 6, of which waited for: 2 -> 3; matrix products, arithmetic and copies ran while one was open for 0% -> 0% of each run, Pallas kernels for 16% -> 13%
where the time goes in v8:
time: 13.2 us; the launch traced here: 13 us
  starting transfers between devices  7.02 us (53%)
  Pallas kernels  3.85 us (29%)
  waiting for transfers between devices  1.16 us (9%)
  between operations  0.74 us (6%)
  local copies, waits for them, and re-layouts  0.23 us (2%)
    ppermute x3, starting transfers between devices, per_device(): blocks[step] = lax.ppermute(blocks[step], 'date', moves)  4.46 us
    ppermute x3, starting transfers between devices, per_device(): messages[swap] = held(lax.ppermute(messages[swap], ('date', 'col'), moves))  2.56 us
    ppermute x3, waiting for transfers between devices, per_device(): blocks[step] = lax.ppermute(blocks[step], 'date', moves)  1.08 us
    pallas_call x1, Pallas kernels, per_device(): pl.pallas_call(finish_kernel, out_shape=jax.ShapeDtypeStruct((inverse.sha...  0.91 us
    pallas_call x1, Pallas kernels, per_device(): pl.pallas_call(functools.partial(series_kernel, looks), out_shape=pltpu.V...  0.77 us
    pallas_call x1, Pallas kernels, cut(): pl.pallas_call(seam_kernel, out_shape=[pltpu.VMEM((owners, NOTE, LANES),...  0.72 us
    pallas_call x1, Pallas kernels, per_device(): pl.pallas_call(functools.partial(early_kernel, dates_here), out_shape=[pl...  0.7 us
    pallas_call x1, Pallas kernels, per_device(): pl.pallas_call(functools.partial(edge_kernel, dates_here, owners), out_sh...  0.4 us
  transfers between devices with their start and end apart: 6, of which 3 were waited for; matrix products, arithmetic and copies ran while one was open for 0% of the time, Pallas kernels for 13%

profile of v8, /device:TPU:0, one launch (start us, length us, event | category | flops | bytes accessed | tf_op | source)
XLA Modules:
  0.0 13.0 jit_solution(15717042301826587308)
XLA Ops:
  0.0 0.0 copy-start
  0.7 0.2 %copy-done = bf16[4,2,64,256]{3,2,1,0:T(8,128)(2,1)S(1)} copy-done((bf16[4,2,64,256]{3,2,1,0:T(8,128)(2,1)S(1)}, bf16[4,2,64,256]{3,2,1,0:T(8,128)(2,1)}, u32[]{:S(2)}) %copy-start) | copy-done | bytes 262168
  1.0 0.7 %shard_map.48 = (f32[4,8,128]{2,1,0:T(8,128)S(1)}, f32[8,128]{1,0:T(8,128)S(1)}) custom-call(bf16[4,2,64,256]{3,2,1,0:T(8,128)(2,1)S(1)} %copy-done, s32[2,24]{1,0:T(2,128)} %bitcast.1, f32[8,128]{1,0:T(8,128)S(1)} %get-tuple-element.30.live_ref, bf16[256,128]{1,0:T(8,128)(2,1)S(1)} %get-tuple-element.31.pick_ref, f32[64,128]{1,0:T(8,128)S(1)} %get-tuple-element.32.own_ref, ...), custom_call_target="tpu_custom_call" | custom-call | tf_op jit(solution)/shard_map/pallas_call | solution.py:142
  1.7 0.1 shard_map.49
  1.8 0.5 %collective-permute-start.1 = (bf16[272,128]{1,0:T(8,128)(2,1)S(1)}, bf16[272,128]{1,0:T(8,128)(2,1)S(1)}, u32[]{:S(2)}, u32[]{:S(2)}) collective-permute-start(bf16[272,128]{1,0:T(8,128)(2,1)S(1)} %get-tuple-element.37), channel_id=1, source_target_pairs={{0,4},{4,8},{8,12},{12,0},{1,5},{5,9},{9,13},{13,1},{2,6},{6,10},{... | collective-permute-start | bytes 208904 | tf_op jit(solution)/shard_map/ppermute | solution.py:569
  2.3 2.6 %collective-permute-start.2 = (bf16[272,128]{1,0:T(8,128)(2,1)S(1)}, bf16[272,128]{1,0:T(8,128)(2,1)S(1)}, u32[]{:S(2)}, u32[]{:S(2)}) collective-permute-start(bf16[272,128]{1,0:T(8,128)(2,1)S(1)} %get-tuple-element.41), channel_id=1, source_target_pairs={{0,8},{4,12},{8,0},{12,4},{1,9},{5,13},{9,1},{13,5},{2,10},{6,14},... | collective-permute-start | bytes 208904 | tf_op jit(solution)/shard_map/ppermute | solution.py:569
  4.8 1.4 %collective-permute-start = (bf16[272,128]{1,0:T(8,128)(2,1)S(1)}, bf16[272,128]{1,0:T(8,128)(2,1)S(1)}, u32[]{:S(2)}, u32[]{:S(2)}) collective-permute-start(bf16[272,128]{1,0:T(8,128)(2,1)S(1)} %get-tuple-element.36), channel_id=1, source_target_pairs={{0,12},{4,0},{8,4},{12,8},{1,13},{5,1},{9,5},{13,9},{2,14},{6,2},{... | collective-permute-start | bytes 208904 | tf_op jit(solution)/shard_map/ppermute | solution.py:569
  6.2 0.0 collective-permute-done.1.refs_0_.refs_2_
  6.2 0.0 copy-start.1
  6.2 0.7 %shard_map.50 = (bf16[256,256]{1,0:T(8,128)(2,1)S(1)}, bf16[256,256]{1,0:T(8,128)(2,1)S(1)}, f32[2,2,8,2,8,128]{5,4,3,2,1,0:T(8,128)S(1)}, bf16[2,2,32,256]{3,2,1,0:T(8,128)(2,1)S(1)}, f32[2,8,128]{2,1,0:T(8,128)S(1)}) custom-call(bf16[272,128]{1,0:T(8,128)(2,1)S(1)} %collective-permute-done.1.refs_0_.refs_2_, ...), custom_call_target="tpu_custom_call" | custom-call | tf_op jit(solution)/shard_map/pallas_call | solution.py:577
  6.9 0.4 %collective-permute-done.2.refs_3_ = bf16[272,128]{1,0:T(8,128)(2,1)S(1)} collective-permute-done((bf16[272,128]{1,0:T(8,128)(2,1)S(1)}, bf16[272,128]{1,0:T(8,128)(2,1)S(1)}, u32[]{:S(2)}, u32[]{:S(2)}) %collective-permute-start.2) | collective-permute-done | bytes 69664 | tf_op jit(solution)/shard_map/ppermute | solution.py:569
  7.4 0.0 copy-done.1
  7.4 0.2 %shard_map.51 = (f32[1,2,2,128,128]{4,3,2,1,0:T(8,128)S(1)}, f32[1,2,8,128]{3,2,1,0:T(8,128)S(1)}, f32[2,16,128]{2,1,0:T(8,128)S(1)}, f32[16,128]{1,0:T(8,128)S(1)}) custom-call(bf16[256,256]{1,0:T(8,128)(2,1)S(1)} %get-tuple-element.40.refs_0_.refs_5_, f32[15,96]{1,0:T(8,128)S(1)} %copy-done.1, bf16[272,128]{1,0:T(8,128)(2,1)S(1)} %collective-permute-done.1.refs_0_.refs_2_, ...), custom_call_target="tpu_custom_call" | custom-call | tf_op jit(solution)/shard_map/pallas_call | solution.py:594
  7.6 0.6 %collective-permute-done.refs_0_ = bf16[272,128]{1,0:T(8,128)(2,1)S(1)} collective-permute-done((bf16[272,128]{1,0:T(8,128)(2,1)S(1)}, bf16[272,128]{1,0:T(8,128)(2,1)S(1)}, u32[]{:S(2)}, u32[]{:S(2)}) %collective-permute-start) | collective-permute-done | bytes 69664 | tf_op jit(solution)/shard_map/ppermute | solution.py:569
  8.3 0.4 %shard_map.52 = (bf16[2,32,256]{2,1,0:T(8,128)(2,1)S(1)}, f32[1,2,2,8,2,8,128]{6,5,4,3,2,1,0:T(8,128)S(1)}, f32[1,2,8,2,32,128]{5,4,3,2,1,0:T(8,128)S(1)}, f32[1...) custom-call(bf16[272,128]{1,0:T(8,128)(2,1)S(1)} %collective-permute-done.refs_0_, ...), custom_call_target="tpu_custom_call" | custom-call | tf_op jit(solution)/shard_map/pallas_call | solution.py:608
  8.7 2.1 %collective-permute-start.3 = (f32[16,128]{1,0:T(8,128)S(1)}, f32[16,128]{1,0:T(8,128)S(1)}, u32[]{:S(2)}, u32[]{:S(2)}) collective-permute-start(f32[16,128]{1,0:T(8,128)S(1)} %get-tuple-element.52), channel_id=1, source_target_pairs={{0,5},{1,4},{2,6},{3,7},{4,1},{5,0},{6,2},{7,3},{8,13},{9,12},{10,... | collective-permute-start | bytes 24584 | tf_op jit(solution)/shard_map/ppermute | solution.py:642
  10.7 0.0 collective-permute-start.4
  10.7 0.5 %collective-permute-start.5 = (f32[16,128]{1,0:T(8,128)S(1)}, f32[16,128]{1,0:T(8,128)S(1)}, u32[]{:S(2)}, u32[]{:S(2)}) collective-permute-start(f32[16,128]{1,0:T(8,128)S(1)} %get-tuple-element.54), channel_id=1, source_target_pairs={{0,4},{1,5},{2,7},{3,6},{4,0},{5,1},{6,3},{7,2},{8,12},{9,13},{10,... | collective-permute-start | bytes 24584 | tf_op jit(solution)/shard_map/ppermute | solution.py:642
  11.2 0.8 %shard_map.53.looked_ref = f32[2,16,256]{2,1,0:T(8,128)S(1)} custom-call(bf16[2,32,256]{2,1,0:T(8,128)(2,1)S(1)} %get-tuple-element.46.refs_0_, f32[2,2,8,2,8,128]{5,4,3,2,1,0:T(8,128)S(1)} %get-tuple-element.47.refs_1_, bf16[2,2,32,256]{3,2,1,0:T(8,128)(2,1)S(1)} %get-tuple-element.48.refs_2_, f32[1,2,2,8,2,8,128]{6,5,4,3,2,1,0:T(8,128)S(1)} %get-tuple-element.49.refs_3_, ...), custom_call_target="tpu_custom_call" | custom-call | flops 16777216 | bytes 1048576 | tf_op jit(solution)/shard_map/pallas_call | solution.py:628
  12.0 0.1 collective-permute-done.3.refs_0_
  12.1 0.0 collective-permute-done.4.refs_1_
  12.1 0.0 collective-permute-done.5.refs_2_
  12.1 0.9 %shard_map.54 = f32[15,2,8,32]{3,2,1,0:T(8,128)} custom-call(f32[2,16,256]{2,1,0:T(8,128)S(1)} %shard_map.53.looked_ref, bf16[256,256]{1,0:T(8,128)(2,1)S(1)} %get-tuple-element.51.fold_ref, f32[16,128]{1,0:T(8,128)S(1)} %collective-permute-done.3.refs_0_, f32[16,128]{1,0:T(8,128)S(1)} %collective-permute-done.4.refs_1_, ...), custom_call_target="tpu_custom_call" | custom-call | tf_op jit(solution)/shard_map/pallas_call | solution.py:643
  (2 shorter events, 0.0 us)
Async XLA Ops:
  0.0 1.0 %copy-start = (bf16[4,2,64,256]{3,2,1,0:T(8,128)(2,1)S(1)}, bf16[4,2,64,256]{3,2,1,0:T(8,128)(2,1)}, u32[]{:S(2)}) copy-start(bf16[4,2,64,256]{3,2,1,0:T(8,128)(2,1)} %scenes_ref.3) | copy-start | bytes 786436
  1.8 4.5 %collective-permute-start.1 = (bf16[272,128]{1,0:T(8,128)(2,1)S(1)}, bf16[272,128]{1,0:T(8,128)(2,1)S(1)}, u32[]{:S(2)}, u32[]{:S(2)}) collective-permute-start(bf16[272,128]{1,0:T(8,128)(2,1)S(1)} %get-tuple-element.37), channel_id=1, source_target_pairs={{0,4},{4,8},{8,12},{12,0},{1,5},{5,9},{9,13},{13,1},{2,6},{6,10},{... | collective-permute-start | bytes 208904 | tf_op jit(solution)/shard_map/ppermute | solution.py:569
  2.3 5.1 %collective-permute-start.2 = (bf16[272,128]{1,0:T(8,128)(2,1)S(1)}, bf16[272,128]{1,0:T(8,128)(2,1)S(1)}, u32[]{:S(2)}, u32[]{:S(2)}) collective-permute-start(bf16[272,128]{1,0:T(8,128)(2,1)S(1)} %get-tuple-element.41), channel_id=1, source_target_pairs={{0,8},{4,12},{8,0},{12,4},{1,9},{5,13},{9,1},{13,5},{2,10},{6,14},... | collective-permute-start | bytes 208904 | tf_op jit(solution)/shard_map/ppermute | solution.py:569
  4.8 3.4 %collective-permute-start = (bf16[272,128]{1,0:T(8,128)(2,1)S(1)}, bf16[272,128]{1,0:T(8,128)(2,1)S(1)}, u32[]{:S(2)}, u32[]{:S(2)}) collective-permute-start(bf16[272,128]{1,0:T(8,128)(2,1)S(1)} %get-tuple-element.36), channel_id=1, source_target_pairs={{0,12},{4,0},{8,4},{12,8},{1,13},{5,1},{9,5},{13,9},{2,14},{6,2},{... | collective-permute-start | bytes 208904 | tf_op jit(solution)/shard_map/ppermute | solution.py:569
  6.2 1.1 %copy-start.1 = (f32[15,96]{1,0:T(8,128)S(1)}, f32[15,96]{1,0:T(8,128)}, u32[]{:S(2)}) copy-start(f32[15,96]{1,0:T(8,128)} %refs_1_.1) | copy-start | bytes 17284
  8.7 3.4 %collective-permute-start.3 = (f32[16,128]{1,0:T(8,128)S(1)}, f32[16,128]{1,0:T(8,128)S(1)}, u32[]{:S(2)}, u32[]{:S(2)}) collective-permute-start(f32[16,128]{1,0:T(8,128)S(1)} %get-tuple-element.52), channel_id=1, source_target_pairs={{0,5},{1,4},{2,6},{3,7},{4,1},{5,0},{6,2},{7,3},{8,13},{9,12},{10,... | collective-permute-start | bytes 24584 | tf_op jit(solution)/shard_map/ppermute | solution.py:642
  10.7 1.4 %collective-permute-start.4 = (f32[16,128]{1,0:T(8,128)S(1)}, f32[16,128]{1,0:T(8,128)S(1)}, u32[]{:S(2)}, u32[]{:S(2)}) collective-permute-start(f32[16,128]{1,0:T(8,128)S(1)} %get-tuple-element.53), channel_id=1, source_target_pairs={{0,4},{1,6},{2,5},{3,7},{4,0},{5,2},{6,1},{7,3},{8,12},{9,14},{10,... | collective-permute-start | bytes 24584 | tf_op jit(solution)/shard_map/ppermute | solution.py:642
  10.7 1.4 %collective-permute-start.5 = (f32[16,128]{1,0:T(8,128)S(1)}, f32[16,128]{1,0:T(8,128)S(1)}, u32[]{:S(2)}, u32[]{:S(2)}) collective-permute-start(f32[16,128]{1,0:T(8,128)S(1)} %get-tuple-element.54), channel_id=1, source_target_pairs={{0,4},{1,5},{2,7},{3,6},{4,0},{5,1},{6,3},{7,2},{8,12},{9,13},{10,... | collective-permute-start | bytes 24584 | tf_op jit(solution)/shard_map/ppermute | solution.py:642

commit v9 on v8

--- a/solution.py
+++ b/solution.py
@@ -73,7 +73,7 @@
 
 
 def seam_kernel(scenes_ref, dates_ref, live_ref, pick_ref, own_ref, gather_ref, *refs):
-    seams_ref, note_ref, fetched_ref, semaphore = refs
+    *block_refs, seams_ref, note_ref, fetched_ref, semaphore = refs
     fetch = pltpu.make_async_copy(dates_ref, fetched_ref, semaphore)
     fetch.start()
     dates_here, parts, all_rows, columns = scenes_ref.shape
@@ -86,28 +86,29 @@
     for owner in range(seams_ref.shape[0]):
         seams_ref[owner] = lines[owner * NOTE : (owner + 1) * NOTE]
     note_ref[...] = live_ref[...]
+    owners = seams_ref.shape[0]
+    for step, block_ref in enumerate(block_refs):
+        cut_block(scenes_ref, owners, step, block_ref)
     fetch.wait()
     note_ref[:2, : dates_ref.shape[1]] = fetched_ref[...].astype(F32)
+    for step, block_ref in enumerate(block_refs):
+        owner = lax.rem(lax.axis_index("date") + owners - step, owners)
+        tile = jnp.concatenate([note_ref[...], seams_ref[twin_of(owner, owners)]], axis=0)
+        block_ref[block_ref.shape[0] - NOTE_ROWS :] = tile.astype(BF16)
 
 
 def twin_of(owner, owners):
     return owner + 1 - 2 * (owner % 2) if owners % 2 == 0 else owner
 
 
-def cut_kernel(scenes_ref, note_ref, seams_ref, *block_refs):
-    owners = len(block_refs)
-    me = lax.axis_index("date")
-    rows = scenes_ref.shape[2] // owners
-    sides = scenes_ref.shape[3] // LANES
-    for step, block_ref in enumerate(block_refs):
-        owner = lax.rem(me + owners - step, owners)
-        first = pl.multiple_of(owner * rows, rows)
-        height = (block_ref.shape[0] - NOTE_ROWS) // sides
-        for side in range(sides):
-            cells = scenes_ref[:, :, pl.ds(first, rows), side * LANES : (side + 1) * LANES]
-            block_ref[side * height : (side + 1) * height] = cells.reshape(height, LANES)
-        seam = seams_ref[twin_of(owner, owners)]
-        block_ref[sides * height :] = jnp.concatenate([note_ref[...], seam], axis=0).astype(BF16)
+def cut_block(scenes_ref, owners, step, block_ref):
+    dates_here, parts, all_rows, columns = scenes_ref.shape
+    rows = all_rows // owners
+    first = pl.multiple_of(lax.rem(lax.axis_index("date") + owners - step, owners) * rows, rows)
+    height = dates_here * parts * rows
+    for side in range(columns // LANES):
+        cells = scenes_ref[:, :, pl.ds(first, rows), side * LANES : (side + 1) * LANES]
+        block_ref[side * height : (side + 1) * height] = cells.reshape(height, LANES)
 
 
 def cells_of(block_ref, sides):
@@ -139,24 +140,27 @@
         in_specs=[IN_SMEM, IN_VMEM],
         out_specs=[IN_VMEM] * 4,
     )(pair_count, held(blank))
-    seams, note = pl.pallas_call(
+    aligned = rows % 16 == 0
+    lines = [pltpu.VMEM((owners, NOTE, LANES), F32), pltpu.VMEM((NOTE, LANES), F32)]
+    blocks = pl.pallas_call(
         seam_kernel,
-        out_shape=[pltpu.VMEM((owners, NOTE, LANES), F32), pltpu.VMEM((NOTE, LANES), F32)],
+        out_shape=[pltpu.VMEM((sides * height + NOTE_ROWS, LANES), BF16)] * owners
+        if aligned
+        else lines,
         in_specs=[IN_VMEM, ANYWHERE] + [IN_VMEM] * 4,
-        out_specs=[IN_VMEM] * 2,
-        scratch_shapes=[pltpu.VMEM(pair_dates.shape, jnp.int32), pltpu.SemaphoreType.DMA],
+        out_specs=[IN_VMEM] * (owners if aligned else 2),
+        scratch_shapes=[
+            *(lines if aligned else []),
+            pltpu.VMEM(pair_dates.shape, jnp.int32),
+            pltpu.SemaphoreType.DMA,
+        ],
     )(held(scenes), pair_dates, held(live), *[held(array) for array in constants])
-    if rows % 16 == 0:
-        blocks = pl.pallas_call(
-            cut_kernel,
-            out_shape=[pltpu.VMEM((sides * height + NOTE_ROWS, LANES), BF16)] * owners,
-            in_specs=[IN_VMEM] * 3,
-            out_specs=[IN_VMEM] * owners,
-        )(held(scenes), held(note), held(seams))
+    if aligned:
         return list(blocks)
+    seams, note = blocks
+    blocks = []
     me = lax.axis_index("date")
     apart = scenes.reshape(dates_here * parts, owners, rows, columns)
-    blocks = []
     for step in range(owners):
         owner = lax.rem(me + owners - step, owners)
         cells = lax.dynamic_index_in_dim(apart, owner, 1, False).reshape(height, columns)

time: 13.2 us -> 13.1 us (level)
    pallas_call x2 -> x1, Pallas kernels: 0.79 us -> 0.7 us  [cut(): pl.pallas_call(seam_kernel, out_shape=[pltpu.VMEM((sides * height + NOTE_...]
where the time goes in v9:
time: 13.1 us; the launch traced here: 12.9 us
  starting transfers between devices  7.02 us (54%)
  Pallas kernels  3.76 us (29%)
  waiting for transfers between devices  1.16 us (9%)
  between operations  0.73 us (6%)
  local copies, waits for them, and re-layouts  0.23 us (2%)
    ppermute x3, starting transfers between devices, per_device(): blocks[step] = lax.ppermute(blocks[step], 'date', moves)  4.46 us
    ppermute x3, starting transfers between devices, per_device(): messages[swap] = held(lax.ppermute(messages[swap], ('date', 'col'), moves))  2.57 us
    ppermute x3, waiting for transfers between devices, per_device(): blocks[step] = lax.ppermute(blocks[step], 'date', moves)  1.08 us
    pallas_call x1, Pallas kernels, per_device(): pl.pallas_call(finish_kernel, out_shape=jax.ShapeDtypeStruct((inverse.sha...  0.91 us
    pallas_call x1, Pallas kernels, per_device(): pl.pallas_call(functools.partial(series_kernel, looks), out_shape=pltpu.V...  0.77 us
    pallas_call x1, Pallas kernels, cut(): pl.pallas_call(seam_kernel, out_shape=[pltpu.VMEM((sides * height + NOTE_...  0.7 us
    pallas_call x1, Pallas kernels, per_device(): pl.pallas_call(functools.partial(early_kernel, dates_here), out_shape=[pl...  0.7 us
    pallas_call x1, Pallas kernels, per_device(): pl.pallas_call(functools.partial(edge_kernel, dates_here, owners), out_sh...  0.4 us
  transfers between devices with their start and end apart: 6, of which 3 were waited for; matrix products, arithmetic and copies ran while one was open for 0% of the time, Pallas kernels for 13%

profile of v9, /device:TPU:0, one launch (start us, length us, event | category | flops | bytes accessed | tf_op | source)
XLA Modules:
  0.0 12.9 jit_solution(4805384130538554789)
XLA Ops:
  0.0 0.0 copy-start
  0.7 0.2 %copy-done = bf16[4,2,64,256]{3,2,1,0:T(8,128)(2,1)S(1)} copy-done((bf16[4,2,64,256]{3,2,1,0:T(8,128)(2,1)S(1)}, bf16[4,2,64,256]{3,2,1,0:T(8,128)(2,1)}, u32[]{:S(2)}) %copy-start) | copy-done | bytes 262168
  1.0 0.7 %shard_map.48 = (bf16[272,128]{1,0:T(8,128)(2,1)S(1)}, bf16[272,128]{1,0:T(8,128)(2,1)S(1)}, bf16[272,128]{1,0:T(8,128)(2,1)S(1)}, bf16[272,128]{1,0:T(8,128)(2,1)S(1)}) custom-call(bf16[4,2,64,256]{3,2,1,0:T(8,128)(2,1)S(1)} %copy-done, s32[2,24]{1,0:T(2,128)} %bitcast.1, f32[8,128]{1,0:T(8,128)S(1)} %get-tuple-element.28.live_ref, ...), custom_call_target="tpu_custom_call" | custom-call | tf_op jit(solution)/shard_map/pallas_call | solution.py:145
  1.7 0.5 %collective-permute-start.1 = (bf16[272,128]{1,0:T(8,128)(2,1)S(1)}, bf16[272,128]{1,0:T(8,128)(2,1)S(1)}, u32[]{:S(2)}, u32[]{:S(2)}) collective-permute-start(bf16[272,128]{1,0:T(8,128)(2,1)S(1)} %get-tuple-element.33), channel_id=1, source_target_pairs={{0,4},{4,8},{8,12},{12,0},{1,5},{5,9},{9,13},{13,1},{2,6},{6,10},{... | collective-permute-start | bytes 208904 | tf_op jit(solution)/shard_map/ppermute | solution.py:573
  2.2 2.6 %collective-permute-start.2 = (bf16[272,128]{1,0:T(8,128)(2,1)S(1)}, bf16[272,128]{1,0:T(8,128)(2,1)S(1)}, u32[]{:S(2)}, u32[]{:S(2)}) collective-permute-start(bf16[272,128]{1,0:T(8,128)(2,1)S(1)} %get-tuple-element.37), channel_id=1, source_target_pairs={{0,8},{4,12},{8,0},{12,4},{1,9},{5,13},{9,1},{13,5},{2,10},{6,14},... | collective-permute-start | bytes 208904 | tf_op jit(solution)/shard_map/ppermute | solution.py:573
  4.7 1.4 %collective-permute-start = (bf16[272,128]{1,0:T(8,128)(2,1)S(1)}, bf16[272,128]{1,0:T(8,128)(2,1)S(1)}, u32[]{:S(2)}, u32[]{:S(2)}) collective-permute-start(bf16[272,128]{1,0:T(8,128)(2,1)S(1)} %get-tuple-element.32), channel_id=1, source_target_pairs={{0,12},{4,0},{8,4},{12,8},{1,13},{5,1},{9,5},{13,9},{2,14},{6,2},{... | collective-permute-start | bytes 208904 | tf_op jit(solution)/shard_map/ppermute | solution.py:573
  6.1 0.0 collective-permute-done.1.refs_0_.refs_2_
  6.1 0.0 copy-start.1
  6.1 0.7 %shard_map.49 = (bf16[256,256]{1,0:T(8,128)(2,1)S(1)}, bf16[256,256]{1,0:T(8,128)(2,1)S(1)}, f32[2,2,8,2,8,128]{5,4,3,2,1,0:T(8,128)S(1)}, bf16[2,2,32,256]{3,2,1,0:T(8,128)(2,1)S(1)}, f32[2,8,128]{2,1,0:T(8,128)S(1)}) custom-call(bf16[272,128]{1,0:T(8,128)(2,1)S(1)} %collective-permute-done.1.refs_0_.refs_2_, ...), custom_call_target="tpu_custom_call" | custom-call | tf_op jit(solution)/shard_map/pallas_call | solution.py:581
  6.8 0.4 %collective-permute-done.2.refs_3_ = bf16[272,128]{1,0:T(8,128)(2,1)S(1)} collective-permute-done((bf16[272,128]{1,0:T(8,128)(2,1)S(1)}, bf16[272,128]{1,0:T(8,128)(2,1)S(1)}, u32[]{:S(2)}, u32[]{:S(2)}) %collective-permute-start.2) | collective-permute-done | bytes 69664 | tf_op jit(solution)/shard_map/ppermute | solution.py:573
  7.3 0.0 copy-done.1
  7.3 0.2 %shard_map.50 = (f32[1,2,2,128,128]{4,3,2,1,0:T(8,128)S(1)}, f32[1,2,8,128]{3,2,1,0:T(8,128)S(1)}, f32[2,16,128]{2,1,0:T(8,128)S(1)}, f32[16,128]{1,0:T(8,128)S(1)}) custom-call(bf16[256,256]{1,0:T(8,128)(2,1)S(1)} %get-tuple-element.36.refs_0_.refs_5_, f32[15,96]{1,0:T(8,128)S(1)} %copy-done.1, bf16[272,128]{1,0:T(8,128)(2,1)S(1)} %collective-permute-done.1.refs_0_.refs_2_, ...), custom_call_target="tpu_custom_call" | custom-call | tf_op jit(solution)/shard_map/pallas_call | solution.py:598
  7.5 0.6 %collective-permute-done.refs_0_ = bf16[272,128]{1,0:T(8,128)(2,1)S(1)} collective-permute-done((bf16[272,128]{1,0:T(8,128)(2,1)S(1)}, bf16[272,128]{1,0:T(8,128)(2,1)S(1)}, u32[]{:S(2)}, u32[]{:S(2)}) %collective-permute-start) | collective-permute-done | bytes 69664 | tf_op jit(solution)/shard_map/ppermute | solution.py:573
  8.2 0.4 %shard_map.51 = (bf16[2,32,256]{2,1,0:T(8,128)(2,1)S(1)}, f32[1,2,2,8,2,8,128]{6,5,4,3,2,1,0:T(8,128)S(1)}, f32[1,2,8,2,32,128]{5,4,3,2,1,0:T(8,128)S(1)}, f32[1...) custom-call(bf16[272,128]{1,0:T(8,128)(2,1)S(1)} %collective-permute-done.refs_0_, ...), custom_call_target="tpu_custom_call" | custom-call | tf_op jit(solution)/shard_map/pallas_call | solution.py:612
  8.6 2.1 %collective-permute-start.3 = (f32[16,128]{1,0:T(8,128)S(1)}, f32[16,128]{1,0:T(8,128)S(1)}, u32[]{:S(2)}, u32[]{:S(2)}) collective-permute-start(f32[16,128]{1,0:T(8,128)S(1)} %get-tuple-element.48), channel_id=1, source_target_pairs={{0,5},{1,4},{2,6},{3,7},{4,1},{5,0},{6,2},{7,3},{8,13},{9,12},{10,... | collective-permute-start | bytes 24584 | tf_op jit(solution)/shard_map/ppermute | solution.py:646
  10.6 0.0 collective-permute-start.4
  10.6 0.5 %collective-permute-start.5 = (f32[16,128]{1,0:T(8,128)S(1)}, f32[16,128]{1,0:T(8,128)S(1)}, u32[]{:S(2)}, u32[]{:S(2)}) collective-permute-start(f32[16,128]{1,0:T(8,128)S(1)} %get-tuple-element.50), channel_id=1, source_target_pairs={{0,4},{1,5},{2,7},{3,6},{4,0},{5,1},{6,3},{7,2},{8,12},{9,13},{10,... | collective-permute-start | bytes 24584 | tf_op jit(solution)/shard_map/ppermute | solution.py:646
  11.1 0.8 %shard_map.52.looked_ref = f32[2,16,256]{2,1,0:T(8,128)S(1)} custom-call(bf16[2,32,256]{2,1,0:T(8,128)(2,1)S(1)} %get-tuple-element.42.refs_0_, f32[2,2,8,2,8,128]{5,4,3,2,1,0:T(8,128)S(1)} %get-tuple-element.43.refs_1_, bf16[2,2,32,256]{3,2,1,0:T(8,128)(2,1)S(1)} %get-tuple-element.44.refs_2_, f32[1,2,2,8,2,8,128]{6,5,4,3,2,1,0:T(8,128)S(1)} %get-tuple-element.45.refs_3_, ...), custom_call_target="tpu_custom_call" | custom-call | flops 16777216 | bytes 1048576 | tf_op jit(solution)/shard_map/pallas_call | solution.py:632
  11.9 0.1 collective-permute-done.3.refs_0_
  12.0 0.0 collective-permute-done.4.refs_1_
  12.0 0.0 collective-permute-done.5.refs_2_
  12.0 0.9 %shard_map.53 = f32[15,2,8,32]{3,2,1,0:T(8,128)} custom-call(f32[2,16,256]{2,1,0:T(8,128)S(1)} %shard_map.52.looked_ref, bf16[256,256]{1,0:T(8,128)(2,1)S(1)} %get-tuple-element.47.fold_ref, f32[16,128]{1,0:T(8,128)S(1)} %collective-permute-done.3.refs_0_, f32[16,128]{1,0:T(8,128)S(1)} %collective-permute-done.4.refs_1_, ...), custom_call_target="tpu_custom_call" | custom-call | tf_op jit(solution)/shard_map/pallas_call | solution.py:647
  (2 shorter events, 0.0 us)
Async XLA Ops:
  0.0 1.0 %copy-start = (bf16[4,2,64,256]{3,2,1,0:T(8,128)(2,1)S(1)}, bf16[4,2,64,256]{3,2,1,0:T(8,128)(2,1)}, u32[]{:S(2)}) copy-start(bf16[4,2,64,256]{3,2,1,0:T(8,128)(2,1)} %scenes_ref.1) | copy-start | bytes 786436
  1.7 4.5 %collective-permute-start.1 = (bf16[272,128]{1,0:T(8,128)(2,1)S(1)}, bf16[272,128]{1,0:T(8,128)(2,1)S(1)}, u32[]{:S(2)}, u32[]{:S(2)}) collective-permute-start(bf16[272,128]{1,0:T(8,128)(2,1)S(1)} %get-tuple-element.33), channel_id=1, source_target_pairs={{0,4},{4,8},{8,12},{12,0},{1,5},{5,9},{9,13},{13,1},{2,6},{6,10},{... | collective-permute-start | bytes 208904 | tf_op jit(solution)/shard_map/ppermute | solution.py:573
  2.2 5.1 %collective-permute-start.2 = (bf16[272,128]{1,0:T(8,128)(2,1)S(1)}, bf16[272,128]{1,0:T(8,128)(2,1)S(1)}, u32[]{:S(2)}, u32[]{:S(2)}) collective-permute-start(bf16[272,128]{1,0:T(8,128)(2,1)S(1)} %get-tuple-element.37), channel_id=1, source_target_pairs={{0,8},{4,12},{8,0},{12,4},{1,9},{5,13},{9,1},{13,5},{2,10},{6,14},... | collective-permute-start | bytes 208904 | tf_op jit(solution)/shard_map/ppermute | solution.py:573
  4.7 3.4 %collective-permute-start = (bf16[272,128]{1,0:T(8,128)(2,1)S(1)}, bf16[272,128]{1,0:T(8,128)(2,1)S(1)}, u32[]{:S(2)}, u32[]{:S(2)}) collective-permute-start(bf16[272,128]{1,0:T(8,128)(2,1)S(1)} %get-tuple-element.32), channel_id=1, source_target_pairs={{0,12},{4,0},{8,4},{12,8},{1,13},{5,1},{9,5},{13,9},{2,14},{6,2},{... | collective-permute-start | bytes 208904 | tf_op jit(solution)/shard_map/ppermute | solution.py:573
  6.1 1.1 %copy-start.1 = (f32[15,96]{1,0:T(8,128)S(1)}, f32[15,96]{1,0:T(8,128)}, u32[]{:S(2)}) copy-start(f32[15,96]{1,0:T(8,128)} %refs_1_.1) | copy-start | bytes 17284
  8.6 3.4 %collective-permute-start.3 = (f32[16,128]{1,0:T(8,128)S(1)}, f32[16,128]{1,0:T(8,128)S(1)}, u32[]{:S(2)}, u32[]{:S(2)}) collective-permute-start(f32[16,128]{1,0:T(8,128)S(1)} %get-tuple-element.48), channel_id=1, source_target_pairs={{0,5},{1,4},{2,6},{3,7},{4,1},{5,0},{6,2},{7,3},{8,13},{9,12},{10,... | collective-permute-start | bytes 24584 | tf_op jit(solution)/shard_map/ppermute | solution.py:646
  10.6 1.4 %collective-permute-start.4 = (f32[16,128]{1,0:T(8,128)S(1)}, f32[16,128]{1,0:T(8,128)S(1)}, u32[]{:S(2)}, u32[]{:S(2)}) collective-permute-start(f32[16,128]{1,0:T(8,128)S(1)} %get-tuple-element.49), channel_id=1, source_target_pairs={{0,4},{1,6},{2,5},{3,7},{4,0},{5,2},{6,1},{7,3},{8,12},{9,14},{10,... | collective-permute-start | bytes 24584 | tf_op jit(solution)/shard_map/ppermute | solution.py:646
  10.6 1.4 %collective-permute-start.5 = (f32[16,128]{1,0:T(8,128)S(1)}, f32[16,128]{1,0:T(8,128)S(1)}, u32[]{:S(2)}, u32[]{:S(2)}) collective-permute-start(f32[16,128]{1,0:T(8,128)S(1)} %get-tuple-element.50), channel_id=1, source_target_pairs={{0,4},{1,5},{2,7},{3,6},{4,0},{5,1},{6,3},{7,2},{8,12},{9,13},{10,... | collective-permute-start | bytes 24584 | tf_op jit(solution)/shard_map/ppermute | solution.py:646

commit v10 on v9

--- a/solution.py
+++ b/solution.py
@@ -459,9 +459,10 @@
     head = iota((tall, LANES), 1) % 8 < 4
     to_left = jnp.where(head, sums[0], pltpu.roll(sums[1], 4, 1))
     to_right = jnp.where(head, pltpu.roll(sums[0], LANES - 4, 1), sums[1])
-    here = lax.rem(lax.axis_index("col"), len(message_refs))
+    here, last = lax.axis_index("col"), lax.axis_size("col") - 1
     for swap, message_ref in enumerate(message_refs):
-        message_ref[...] = jnp.where(here == swap, to_right, to_left)
+        onward = (here % len(message_refs) == swap) & (here != last)
+        message_ref[...] = jnp.where(onward, to_right, to_left)
 
 
 def series_kernel(looks, *refs):

time: 13.1 us -> 13.1 us (level)
  no operation moved by 1% of the time
where the time goes in v10:
time: 13.1 us; the launch traced here: 12.9 us
  starting transfers between devices  7.02 us (54%)
  Pallas kernels  3.76 us (29%)
  waiting for transfers between devices  1.16 us (9%)
  between operations  0.73 us (6%)
  local copies, waits for them, and re-layouts  0.23 us (2%)
    ppermute x3, starting transfers between devices, per_device(): blocks[step] = lax.ppermute(blocks[step], 'date', moves)  4.46 us
    ppermute x3, starting transfers between devices, per_device(): messages[swap] = held(lax.ppermute(messages[swap], ('date', 'col'), moves))  2.57 us
    ppermute x3, waiting for transfers between devices, per_device(): blocks[step] = lax.ppermute(blocks[step], 'date', moves)  1.08 us
    pallas_call x1, Pallas kernels, per_device(): pl.pallas_call(finish_kernel, out_shape=jax.ShapeDtypeStruct((inverse.sha...  0.91 us
    pallas_call x1, Pallas kernels, per_device(): pl.pallas_call(functools.partial(series_kernel, looks), out_shape=pltpu.V...  0.77 us
    pallas_call x1, Pallas kernels, cut(): pl.pallas_call(seam_kernel, out_shape=[pltpu.VMEM((sides * height + NOTE_...  0.7 us
    pallas_call x1, Pallas kernels, per_device(): pl.pallas_call(functools.partial(early_kernel, dates_here), out_shape=[pl...  0.7 us
    pallas_call x1, Pallas kernels, per_device(): pl.pallas_call(functools.partial(edge_kernel, dates_here, owners), out_sh...  0.4 us
  transfers between devices with their start and end apart: 6, of which 3 were waited for; matrix products, arithmetic and copies ran while one was open for 0% of the time, Pallas kernels for 13%

profile of v10, /device:TPU:0, one launch (start us, length us, event | category | flops | bytes accessed | tf_op | source)
XLA Modules:
  0.0 12.9 jit_solution(12416591157433642157)
XLA Ops:
  0.0 0.0 copy-start
  0.7 0.2 %copy-done = bf16[4,2,64,256]{3,2,1,0:T(8,128)(2,1)S(1)} copy-done((bf16[4,2,64,256]{3,2,1,0:T(8,128)(2,1)S(1)}, bf16[4,2,64,256]{3,2,1,0:T(8,128)(2,1)}, u32[]{:S(2)}) %copy-start) | copy-done | bytes 262168
  1.0 0.7 %shard_map.48 = (bf16[272,128]{1,0:T(8,128)(2,1)S(1)}, bf16[272,128]{1,0:T(8,128)(2,1)S(1)}, bf16[272,128]{1,0:T(8,128)(2,1)S(1)}, bf16[272,128]{1,0:T(8,128)(2,1)S(1)}) custom-call(bf16[4,2,64,256]{3,2,1,0:T(8,128)(2,1)S(1)} %copy-done, s32[2,24]{1,0:T(2,128)} %bitcast.1, f32[8,128]{1,0:T(8,128)S(1)} %get-tuple-element.28.live_ref, ...), custom_call_target="tpu_custom_call" | custom-call | tf_op jit(solution)/shard_map/pallas_call | solution.py:145
  1.7 0.5 %collective-permute-start.1 = (bf16[272,128]{1,0:T(8,128)(2,1)S(1)}, bf16[272,128]{1,0:T(8,128)(2,1)S(1)}, u32[]{:S(2)}, u32[]{:S(2)}) collective-permute-start(bf16[272,128]{1,0:T(8,128)(2,1)S(1)} %get-tuple-element.33), channel_id=1, source_target_pairs={{0,4},{4,8},{8,12},{12,0},{1,5},{5,9},{9,13},{13,1},{2,6},{6,10},{... | collective-permute-start | bytes 208904 | tf_op jit(solution)/shard_map/ppermute | solution.py:574
  2.2 2.6 %collective-permute-start.2 = (bf16[272,128]{1,0:T(8,128)(2,1)S(1)}, bf16[272,128]{1,0:T(8,128)(2,1)S(1)}, u32[]{:S(2)}, u32[]{:S(2)}) collective-permute-start(bf16[272,128]{1,0:T(8,128)(2,1)S(1)} %get-tuple-element.37), channel_id=1, source_target_pairs={{0,8},{4,12},{8,0},{12,4},{1,9},{5,13},{9,1},{13,5},{2,10},{6,14},... | collective-permute-start | bytes 208904 | tf_op jit(solution)/shard_map/ppermute | solution.py:574
  4.7 1.4 %collective-permute-start = (bf16[272,128]{1,0:T(8,128)(2,1)S(1)}, bf16[272,128]{1,0:T(8,128)(2,1)S(1)}, u32[]{:S(2)}, u32[]{:S(2)}) collective-permute-start(bf16[272,128]{1,0:T(8,128)(2,1)S(1)} %get-tuple-element.32), channel_id=1, source_target_pairs={{0,12},{4,0},{8,4},{12,8},{1,13},{5,1},{9,5},{13,9},{2,14},{6,2},{... | collective-permute-start | bytes 208904 | tf_op jit(solution)/shard_map/ppermute | solution.py:574
  6.1 0.0 collective-permute-done.1.refs_0_.refs_2_
  6.1 0.0 copy-start.1
  6.1 0.7 %shard_map.49 = (bf16[256,256]{1,0:T(8,128)(2,1)S(1)}, bf16[256,256]{1,0:T(8,128)(2,1)S(1)}, f32[2,2,8,2,8,128]{5,4,3,2,1,0:T(8,128)S(1)}, bf16[2,2,32,256]{3,2,1,0:T(8,128)(2,1)S(1)}, f32[2,8,128]{2,1,0:T(8,128)S(1)}) custom-call(bf16[272,128]{1,0:T(8,128)(2,1)S(1)} %collective-permute-done.1.refs_0_.refs_2_, ...), custom_call_target="tpu_custom_call" | custom-call | tf_op jit(solution)/shard_map/pallas_call | solution.py:582
  6.8 0.4 %collective-permute-done.2.refs_3_ = bf16[272,128]{1,0:T(8,128)(2,1)S(1)} collective-permute-done((bf16[272,128]{1,0:T(8,128)(2,1)S(1)}, bf16[272,128]{1,0:T(8,128)(2,1)S(1)}, u32[]{:S(2)}, u32[]{:S(2)}) %collective-permute-start.2) | collective-permute-done | bytes 69664 | tf_op jit(solution)/shard_map/ppermute | solution.py:574
  7.3 0.0 copy-done.1
  7.3 0.2 %shard_map.50 = (f32[1,2,2,128,128]{4,3,2,1,0:T(8,128)S(1)}, f32[1,2,8,128]{3,2,1,0:T(8,128)S(1)}, f32[2,16,128]{2,1,0:T(8,128)S(1)}, f32[16,128]{1,0:T(8,128)S(1)}) custom-call(bf16[256,256]{1,0:T(8,128)(2,1)S(1)} %get-tuple-element.36.refs_0_.refs_5_, f32[15,96]{1,0:T(8,128)S(1)} %copy-done.1, bf16[272,128]{1,0:T(8,128)(2,1)S(1)} %collective-permute-done.1.refs_0_.refs_2_, ...), custom_call_target="tpu_custom_call" | custom-call | tf_op jit(solution)/shard_map/pallas_call | solution.py:599
  7.5 0.6 %collective-permute-done.refs_0_ = bf16[272,128]{1,0:T(8,128)(2,1)S(1)} collective-permute-done((bf16[272,128]{1,0:T(8,128)(2,1)S(1)}, bf16[272,128]{1,0:T(8,128)(2,1)S(1)}, u32[]{:S(2)}, u32[]{:S(2)}) %collective-permute-start) | collective-permute-done | bytes 69664 | tf_op jit(solution)/shard_map/ppermute | solution.py:574
  8.2 0.4 %shard_map.51 = (bf16[2,32,256]{2,1,0:T(8,128)(2,1)S(1)}, f32[1,2,2,8,2,8,128]{6,5,4,3,2,1,0:T(8,128)S(1)}, f32[1,2,8,2,32,128]{5,4,3,2,1,0:T(8,128)S(1)}, f32[1...) custom-call(bf16[272,128]{1,0:T(8,128)(2,1)S(1)} %collective-permute-done.refs_0_, ...), custom_call_target="tpu_custom_call" | custom-call | tf_op jit(solution)/shard_map/pallas_call | solution.py:613
  8.6 2.1 %collective-permute-start.3 = (f32[16,128]{1,0:T(8,128)S(1)}, f32[16,128]{1,0:T(8,128)S(1)}, u32[]{:S(2)}, u32[]{:S(2)}) collective-permute-start(f32[16,128]{1,0:T(8,128)S(1)} %get-tuple-element.48), channel_id=1, source_target_pairs={{0,5},{1,4},{2,6},{3,7},{4,1},{5,0},{6,2},{7,3},{8,13},{9,12},{10,... | collective-permute-start | bytes 24584 | tf_op jit(solution)/shard_map/ppermute | solution.py:647
  10.6 0.0 collective-permute-start.4
  10.6 0.5 %collective-permute-start.5 = (f32[16,128]{1,0:T(8,128)S(1)}, f32[16,128]{1,0:T(8,128)S(1)}, u32[]{:S(2)}, u32[]{:S(2)}) collective-permute-start(f32[16,128]{1,0:T(8,128)S(1)} %get-tuple-element.50), channel_id=1, source_target_pairs={{0,4},{1,5},{2,7},{3,6},{4,0},{5,1},{6,3},{7,2},{8,12},{9,13},{10,... | collective-permute-start | bytes 24584 | tf_op jit(solution)/shard_map/ppermute | solution.py:647
  11.1 0.8 %shard_map.52.looked_ref = f32[2,16,256]{2,1,0:T(8,128)S(1)} custom-call(bf16[2,32,256]{2,1,0:T(8,128)(2,1)S(1)} %get-tuple-element.42.refs_0_, f32[2,2,8,2,8,128]{5,4,3,2,1,0:T(8,128)S(1)} %get-tuple-element.43.refs_1_, bf16[2,2,32,256]{3,2,1,0:T(8,128)(2,1)S(1)} %get-tuple-element.44.refs_2_, f32[1,2,2,8,2,8,128]{6,5,4,3,2,1,0:T(8,128)S(1)} %get-tuple-element.45.refs_3_, ...), custom_call_target="tpu_custom_call" | custom-call | flops 16777216 | bytes 1048576 | tf_op jit(solution)/shard_map/pallas_call | solution.py:633
  11.9 0.1 collective-permute-done.3.refs_0_
  12.0 0.0 collective-permute-done.4.refs_1_
  12.0 0.0 collective-permute-done.5.refs_2_
  12.0 0.9 %shard_map.53 = f32[15,2,8,32]{3,2,1,0:T(8,128)} custom-call(f32[2,16,256]{2,1,0:T(8,128)S(1)} %shard_map.52.looked_ref, bf16[256,256]{1,0:T(8,128)(2,1)S(1)} %get-tuple-element.47.fold_ref, f32[16,128]{1,0:T(8,128)S(1)} %collective-permute-done.3.refs_0_, f32[16,128]{1,0:T(8,128)S(1)} %collective-permute-done.4.refs_1_, ...), custom_call_target="tpu_custom_call" | custom-call | tf_op jit(solution)/shard_map/pallas_call | solution.py:648
  (2 shorter events, 0.0 us)
Async XLA Ops:
  0.0 1.0 %copy-start = (bf16[4,2,64,256]{3,2,1,0:T(8,128)(2,1)S(1)}, bf16[4,2,64,256]{3,2,1,0:T(8,128)(2,1)}, u32[]{:S(2)}) copy-start(bf16[4,2,64,256]{3,2,1,0:T(8,128)(2,1)} %scenes_ref.1) | copy-start | bytes 786436
  1.7 4.5 %collective-permute-start.1 = (bf16[272,128]{1,0:T(8,128)(2,1)S(1)}, bf16[272,128]{1,0:T(8,128)(2,1)S(1)}, u32[]{:S(2)}, u32[]{:S(2)}) collective-permute-start(bf16[272,128]{1,0:T(8,128)(2,1)S(1)} %get-tuple-element.33), channel_id=1, source_target_pairs={{0,4},{4,8},{8,12},{12,0},{1,5},{5,9},{9,13},{13,1},{2,6},{6,10},{... | collective-permute-start | bytes 208904 | tf_op jit(solution)/shard_map/ppermute | solution.py:574
  2.2 5.1 %collective-permute-start.2 = (bf16[272,128]{1,0:T(8,128)(2,1)S(1)}, bf16[272,128]{1,0:T(8,128)(2,1)S(1)}, u32[]{:S(2)}, u32[]{:S(2)}) collective-permute-start(bf16[272,128]{1,0:T(8,128)(2,1)S(1)} %get-tuple-element.37), channel_id=1, source_target_pairs={{0,8},{4,12},{8,0},{12,4},{1,9},{5,13},{9,1},{13,5},{2,10},{6,14},... | collective-permute-start | bytes 208904 | tf_op jit(solution)/shard_map/ppermute | solution.py:574
  4.7 3.4 %collective-permute-start = (bf16[272,128]{1,0:T(8,128)(2,1)S(1)}, bf16[272,128]{1,0:T(8,128)(2,1)S(1)}, u32[]{:S(2)}, u32[]{:S(2)}) collective-permute-start(bf16[272,128]{1,0:T(8,128)(2,1)S(1)} %get-tuple-element.32), channel_id=1, source_target_pairs={{0,12},{4,0},{8,4},{12,8},{1,13},{5,1},{9,5},{13,9},{2,14},{6,2},{... | collective-permute-start | bytes 208904 | tf_op jit(solution)/shard_map/ppermute | solution.py:574
  6.1 1.1 %copy-start.1 = (f32[15,96]{1,0:T(8,128)S(1)}, f32[15,96]{1,0:T(8,128)}, u32[]{:S(2)}) copy-start(f32[15,96]{1,0:T(8,128)} %refs_1_.1) | copy-start | bytes 17284
  8.6 3.4 %collective-permute-start.3 = (f32[16,128]{1,0:T(8,128)S(1)}, f32[16,128]{1,0:T(8,128)S(1)}, u32[]{:S(2)}, u32[]{:S(2)}) collective-permute-start(f32[16,128]{1,0:T(8,128)S(1)} %get-tuple-element.48), channel_id=1, source_target_pairs={{0,5},{1,4},{2,6},{3,7},{4,1},{5,0},{6,2},{7,3},{8,13},{9,12},{10,... | collective-permute-start | bytes 24584 | tf_op jit(solution)/shard_map/ppermute | solution.py:647
  10.6 1.4 %collective-permute-start.4 = (f32[16,128]{1,0:T(8,128)S(1)}, f32[16,128]{1,0:T(8,128)S(1)}, u32[]{:S(2)}, u32[]{:S(2)}) collective-permute-start(f32[16,128]{1,0:T(8,128)S(1)} %get-tuple-element.49), channel_id=1, source_target_pairs={{0,4},{1,6},{2,5},{3,7},{4,0},{5,2},{6,1},{7,3},{8,12},{9,14},{10,... | collective-permute-start | bytes 24584 | tf_op jit(solution)/shard_map/ppermute | solution.py:647
  10.6 1.4 %collective-permute-start.5 = (f32[16,128]{1,0:T(8,128)S(1)}, f32[16,128]{1,0:T(8,128)S(1)}, u32[]{:S(2)}, u32[]{:S(2)}) collective-permute-start(f32[16,128]{1,0:T(8,128)S(1)} %get-tuple-element.50), channel_id=1, source_target_pairs={{0,4},{1,5},{2,7},{3,6},{4,0},{5,1},{6,3},{7,2},{8,12},{9,13},{10,... | collective-permute-start | bytes 24584 | tf_op jit(solution)/shard_map/ppermute | solution.py:647

commit v11 on v9

--- a/solution.py
+++ b/solution.py
@@ -43,16 +43,6 @@
     column, lane = iota((columns, columns), 0), iota((columns, columns), 1)
     here = (column // 8 == lane % looks) & (column % 8 == lane // looks)
     return jnp.where(here, 1.0, 0.0).astype(BF16)
-
-
-def fold_of(shape, looks, half_rows):
-    cell, target = iota(shape, 0), iota(shape, 1)
-    right = cell < LANES
-    cell = cell % LANES
-    half_row = cell // 16
-    here = right & (target == half_row * looks + looks - 1)
-    here = here | ~right & (target == half_row * looks)
-    return jnp.where(here & (half_row < half_rows), 1.0, 0.0).astype(BF16)
 
 
 def live_kernel(rows, slots, count_ref, blank_ref, live_ref, pick_ref, own_ref, gather_ref):
@@ -345,14 +335,13 @@
 
 
 def early_kernel(dates_here, *refs):
-    *block_refs, comb_ref, fold_ref, ring_ref, pair_ref, seam_ref, rows_ref = refs
+    *block_refs, comb_ref, ring_ref, pair_ref, seam_ref, rows_ref = refs
     columns = comb_ref.shape[0]
     looks = columns // 8
     tiles = ring_ref.shape[3]
     half_rows = rows_ref.shape[2] // GROUP // 2
     comb = comb_of(columns)
     comb_ref[...] = comb
-    fold_ref[...] = fold_of(fold_ref.shape, looks, half_rows)
     for index, block_ref in enumerate(block_refs):
         spread_block(block_ref, comb, dates_here, index * dates_here, rows_ref)
         seam_of(block_ref, dates_here, index * dates_here, seam_ref)
@@ -436,11 +425,22 @@
             values.append(mine[1] * other[0] - mine[0] * other[1])
         for part in range(2):
             value = jnp.concatenate(values[part::2], axis=0)
+            for shift in (1, 2, 8):
+                value = value + pltpu.roll(value, LANES - shift, 1)
+            if part:
+                value = pltpu.roll(value, 1, 1)
             count = value.shape[0]
             bits = halves(value)
             for half in range(2):
                 at = half * pairs + unit * count
                 pair_ref[part, at : at + count, :] = bits[half]
+    sums = []
+    for part in range(2):
+        summed = jnp.dot(weights[part], pair_ref[part], preferred_element_type=F32)
+        sums.append(summed[:tall] + summed[tall:])
+    message = jnp.where(iota((tall, LANES), 1) % 4 == 1, sums[1], sums[0])
+    for message_ref in message_refs:
+        message_ref[...] = message
     looks = comb_ref.shape[0] // 8
     half_rows = rows_ref.shape[3] // GROUP // 2
     for group in range(1, dates // GROUP):
@@ -452,16 +452,6 @@
                 far_ref[group - 1, part, place, tile, at, :] = cells
 
         pack_group(rows_ref.at[group - 1], looks, half_rows, keep)
-    sums = []
-    for part in range(2):
-        summed = jnp.dot(weights[part], pair_ref[part], preferred_element_type=F32)
-        sums.append(summed[:tall] + summed[tall:])
-    head = iota((tall, LANES), 1) % 8 < 4
-    to_left = jnp.where(head, sums[0], pltpu.roll(sums[1], 4, 1))
-    to_right = jnp.where(head, pltpu.roll(sums[0], LANES - 4, 1), sums[1])
-    here = lax.rem(lax.axis_index("col"), len(message_refs))
-    for swap, message_ref in enumerate(message_refs):
-        message_ref[...] = jnp.where(here == swap, to_right, to_left)
 
 
 def series_kernel(looks, *refs):
@@ -508,7 +498,7 @@
             looked_ref[part, :, across] = summed[:tall] + summed[tall:]
 
 
-def finish_kernel(looked_ref, fold_ref, *refs):
+def finish_kernel(looked_ref, *refs):
     *message_refs, out_ref, sum_ref, done_ref, semaphores = refs
     parts, times, half_rows, looks = done_ref.shape
     tall = looked_ref.shape[1]
@@ -520,20 +510,19 @@
         message = message_ref[...]
         from_right = jnp.where((here != last) & (here % swaps == swap), message, from_right)
         from_left = jnp.where((here != 0) & ((here - 1) % swaps == swap), message, from_left)
-    edges = jnp.concatenate([from_right, from_left], axis=1)
-    head = iota(edges.shape, 1) % 8 < 4
-    edges = [jnp.where(head, edges, 0.0), jnp.where(head, 0.0, edges)]
-    edges = jnp.concatenate(halves(jnp.concatenate(edges, axis=0)), axis=0)
-    edges = jnp.dot(edges, fold_ref[...], preferred_element_type=F32)
-    edges = edges[: parts * tall] + edges[parts * tall :]
+    lane = iota((tall, LANES), 1)
     sent = []
     for part in range(parts):
-        value = looked_ref[part] + edges[part * tall : (part + 1) * tall]
         for half_row in range(half_rows):
             tile, near = half_row // pack, half_row % pack
-            one = value[:, tile * LANES : (tile + 1) * LANES]
-            at = half_row * tall
-            sum_ref[part, at : at + tall, :] = pltpu.roll(one, -near * looks % LANES, 1)
+            value = looked_ref[part, :, tile * LANES : (tile + 1) * LANES]
+            value = pltpu.roll(value, -near * looks % LANES, 1)
+            at = 16 * half_row + part
+            right = pltpu.roll(from_right, (looks - 1 - at) % LANES, 1)
+            left = pltpu.roll(from_left, (-4 - at) % LANES, 1)
+            value = jnp.where(lane == looks - 1, value + right, value)
+            value = jnp.where(lane == 0, value + left, value)
+            sum_ref[part, half_row * tall : (half_row + 1) * tall, :] = value
         for time in range(times):
             rows = sum_ref[part, pl.ds(time, half_rows, stride=tall), :]
             done_ref[part, time] = rows[:, :looks]
@@ -578,17 +567,16 @@
     order = [blocks[(place - 1) % owners] for place in range(owners)]
     order = [held(block) for block in order]
     group_rows = pltpu.VMEM((parts, sides, rows * GROUP, LANES), F32)
-    comb, fold, first_group, first_pairs, first_seam = pl.pallas_call(
+    comb, first_group, first_pairs, first_seam = pl.pallas_call(
         functools.partial(early_kernel, dates_here),
         out_shape=[
             pltpu.VMEM((columns, columns), BF16),
-            pltpu.VMEM((2 * LANES, tiles * LANES), BF16),
             pltpu.VMEM((parts, 2, 8, tiles, GROUP, LANES), F32),
             pltpu.VMEM((parts, 2, GROUP * GROUP // 2, tiles * LANES), BF16),
             pltpu.VMEM((parts, GROUP, LANES), F32),
         ],
         in_specs=[IN_VMEM] * (GROUP // dates_here),
-        out_specs=[IN_VMEM] * 5,
+        out_specs=[IN_VMEM] * 4,
         scratch_shapes=[group_rows],
         compiler_params=pltpu.CompilerParams(vmem_limit_bytes=40 << 20),
     )(*order[: GROUP // dates_here])
@@ -649,14 +637,14 @@
         out_shape=jax.ShapeDtypeStruct(
             (inverse.shape[0], parts, half_rows, columns // 8), F32
         ),
-        in_specs=[IN_VMEM] * (swaps + 2),
+        in_specs=[IN_VMEM] * (swaps + 1),
         out_specs=ANYWHERE,
         scratch_shapes=[
             pltpu.VMEM((parts, half_rows * tall, LANES), F32),
             pltpu.VMEM((parts, inverse.shape[0], half_rows, columns // 8), F32),
             pltpu.SemaphoreType.DMA((parts,)),
         ],
-    )(held(looked), held(fold), *messages)
+    )(held(looked), *messages)
 
 
 def solution(mesh):

time: 13.1 us -> 13.1 us (level)
  no operation moved by 1% of the time
where the time goes in v11:
time: 13.1 us; the launch traced here: 12.9 us
  starting transfers between devices  7.02 us (54%)
  Pallas kernels  3.73 us (28%)
  waiting for transfers between devices  1.2 us (9%)
  between operations  0.74 us (6%)
  local copies, waits for them, and re-layouts  0.23 us (2%)
    ppermute x3, starting transfers between devices, per_device(): blocks[step] = lax.ppermute(blocks[step], 'date', moves)  4.46 us
    ppermute x3, starting transfers between devices, per_device(): messages[swap] = held(lax.ppermute(messages[swap], ('date', 'col'), moves))  2.57 us
    ppermute x3, waiting for transfers between devices, per_device(): blocks[step] = lax.ppermute(blocks[step], 'date', moves)  1.12 us
    pallas_call x1, Pallas kernels, per_device(): pl.pallas_call(finish_kernel, out_shape=jax.ShapeDtypeStruct((inverse.sha...  0.84 us
    pallas_call x1, Pallas kernels, per_device(): pl.pallas_call(functools.partial(series_kernel, looks), out_shape=pltpu.V...  0.77 us
    pallas_call x1, Pallas kernels, cut(): pl.pallas_call(seam_kernel, out_shape=[pltpu.VMEM((sides * height + NOTE_...  0.7 us
    pallas_call x1, Pallas kernels, per_device(): pl.pallas_call(functools.partial(early_kernel, dates_here), out_shape=[pl...  0.65 us
    pallas_call x1, Pallas kernels, per_device(): pl.pallas_call(functools.partial(edge_kernel, dates_here, owners), out_sh...  0.48 us
  transfers between devices with their start and end apart: 6, of which 3 were waited for; matrix products, arithmetic and copies ran while one was open for 0% of the time, Pallas kernels for 13%

profile of v11, /device:TPU:0, one launch (start us, length us, event | category | flops | bytes accessed | tf_op | source)
XLA Modules:
  0.0 12.9 jit_solution(7452927027413245737)
XLA Ops:
  0.0 0.0 copy-start
  0.7 0.2 %copy-done = bf16[4,2,64,256]{3,2,1,0:T(8,128)(2,1)S(1)} copy-done((bf16[4,2,64,256]{3,2,1,0:T(8,128)(2,1)S(1)}, bf16[4,2,64,256]{3,2,1,0:T(8,128)(2,1)}, u32[]{:S(2)}) %copy-start) | copy-done | bytes 262168
  1.0 0.7 %shard_map.48 = (bf16[272,128]{1,0:T(8,128)(2,1)S(1)}, bf16[272,128]{1,0:T(8,128)(2,1)S(1)}, bf16[272,128]{1,0:T(8,128)(2,1)S(1)}, bf16[272,128]{1,0:T(8,128)(2,1)S(1)}) custom-call(bf16[4,2,64,256]{3,2,1,0:T(8,128)(2,1)S(1)} %copy-done, s32[2,24]{1,0:T(2,128)} %bitcast.1, f32[8,128]{1,0:T(8,128)S(1)} %get-tuple-element.27.live_ref, ...), custom_call_target="tpu_custom_call" | custom-call | tf_op jit(solution)/shard_map/pallas_call | solution.py:135
  1.7 0.5 %collective-permute-start.1 = (bf16[272,128]{1,0:T(8,128)(2,1)S(1)}, bf16[272,128]{1,0:T(8,128)(2,1)S(1)}, u32[]{:S(2)}, u32[]{:S(2)}) collective-permute-start(bf16[272,128]{1,0:T(8,128)(2,1)S(1)} %get-tuple-element.32), channel_id=1, source_target_pairs={{0,4},{4,8},{8,12},{12,0},{1,5},{5,9},{9,13},{13,1},{2,6},{6,10},{... | collective-permute-start | bytes 208904 | tf_op jit(solution)/shard_map/ppermute | solution.py:562
  2.2 2.6 %collective-permute-start.2 = (bf16[272,128]{1,0:T(8,128)(2,1)S(1)}, bf16[272,128]{1,0:T(8,128)(2,1)S(1)}, u32[]{:S(2)}, u32[]{:S(2)}) collective-permute-start(bf16[272,128]{1,0:T(8,128)(2,1)S(1)} %get-tuple-element.36), channel_id=1, source_target_pairs={{0,8},{4,12},{8,0},{12,4},{1,9},{5,13},{9,1},{13,5},{2,10},{6,14},... | collective-permute-start | bytes 208904 | tf_op jit(solution)/shard_map/ppermute | solution.py:562
  4.7 1.4 %collective-permute-start = (bf16[272,128]{1,0:T(8,128)(2,1)S(1)}, bf16[272,128]{1,0:T(8,128)(2,1)S(1)}, u32[]{:S(2)}, u32[]{:S(2)}) collective-permute-start(bf16[272,128]{1,0:T(8,128)(2,1)S(1)} %get-tuple-element.31), channel_id=1, source_target_pairs={{0,12},{4,0},{8,4},{12,8},{1,13},{5,1},{9,5},{13,9},{2,14},{6,2},{... | collective-permute-start | bytes 208904 | tf_op jit(solution)/shard_map/ppermute | solution.py:562
  6.1 0.0 collective-permute-done.1.refs_0_.refs_2_
  6.1 0.0 copy-start.1
  6.1 0.7 %shard_map.49 = (bf16[256,256]{1,0:T(8,128)(2,1)S(1)}, f32[2,2,8,2,8,128]{5,4,3,2,1,0:T(8,128)S(1)}, bf16[2,2,32,256]{3,2,1,0:T(8,128)(2,1)S(1)}, f32[2,8,128]{2,1,0:T(8,128)S(1)}) custom-call(bf16[272,128]{1,0:T(8,128)(2,1)S(1)} %collective-permute-done.1.refs_0_.refs_2_, bf16[272,128]{1,0:T(8,128)(2,1)S(1)} %get-tuple-element.33.refs_1_.refs_4_), custom_call_target="tpu_custom_call" | custom-call | tf_op jit(solution)/shard_map/pallas_call | solution.py:570
  6.8 0.5 %collective-permute-done.2.refs_3_ = bf16[272,128]{1,0:T(8,128)(2,1)S(1)} collective-permute-done((bf16[272,128]{1,0:T(8,128)(2,1)S(1)}, bf16[272,128]{1,0:T(8,128)(2,1)S(1)}, u32[]{:S(2)}, u32[]{:S(2)}) %collective-permute-start.2) | collective-permute-done | bytes 69664 | tf_op jit(solution)/shard_map/ppermute | solution.py:562
  7.3 0.0 copy-done.1
  7.3 0.2 %shard_map.50 = (f32[1,2,2,128,128]{4,3,2,1,0:T(8,128)S(1)}, f32[1,2,8,128]{3,2,1,0:T(8,128)S(1)}, f32[2,16,128]{2,1,0:T(8,128)S(1)}, f32[16,128]{1,0:T(8,128)S(1)}) custom-call(bf16[256,256]{1,0:T(8,128)(2,1)S(1)} %get-tuple-element.35.refs_0_.refs_5_, f32[15,96]{1,0:T(8,128)S(1)} %copy-done.1, bf16[272,128]{1,0:T(8,128)(2,1)S(1)} %collective-permute-done.1.refs_0_.refs_2_, ...), custom_call_target="tpu_custom_call" | custom-call | tf_op jit(solution)/shard_map/pallas_call | solution.py:586
  7.5 0.6 %collective-permute-done.refs_0_ = bf16[272,128]{1,0:T(8,128)(2,1)S(1)} collective-permute-done((bf16[272,128]{1,0:T(8,128)(2,1)S(1)}, bf16[272,128]{1,0:T(8,128)(2,1)S(1)}, u32[]{:S(2)}, u32[]{:S(2)}) %collective-permute-start) | collective-permute-done | bytes 69664 | tf_op jit(solution)/shard_map/ppermute | solution.py:562
  8.2 0.5 %shard_map.51 = (bf16[2,32,256]{2,1,0:T(8,128)(2,1)S(1)}, f32[1,2,2,8,2,8,128]{6,5,4,3,2,1,0:T(8,128)S(1)}, f32[1,2,8,2,32,128]{5,4,3,2,1,0:T(8,128)S(1)}, f32[1...) custom-call(bf16[272,128]{1,0:T(8,128)(2,1)S(1)} %collective-permute-done.refs_0_, ...), custom_call_target="tpu_custom_call" | custom-call | tf_op jit(solution)/shard_map/pallas_call | solution.py:600
  8.7 2.1 %collective-permute-start.3 = (f32[16,128]{1,0:T(8,128)S(1)}, f32[16,128]{1,0:T(8,128)S(1)}, u32[]{:S(2)}, u32[]{:S(2)}) collective-permute-start(f32[16,128]{1,0:T(8,128)S(1)} %get-tuple-element.46), channel_id=1, source_target_pairs={{0,5},{1,4},{2,6},{3,7},{4,1},{5,0},{6,2},{7,3},{8,13},{9,12},{10,... | collective-permute-start | bytes 24584 | tf_op jit(solution)/shard_map/ppermute | solution.py:634
  10.7 0.0 collective-permute-start.4
  10.7 0.5 %collective-permute-start.5 = (f32[16,128]{1,0:T(8,128)S(1)}, f32[16,128]{1,0:T(8,128)S(1)}, u32[]{:S(2)}, u32[]{:S(2)}) collective-permute-start(f32[16,128]{1,0:T(8,128)S(1)} %get-tuple-element.48), channel_id=1, source_target_pairs={{0,4},{1,5},{2,7},{3,6},{4,0},{5,1},{6,3},{7,2},{8,12},{9,13},{10,... | collective-permute-start | bytes 24584 | tf_op jit(solution)/shard_map/ppermute | solution.py:634
  11.2 0.8 %shard_map.52.looked_ref = f32[2,16,256]{2,1,0:T(8,128)S(1)} custom-call(bf16[2,32,256]{2,1,0:T(8,128)(2,1)S(1)} %get-tuple-element.41.refs_0_, f32[2,2,8,2,8,128]{5,4,3,2,1,0:T(8,128)S(1)} %get-tuple-element.42.refs_1_, bf16[2,2,32,256]{3,2,1,0:T(8,128)(2,1)S(1)} %get-tuple-element.43.refs_2_, f32[1,2,2,8,2,8,128]{6,5,4,3,2,1,0:T(8,128)S(1)} %get-tuple-element.44.refs_3_, ...), custom_call_target="tpu_custom_call" | custom-call | flops 16777216 | bytes 1048576 | tf_op jit(solution)/shard_map/pallas_call | solution.py:620
  12.0 0.1 collective-permute-done.3.refs_0_
  12.1 0.0 collective-permute-done.4.refs_1_
  12.1 0.0 collective-permute-done.5.refs_2_
  12.1 0.8 %shard_map.53 = f32[15,2,8,32]{3,2,1,0:T(8,128)} custom-call(f32[2,16,256]{2,1,0:T(8,128)S(1)} %shard_map.52.looked_ref, f32[16,128]{1,0:T(8,128)S(1)} %collective-permute-done.3.refs_0_, f32[16,128]{1,0:T(8,128)S(1)} %collective-permute-done.4.refs_1_, f32[16,128]{1,0:T(8,128)S(1)} %collective-permute-done.5.refs_2_), custom_call_target="tpu_custom_call" | custom-call | tf_op jit(solution)/shard_map/pallas_call | solution.py:635
  (2 shorter events, 0.0 us)
Async XLA Ops:
  0.0 1.0 %copy-start = (bf16[4,2,64,256]{3,2,1,0:T(8,128)(2,1)S(1)}, bf16[4,2,64,256]{3,2,1,0:T(8,128)(2,1)}, u32[]{:S(2)}) copy-start(bf16[4,2,64,256]{3,2,1,0:T(8,128)(2,1)} %scenes_ref.1) | copy-start | bytes 786436
  1.7 4.5 %collective-permute-start.1 = (bf16[272,128]{1,0:T(8,128)(2,1)S(1)}, bf16[272,128]{1,0:T(8,128)(2,1)S(1)}, u32[]{:S(2)}, u32[]{:S(2)}) collective-permute-start(bf16[272,128]{1,0:T(8,128)(2,1)S(1)} %get-tuple-element.32), channel_id=1, source_target_pairs={{0,4},{4,8},{8,12},{12,0},{1,5},{5,9},{9,13},{13,1},{2,6},{6,10},{... | collective-permute-start | bytes 208904 | tf_op jit(solution)/shard_map/ppermute | solution.py:562
  2.2 5.1 %collective-permute-start.2 = (bf16[272,128]{1,0:T(8,128)(2,1)S(1)}, bf16[272,128]{1,0:T(8,128)(2,1)S(1)}, u32[]{:S(2)}, u32[]{:S(2)}) collective-permute-start(bf16[272,128]{1,0:T(8,128)(2,1)S(1)} %get-tuple-element.36), channel_id=1, source_target_pairs={{0,8},{4,12},{8,0},{12,4},{1,9},{5,13},{9,1},{13,5},{2,10},{6,14},... | collective-permute-start | bytes 208904 | tf_op jit(solution)/shard_map/ppermute | solution.py:562
  4.7 3.4 %collective-permute-start = (bf16[272,128]{1,0:T(8,128)(2,1)S(1)}, bf16[272,128]{1,0:T(8,128)(2,1)S(1)}, u32[]{:S(2)}, u32[]{:S(2)}) collective-permute-start(bf16[272,128]{1,0:T(8,128)(2,1)S(1)} %get-tuple-element.31), channel_id=1, source_target_pairs={{0,12},{4,0},{8,4},{12,8},{1,13},{5,1},{9,5},{13,9},{2,14},{6,2},{... | collective-permute-start | bytes 208904 | tf_op jit(solution)/shard_map/ppermute | solution.py:562
  6.1 1.1 %copy-start.1 = (f32[15,96]{1,0:T(8,128)S(1)}, f32[15,96]{1,0:T(8,128)}, u32[]{:S(2)}) copy-start(f32[15,96]{1,0:T(8,128)} %refs_1_.1) | copy-start | bytes 17284
  8.7 3.4 %collective-permute-start.3 = (f32[16,128]{1,0:T(8,128)S(1)}, f32[16,128]{1,0:T(8,128)S(1)}, u32[]{:S(2)}, u32[]{:S(2)}) collective-permute-start(f32[16,128]{1,0:T(8,128)S(1)} %get-tuple-element.46), channel_id=1, source_target_pairs={{0,5},{1,4},{2,6},{3,7},{4,1},{5,0},{6,2},{7,3},{8,13},{9,12},{10,... | collective-permute-start | bytes 24584 | tf_op jit(solution)/shard_map/ppermute | solution.py:634
  10.7 1.4 %collective-permute-start.4 = (f32[16,128]{1,0:T(8,128)S(1)}, f32[16,128]{1,0:T(8,128)S(1)}, u32[]{:S(2)}, u32[]{:S(2)}) collective-permute-start(f32[16,128]{1,0:T(8,128)S(1)} %get-tuple-element.47), channel_id=1, source_target_pairs={{0,4},{1,6},{2,5},{3,7},{4,0},{5,2},{6,1},{7,3},{8,12},{9,14},{10,... | collective-permute-start | bytes 24584 | tf_op jit(solution)/shard_map/ppermute | solution.py:634
  10.7 1.4 %collective-permute-start.5 = (f32[16,128]{1,0:T(8,128)S(1)}, f32[16,128]{1,0:T(8,128)S(1)}, u32[]{:S(2)}, u32[]{:S(2)}) collective-permute-start(f32[16,128]{1,0:T(8,128)S(1)} %get-tuple-element.48), channel_id=1, source_target_pairs={{0,4},{1,5},{2,7},{3,6},{4,0},{5,1},{6,3},{7,2},{8,12},{9,13},{10,... | collective-permute-start | bytes 24584 | tf_op jit(solution)/shard_map/ppermute | solution.py:634

commit v12 on v11

--- a/solution.py
+++ b/solution.py
@@ -425,10 +425,8 @@
             values.append(mine[1] * other[0] - mine[0] * other[1])
         for part in range(2):
             value = jnp.concatenate(values[part::2], axis=0)
-            for shift in (1, 2, 8):
-                value = value + pltpu.roll(value, LANES - shift, 1)
-            if part:
-                value = pltpu.roll(value, 1, 1)
+            for shift in (1 if part else LANES - 1, LANES - 2, LANES - 8):
+                value = value + pltpu.roll(value, shift, 1)
             count = value.shape[0]
             bits = halves(value)
             for half in range(2):

time: 13.1 us -> 13 us (level)
  no operation moved by 1% of the time
where the time goes in v12:
time: 13 us; the launch traced here: 12.9 us
  starting transfers between devices  7.02 us (54%)
  Pallas kernels  3.67 us (28%)
  waiting for transfers between devices  1.2 us (9%)
  between operations  0.74 us (6%)
  local copies, waits for them, and re-layouts  0.23 us (2%)
    ppermute x3, starting transfers between devices, per_device(): blocks[step] = lax.ppermute(blocks[step], 'date', moves)  4.46 us
    ppermute x3, starting transfers between devices, per_device(): messages[swap] = held(lax.ppermute(messages[swap], ('date', 'col'), moves))  2.57 us
    ppermute x3, waiting for transfers between devices, per_device(): blocks[step] = lax.ppermute(blocks[step], 'date', moves)  1.12 us
    pallas_call x1, Pallas kernels, per_device(): pl.pallas_call(finish_kernel, out_shape=jax.ShapeDtypeStruct((inverse.sha...  0.84 us
    pallas_call x1, Pallas kernels, per_device(): pl.pallas_call(functools.partial(series_kernel, looks), out_shape=pltpu.V...  0.77 us
    pallas_call x1, Pallas kernels, cut(): pl.pallas_call(seam_kernel, out_shape=[pltpu.VMEM((sides * height + NOTE_...  0.7 us
    pallas_call x1, Pallas kernels, per_device(): pl.pallas_call(functools.partial(early_kernel, dates_here), out_shape=[pl...  0.65 us
    pallas_call x1, Pallas kernels, per_device(): pl.pallas_call(functools.partial(edge_kernel, dates_here, owners), out_sh...  0.42 us
  transfers between devices with their start and end apart: 6, of which 3 were waited for; matrix products, arithmetic and copies ran while one was open for 0% of the time, Pallas kernels for 13%

profile of v12, /device:TPU:0, one launch (start us, length us, event | category | flops | bytes accessed | tf_op | source)
XLA Modules:
  0.0 12.9 jit_solution(13474009106335892177)
XLA Ops:
  0.0 0.0 copy-start
  0.7 0.2 %copy-done = bf16[4,2,64,256]{3,2,1,0:T(8,128)(2,1)S(1)} copy-done((bf16[4,2,64,256]{3,2,1,0:T(8,128)(2,1)S(1)}, bf16[4,2,64,256]{3,2,1,0:T(8,128)(2,1)}, u32[]{:S(2)}) %copy-start) | copy-done | bytes 262168
  1.0 0.7 %shard_map.48 = (bf16[272,128]{1,0:T(8,128)(2,1)S(1)}, bf16[272,128]{1,0:T(8,128)(2,1)S(1)}, bf16[272,128]{1,0:T(8,128)(2,1)S(1)}, bf16[272,128]{1,0:T(8,128)(2,1)S(1)}) custom-call(bf16[4,2,64,256]{3,2,1,0:T(8,128)(2,1)S(1)} %copy-done, s32[2,24]{1,0:T(2,128)} %bitcast.1, f32[8,128]{1,0:T(8,128)S(1)} %get-tuple-element.27.live_ref, ...), custom_call_target="tpu_custom_call" | custom-call | tf_op jit(solution)/shard_map/pallas_call | solution.py:135
  1.7 0.5 %collective-permute-start.1 = (bf16[272,128]{1,0:T(8,128)(2,1)S(1)}, bf16[272,128]{1,0:T(8,128)(2,1)S(1)}, u32[]{:S(2)}, u32[]{:S(2)}) collective-permute-start(bf16[272,128]{1,0:T(8,128)(2,1)S(1)} %get-tuple-element.32), channel_id=1, source_target_pairs={{0,4},{4,8},{8,12},{12,0},{1,5},{5,9},{9,13},{13,1},{2,6},{6,10},{... | collective-permute-start | bytes 208904 | tf_op jit(solution)/shard_map/ppermute | solution.py:560
  2.2 2.6 %collective-permute-start.2 = (bf16[272,128]{1,0:T(8,128)(2,1)S(1)}, bf16[272,128]{1,0:T(8,128)(2,1)S(1)}, u32[]{:S(2)}, u32[]{:S(2)}) collective-permute-start(bf16[272,128]{1,0:T(8,128)(2,1)S(1)} %get-tuple-element.36), channel_id=1, source_target_pairs={{0,8},{4,12},{8,0},{12,4},{1,9},{5,13},{9,1},{13,5},{2,10},{6,14},... | collective-permute-start | bytes 208904 | tf_op jit(solution)/shard_map/ppermute | solution.py:560
  4.7 1.4 %collective-permute-start = (bf16[272,128]{1,0:T(8,128)(2,1)S(1)}, bf16[272,128]{1,0:T(8,128)(2,1)S(1)}, u32[]{:S(2)}, u32[]{:S(2)}) collective-permute-start(bf16[272,128]{1,0:T(8,128)(2,1)S(1)} %get-tuple-element.31), channel_id=1, source_target_pairs={{0,12},{4,0},{8,4},{12,8},{1,13},{5,1},{9,5},{13,9},{2,14},{6,2},{... | collective-permute-start | bytes 208904 | tf_op jit(solution)/shard_map/ppermute | solution.py:560
  6.1 0.0 collective-permute-done.1.refs_0_.refs_2_
  6.1 0.0 copy-start.1
  6.1 0.7 %shard_map.49 = (bf16[256,256]{1,0:T(8,128)(2,1)S(1)}, f32[2,2,8,2,8,128]{5,4,3,2,1,0:T(8,128)S(1)}, bf16[2,2,32,256]{3,2,1,0:T(8,128)(2,1)S(1)}, f32[2,8,128]{2,1,0:T(8,128)S(1)}) custom-call(bf16[272,128]{1,0:T(8,128)(2,1)S(1)} %collective-permute-done.1.refs_0_.refs_2_, bf16[272,128]{1,0:T(8,128)(2,1)S(1)} %get-tuple-element.33.refs_1_.refs_4_), custom_call_target="tpu_custom_call" | custom-call | tf_op jit(solution)/shard_map/pallas_call | solution.py:568
  6.8 0.5 %collective-permute-done.2.refs_3_ = bf16[272,128]{1,0:T(8,128)(2,1)S(1)} collective-permute-done((bf16[272,128]{1,0:T(8,128)(2,1)S(1)}, bf16[272,128]{1,0:T(8,128)(2,1)S(1)}, u32[]{:S(2)}, u32[]{:S(2)}) %collective-permute-start.2) | collective-permute-done | bytes 69664 | tf_op jit(solution)/shard_map/ppermute | solution.py:560
  7.3 0.0 copy-done.1
  7.3 0.2 %shard_map.50 = (f32[1,2,2,128,128]{4,3,2,1,0:T(8,128)S(1)}, f32[1,2,8,128]{3,2,1,0:T(8,128)S(1)}, f32[2,16,128]{2,1,0:T(8,128)S(1)}, f32[16,128]{1,0:T(8,128)S(1)}) custom-call(bf16[256,256]{1,0:T(8,128)(2,1)S(1)} %get-tuple-element.35.refs_0_.refs_5_, f32[15,96]{1,0:T(8,128)S(1)} %copy-done.1, bf16[272,128]{1,0:T(8,128)(2,1)S(1)} %collective-permute-done.1.refs_0_.refs_2_, ...), custom_call_target="tpu_custom_call" | custom-call | tf_op jit(solution)/shard_map/pallas_call | solution.py:584
  7.5 0.6 %collective-permute-done.refs_0_ = bf16[272,128]{1,0:T(8,128)(2,1)S(1)} collective-permute-done((bf16[272,128]{1,0:T(8,128)(2,1)S(1)}, bf16[272,128]{1,0:T(8,128)(2,1)S(1)}, u32[]{:S(2)}, u32[]{:S(2)}) %collective-permute-start) | collective-permute-done | bytes 69664 | tf_op jit(solution)/shard_map/ppermute | solution.py:560
  8.2 0.4 %shard_map.51 = (bf16[2,32,256]{2,1,0:T(8,128)(2,1)S(1)}, f32[1,2,2,8,2,8,128]{6,5,4,3,2,1,0:T(8,128)S(1)}, f32[1,2,8,2,32,128]{5,4,3,2,1,0:T(8,128)S(1)}, f32[1...) custom-call(bf16[272,128]{1,0:T(8,128)(2,1)S(1)} %collective-permute-done.refs_0_, ...), custom_call_target="tpu_custom_call" | custom-call | tf_op jit(solution)/shard_map/pallas_call | solution.py:598
  8.6 2.1 %collective-permute-start.3 = (f32[16,128]{1,0:T(8,128)S(1)}, f32[16,128]{1,0:T(8,128)S(1)}, u32[]{:S(2)}, u32[]{:S(2)}) collective-permute-start(f32[16,128]{1,0:T(8,128)S(1)} %get-tuple-element.46), channel_id=1, source_target_pairs={{0,5},{1,4},{2,6},{3,7},{4,1},{5,0},{6,2},{7,3},{8,13},{9,12},{10,... | collective-permute-start | bytes 24584 | tf_op jit(solution)/shard_map/ppermute | solution.py:632
  10.6 0.0 collective-permute-start.4
  10.7 0.5 %collective-permute-start.5 = (f32[16,128]{1,0:T(8,128)S(1)}, f32[16,128]{1,0:T(8,128)S(1)}, u32[]{:S(2)}, u32[]{:S(2)}) collective-permute-start(f32[16,128]{1,0:T(8,128)S(1)} %get-tuple-element.48), channel_id=1, source_target_pairs={{0,4},{1,5},{2,7},{3,6},{4,0},{5,1},{6,3},{7,2},{8,12},{9,13},{10,... | collective-permute-start | bytes 24584 | tf_op jit(solution)/shard_map/ppermute | solution.py:632
  11.2 0.8 %shard_map.52.looked_ref = f32[2,16,256]{2,1,0:T(8,128)S(1)} custom-call(bf16[2,32,256]{2,1,0:T(8,128)(2,1)S(1)} %get-tuple-element.41.refs_0_, f32[2,2,8,2,8,128]{5,4,3,2,1,0:T(8,128)S(1)} %get-tuple-element.42.refs_1_, bf16[2,2,32,256]{3,2,1,0:T(8,128)(2,1)S(1)} %get-tuple-element.43.refs_2_, f32[1,2,2,8,2,8,128]{6,5,4,3,2,1,0:T(8,128)S(1)} %get-tuple-element.44.refs_3_, ...), custom_call_target="tpu_custom_call" | custom-call | flops 16777216 | bytes 1048576 | tf_op jit(solution)/shard_map/pallas_call | solution.py:618
  11.9 0.1 collective-permute-done.3.refs_0_
  12.0 0.0 collective-permute-done.4.refs_1_
  12.0 0.0 collective-permute-done.5.refs_2_
  12.0 0.8 %shard_map.53 = f32[15,2,8,32]{3,2,1,0:T(8,128)} custom-call(f32[2,16,256]{2,1,0:T(8,128)S(1)} %shard_map.52.looked_ref, f32[16,128]{1,0:T(8,128)S(1)} %collective-permute-done.3.refs_0_, f32[16,128]{1,0:T(8,128)S(1)} %collective-permute-done.4.refs_1_, f32[16,128]{1,0:T(8,128)S(1)} %collective-permute-done.5.refs_2_), custom_call_target="tpu_custom_call" | custom-call | tf_op jit(solution)/shard_map/pallas_call | solution.py:633
  (2 shorter events, 0.0 us)
Async XLA Ops:
  0.0 1.0 %copy-start = (bf16[4,2,64,256]{3,2,1,0:T(8,128)(2,1)S(1)}, bf16[4,2,64,256]{3,2,1,0:T(8,128)(2,1)}, u32[]{:S(2)}) copy-start(bf16[4,2,64,256]{3,2,1,0:T(8,128)(2,1)} %scenes_ref.1) | copy-start | bytes 786436
  1.7 4.5 %collective-permute-start.1 = (bf16[272,128]{1,0:T(8,128)(2,1)S(1)}, bf16[272,128]{1,0:T(8,128)(2,1)S(1)}, u32[]{:S(2)}, u32[]{:S(2)}) collective-permute-start(bf16[272,128]{1,0:T(8,128)(2,1)S(1)} %get-tuple-element.32), channel_id=1, source_target_pairs={{0,4},{4,8},{8,12},{12,0},{1,5},{5,9},{9,13},{13,1},{2,6},{6,10},{... | collective-permute-start | bytes 208904 | tf_op jit(solution)/shard_map/ppermute | solution.py:560
  2.2 5.1 %collective-permute-start.2 = (bf16[272,128]{1,0:T(8,128)(2,1)S(1)}, bf16[272,128]{1,0:T(8,128)(2,1)S(1)}, u32[]{:S(2)}, u32[]{:S(2)}) collective-permute-start(bf16[272,128]{1,0:T(8,128)(2,1)S(1)} %get-tuple-element.36), channel_id=1, source_target_pairs={{0,8},{4,12},{8,0},{12,4},{1,9},{5,13},{9,1},{13,5},{2,10},{6,14},... | collective-permute-start | bytes 208904 | tf_op jit(solution)/shard_map/ppermute | solution.py:560
  4.7 3.4 %collective-permute-start = (bf16[272,128]{1,0:T(8,128)(2,1)S(1)}, bf16[272,128]{1,0:T(8,128)(2,1)S(1)}, u32[]{:S(2)}, u32[]{:S(2)}) collective-permute-start(bf16[272,128]{1,0:T(8,128)(2,1)S(1)} %get-tuple-element.31), channel_id=1, source_target_pairs={{0,12},{4,0},{8,4},{12,8},{1,13},{5,1},{9,5},{13,9},{2,14},{6,2},{... | collective-permute-start | bytes 208904 | tf_op jit(solution)/shard_map/ppermute | solution.py:560
  6.1 1.1 %copy-start.1 = (f32[15,96]{1,0:T(8,128)S(1)}, f32[15,96]{1,0:T(8,128)}, u32[]{:S(2)}) copy-start(f32[15,96]{1,0:T(8,128)} %refs_1_.1) | copy-start | bytes 17284
  8.6 3.4 %collective-permute-start.3 = (f32[16,128]{1,0:T(8,128)S(1)}, f32[16,128]{1,0:T(8,128)S(1)}, u32[]{:S(2)}, u32[]{:S(2)}) collective-permute-start(f32[16,128]{1,0:T(8,128)S(1)} %get-tuple-element.46), channel_id=1, source_target_pairs={{0,5},{1,4},{2,6},{3,7},{4,1},{5,0},{6,2},{7,3},{8,13},{9,12},{10,... | collective-permute-start | bytes 24584 | tf_op jit(solution)/shard_map/ppermute | solution.py:632
  10.6 1.4 %collective-permute-start.4 = (f32[16,128]{1,0:T(8,128)S(1)}, f32[16,128]{1,0:T(8,128)S(1)}, u32[]{:S(2)}, u32[]{:S(2)}) collective-permute-start(f32[16,128]{1,0:T(8,128)S(1)} %get-tuple-element.47), channel_id=1, source_target_pairs={{0,4},{1,6},{2,5},{3,7},{4,0},{5,2},{6,1},{7,3},{8,12},{9,14},{10,... | collective-permute-start | bytes 24584 | tf_op jit(solution)/shard_map/ppermute | solution.py:632
  10.7 1.4 %collective-permute-start.5 = (f32[16,128]{1,0:T(8,128)S(1)}, f32[16,128]{1,0:T(8,128)S(1)}, u32[]{:S(2)}, u32[]{:S(2)}) collective-permute-start(f32[16,128]{1,0:T(8,128)S(1)} %get-tuple-element.48), channel_id=1, source_target_pairs={{0,4},{1,5},{2,7},{3,6},{4,0},{5,1},{6,3},{7,2},{8,12},{9,13},{10,... | collective-permute-start | bytes 24584 | tf_op jit(solution)/shard_map/ppermute | solution.py:632
